TPU v7x, 128 devices: a whole 4x4x4 slice. The times are simulated.
128 devices in a mesh: ctx: 16 (over x, y_hi, core), tp: 8 (over z, y_lo).
Axes of the slice: x: 4, y: 4 (y_hi: 2, y_lo: 2; y = y_hi * 2 + y_lo), z: 4, core: 2. Of those that a mesh axis runs over, the one named last changes fastest.
Arguments:
- tokens: bfloat16 [8192, 1024], P(('ctx', 'tp')), may hold values from -6 to 6
- cotangent: bfloat16 [8192, 1024], P(('ctx', 'tp')), may hold values from -6 to 6
- positions: int32 [8192], replicated, may hold values from 0 to 16382, as said below
- span_order: int32 [32], replicated, may hold values from 0 to 31, each once
- first_gain: float32 [1024], replicated, may hold values from 0.25 to 1.75
- w_query: bfloat16 [1024, 1024], P(None, 'tp'), may hold values from -0.1875 to 0.1875
- w_key: bfloat16 [1024, 512], P(None, 'tp'), may hold values from -0.1875 to 0.1875
- w_value: bfloat16 [1024, 512], P(None, 'tp'), may hold values from -0.1875 to 0.1875
- query_gain: float32 [64], replicated, may hold values from 0.25 to 1.75
- key_gain: float32 [64], replicated, may hold values from 0.25 to 1.75
- w_out: bfloat16 [1024, 1024], P('tp'), may hold values from -1.5 to 1.5
- second_gain: float32 [1024], replicated, may hold values from 0.25 to 1.75
- w_gate: bfloat16 [1024, 4608], P(None, 'tp'), may hold values from -0.1875 to 0.1875
- w_up: bfloat16 [1024, 4608], P(None, 'tp'), may hold values from -0.1875 to 0.1875
- w_down: bfloat16 [4608, 1024], P('tp'), may hold values from -0.09375 to 0.09375
Outputs:
- block_out: bfloat16 [8192, 1024], P(('ctx', 'tp'))
- grad_tokens: bfloat16 [8192, 1024], P(('ctx', 'tp'))
- grad_first_gain: float32 [1024], replicated
- grad_w_query: float32 [1024, 1024], P('ctx', 'tp')
- grad_w_key: float32 [1024, 512], P('ctx', 'tp')
- grad_w_value: float32 [1024, 512], P('ctx', 'tp')
- grad_query_gain: float32 [64], replicated
- grad_key_gain: float32 [64], replicated
- grad_w_out: float32 [1024, 1024], P('tp', 'ctx')
- grad_second_gain: float32 [1024], replicated
- grad_w_gate: float32 [1024, 4608], P('ctx', 'tp')
- grad_w_up: float32 [1024, 4608], P('ctx', 'tp')
- grad_w_down: float32 [4608, 1024], P('tp', 'ctx')
Inputs may be any that keep to these rules, and one draw needn't show every extreme that they name: `positions`: strictly increasing along the sequence, starting at 0, steps of 1 to 3, the last equal to 16382. A permutation: stored rows j * 256 to (j + 1) * 256 - 1 hold span span_order[j] of the sequence.
All inputs are finite; a program needn't handle non-finite values.
Results may differ from a plain program's by a relative error of at most 0.03.
Values may be sent and summed in bfloat16 or wider, within the bound.
No kernel may reach another device: no remote copies, remote signals or barrier semaphores. Data moves between devices by JAX's collectives and lax.ppermute only.
A program may use at most 128 MiB of HBM per device.

v0:
```python
from functools import partial
import math

import jax
import jax.numpy as jnp
from jax import lax
from jax.sharding import PartitionSpec as P

eps = 1e-05
theta = 1000000.0
neg_big = -1e30


def side_by_side(arrays, axis, dim, along):
    widths = [a.shape[along] for a in arrays]
    both = jnp.concatenate(arrays, axis=along)
    out = lax.psum_scatter(both, axis, scatter_dimension=dim, tiled=True)
    return tuple(jnp.split(out, [sum(widths[:k]) for k in range(1, len(widths))], axis=along))


def cut_along(x, dim, length):
    dims = x.shape
    tiles = x.reshape(*dims[:dim], length, dims[dim] // length, *dims[dim + 1 :])
    return jnp.moveaxis(tiles, dim, 0)


def summed_on_arrival(x, axis, dim):
    length = lax.axis_size(axis)
    tiles = lax.all_to_all(cut_along(x, dim, length), axis, 0, 0, tiled=True)
    return jnp.sum(tiles.astype(jnp.float32), axis=0)


def rms_scaled(values, gain):
    scaled = values * lax.rsqrt(jnp.mean(values * values, axis=-1, keepdims=True) + eps)
    return scaled * gain


def rotate(values, cosine, sine):
    half = values.shape[-1] // 2
    first = values[..., :half]
    second = values[..., half:]
    return jnp.concatenate(
        [first * cosine - second * sine, second * cosine + first * sine], axis=-1
    )


def angles(places, width):
    freqs = theta ** (-(jnp.arange(width // 2, dtype=jnp.float32) * 2.0 / width))
    turned = places.astype(jnp.float32)[:, None] * freqs[None, :]
    return (jnp.cos(turned), jnp.sin(turned))


def global_rows(stored, span_order, span):
    slots = stored // span
    hits = slots[:, None] == jnp.arange(span_order.shape[0], dtype=jnp.int32)[None, :]
    owner = jnp.sum(jnp.where(hits, span_order[None, :], 0), axis=1)
    return owner * span + stored % span


def head_prep(pre, gain, cosine, sine, heads):
    rows = pre.shape[0]
    shaped = pre.reshape(rows, heads, -1)
    return rotate(rms_scaled(shaped, gain), cosine[:, None, :], sine[:, None, :]).reshape(rows, -1)


def per_device(
    tokens,
    cotangent,
    positions,
    span_order,
    first_gain,
    w_query,
    w_key,
    w_value,
    query_gain,
    key_gain,
    w_out,
    second_gain,
    w_gate,
    w_up,
    w_down,
):
    ctx_count = lax.axis_size("ctx")
    tp_count = lax.axis_size("tp")
    shard_rows = tokens.shape[0]
    local_rows = shard_rows * tp_count
    span = local_rows // 2
    head_dim = query_gain.shape[0]
    kv_width = w_key.shape[1]
    kv_heads = kv_width // head_dim
    q_heads = w_query.shape[1] // head_dim
    group = q_heads // kv_heads
    scale = 1.0 / math.sqrt(head_dim)
    own_start = lax.axis_index("ctx") * local_rows
    own_stored = own_start + jnp.arange(local_rows, dtype=jnp.int32)
    query_rows = global_rows(own_stored, span_order, span)
    cosine, sine = angles(jnp.take(positions, query_rows), head_dim)
    tokens_f = tokens.astype(jnp.float32)
    normed, first_back = jax.vjp(rms_scaled, tokens_f, first_gain)
    normed_all = lax.all_gather(normed.astype(jnp.bfloat16), "tp", axis=0, tiled=True)
    query_pre = jnp.dot(normed_all, w_query, preferred_element_type=jnp.float32)
    key_pre = jnp.dot(normed_all, w_key, preferred_element_type=jnp.float32)
    value_pre = jnp.dot(normed_all, w_value, preferred_element_type=jnp.float32)
    query_out, query_back = jax.vjp(
        partial(head_prep, cosine=cosine, sine=sine, heads=q_heads), query_pre, query_gain
    )
    key_out, key_back = jax.vjp(
        partial(head_prep, cosine=cosine, sine=sine, heads=kv_heads), key_pre, key_gain
    )
    pairs = jnp.concatenate([key_out.astype(jnp.bfloat16), value_pre.astype(jnp.bfloat16)], axis=1)
    query_four = query_out.astype(jnp.bfloat16).reshape(local_rows, kv_heads, group, head_dim)

    def split_piece(piece, offset, block):
        part = lax.dynamic_slice_in_dim(piece, offset, block, 0)
        keys = part[:, :kv_width].reshape(block, kv_heads, head_dim)
        values = part[:, kv_width:].reshape(block, kv_heads, head_dim)
        return (keys, values)

    start_acc = jnp.zeros((kv_heads, group, local_rows, head_dim), jnp.float32)
    start_top = jnp.full((kv_heads, group, local_rows), neg_big, jnp.float32)
    start_total = jnp.zeros((kv_heads, group, local_rows), jnp.float32)
    piece = lax.all_gather(pairs, "ctx", axis=0, tiled=True)
    count = piece.shape[0]
    block = math.gcd(count, 512)

    def attend_one_block(index, inner):
        acc, top, total = inner
        offset = index * block
        keys, values = split_piece(piece, offset, block)
        rows = global_rows(offset + jnp.arange(block, dtype=jnp.int32), span_order, span)
        allowed = query_rows[:, None] >= rows[None, :]
        scores = scale * jnp.einsum(
            "qkgd,rkd->kgqr", query_four, keys, preferred_element_type=jnp.float32
        )
        scores = jnp.where(allowed, scores, neg_big)
        new_top = jnp.maximum(top, jnp.max(scores, axis=-1))
        weights = jnp.where(allowed, jnp.exp(scores - new_top[..., None]), 0.0)
        factor = jnp.exp(top - new_top)
        total = total * factor + jnp.sum(weights, axis=-1)
        acc = acc * factor[..., None] + jnp.einsum(
            "kgqr,rkd->kgqd",
            weights.astype(jnp.bfloat16),
            values,
            preferred_element_type=jnp.float32,
        )
        return (acc, new_top, total)

    acc, top, total = lax.fori_loop(
        0, count // block, attend_one_block, (start_acc, start_top, start_total)
    )
    attended_full = acc / total[..., None]
    attended_b = attended_full.astype(jnp.bfloat16)
    log_total = top + jnp.log(total)
    mixed_b = attended_b.transpose(2, 0, 1, 3).reshape(local_rows, q_heads * head_dim)
    resid = tokens_f + lax.psum_scatter(
        jnp.dot(mixed_b, w_out, preferred_element_type=jnp.float32).astype(jnp.bfloat16),
        "tp",
        scatter_dimension=0,
        tiled=True,
    ).astype(jnp.float32)
    normed_two, second_back = jax.vjp(rms_scaled, resid, second_gain)
    normed_two_all, upstream_all = (
        lax.all_gather(normed_two.astype(jnp.bfloat16), "tp", axis=0, tiled=True),
        lax.all_gather(cotangent, "tp", axis=0, tiled=True),
    )
    gate = jnp.dot(normed_two_all, w_gate, preferred_element_type=jnp.float32)
    up = jnp.dot(normed_two_all, w_up, preferred_element_type=jnp.float32)
    sigma = jax.nn.sigmoid(gate)
    swish = gate * sigma
    hidden_b = (swish * up).astype(jnp.bfloat16)
    block_out = (
        resid
        + lax.psum_scatter(
            jnp.dot(hidden_b, w_down, preferred_element_type=jnp.float32).astype(jnp.bfloat16),
            "tp",
            scatter_dimension=0,
            tiled=True,
        ).astype(jnp.float32)
    ).astype(jnp.bfloat16)
    upstream = cotangent.astype(jnp.float32)
    hidden_grad = jnp.dot(upstream_all, w_down.T, preferred_element_type=jnp.float32)
    gate_grad_b = (hidden_grad * up * sigma * (1.0 + gate * (1.0 - sigma))).astype(jnp.bfloat16)
    up_grad_b = (hidden_grad * swish).astype(jnp.bfloat16)
    grad_down = jnp.dot(hidden_b.T, upstream_all, preferred_element_type=jnp.float32)
    grad_gate = jnp.dot(normed_two_all.T, gate_grad_b, preferred_element_type=jnp.float32)
    grad_up = jnp.dot(normed_two_all.T, up_grad_b, preferred_element_type=jnp.float32)
    grad_gate, grad_up, grad_down = (
        *tuple(
            (
                part.astype(jnp.float32)
                for part in side_by_side(
                    (grad_gate.astype(jnp.bfloat16), grad_up.astype(jnp.bfloat16)), "ctx", 0, 1
                )
            )
        ),
        lax.psum_scatter(
            grad_down.astype(jnp.bfloat16), "ctx", scatter_dimension=1, tiled=True
        ).astype(jnp.float32),
    )
    normed_two_grad = lax.psum_scatter(
        (
            jnp.dot(gate_grad_b, w_gate.T, preferred_element_type=jnp.float32)
            + jnp.dot(up_grad_b, w_up.T, preferred_element_type=jnp.float32)
        ).astype(jnp.bfloat16),
        "tp",
        scatter_dimension=0,
        tiled=True,
    ).astype(jnp.float32)
    resid_part, second_gain_grad = second_back(normed_two_grad)
    resid_grad = upstream + resid_part
    resid_grad_all = lax.all_gather(resid_grad.astype(jnp.bfloat16), "tp", axis=0, tiled=True)
    grad_out = jnp.dot(mixed_b.T, resid_grad_all, preferred_element_type=jnp.float32)
    mixed_grad_b = jnp.dot(resid_grad_all, w_out.T, preferred_element_type=jnp.float32).astype(
        jnp.bfloat16
    )
    mixed_grad_four = mixed_grad_b.reshape(local_rows, kv_heads, group, head_dim).transpose(
        1, 2, 0, 3
    )
    deltas = jnp.sum(mixed_grad_four.astype(jnp.float32) * attended_full, axis=-1)
    start_query = jnp.zeros((kv_heads, group, local_rows, head_dim), jnp.float32)
    start_pairs = jnp.zeros((local_rows * ctx_count, 2 * kv_width), jnp.float32)
    attend_piece = lax.all_gather(pairs, "ctx", axis=0, tiled=True)
    query_sum = start_query
    current = start_pairs
    query_acc = query_sum
    piece_grad = current
    count = attend_piece.shape[0]
    local_block = math.gcd(count, 512)

    def local_one_block(index, inner):
        query_sum, grad_rows = inner
        offset = index * local_block
        keys, values = split_piece(attend_piece, offset, local_block)
        rows = global_rows(offset + jnp.arange(local_block, dtype=jnp.int32), span_order, span)
        allowed = query_rows[:, None] >= rows[None, :]
        scores = scale * jnp.einsum(
            "qkgd,rkd->kgqr", query_four, keys, preferred_element_type=jnp.float32
        )
        weights = jnp.where(allowed, jnp.exp(scores - log_total[..., None]), 0.0)
        weight_grad = jnp.einsum(
            "kgqd,rkd->kgqr", mixed_grad_four, values, preferred_element_type=jnp.float32
        )
        score_grad_b = (weights * (weight_grad - deltas[..., None])).astype(jnp.bfloat16)
        query_sum = query_sum + scale * jnp.einsum(
            "kgqr,rkd->kgqd", score_grad_b, keys, preferred_element_type=jnp.float32
        )
        key_grad = scale * jnp.einsum(
            "kgqr,qkgd->rkd", score_grad_b, query_four, preferred_element_type=jnp.float32
        )
        value_grad = jnp.einsum(
            "kgqr,kgqd->rkd",
            weights.astype(jnp.bfloat16),
            mixed_grad_four,
            preferred_element_type=jnp.float32,
        )
        joined = jnp.concatenate(
            [key_grad.reshape(local_block, kv_width), value_grad.reshape(local_block, kv_width)],
            axis=1,
        )
        current = lax.dynamic_slice_in_dim(grad_rows, offset, local_block, 0)
        grad_rows = lax.dynamic_update_slice_in_dim(grad_rows, current + joined, offset, 0)
        return (query_sum, grad_rows)

    query_sum, current = lax.fori_loop(
        0, count // local_block, local_one_block, (query_acc, piece_grad)
    )
    pair_grads = summed_on_arrival(current.astype(jnp.bfloat16), "ctx", 0)
    value_pre_b = pair_grads[:, kv_width:].astype(jnp.bfloat16)
    key_pre_grad, key_gain_grad = key_back(pair_grads[:, :kv_width])
    query_grad = query_sum.transpose(2, 0, 1, 3).reshape(local_rows, q_heads * head_dim)
    query_pre_grad, query_gain_grad = query_back(query_grad)
    query_pre_b = query_pre_grad.astype(jnp.bfloat16)
    key_pre_b = key_pre_grad.astype(jnp.bfloat16)
    grad_query = jnp.dot(normed_all.T, query_pre_b, preferred_element_type=jnp.float32)
    grad_key = jnp.dot(normed_all.T, key_pre_b, preferred_element_type=jnp.float32)
    grad_value = jnp.dot(normed_all.T, value_pre_b, preferred_element_type=jnp.float32)
    total_rows = jnp.dot(query_pre_b, w_query.T, preferred_element_type=jnp.float32)
    total_rows = total_rows + jnp.dot(key_pre_b, w_key.T, preferred_element_type=jnp.float32)
    normed_grad = lax.psum_scatter(
        (total_rows + jnp.dot(value_pre_b, w_value.T, preferred_element_type=jnp.float32)).astype(
            jnp.bfloat16
        ),
        "tp",
        scatter_dimension=0,
        tiled=True,
    ).astype(jnp.float32)
    tokens_part, first_gain_grad = first_back(normed_grad)
    grad_tokens = (resid_grad + tokens_part).astype(jnp.bfloat16)
    first_sum, query_sum_g, key_sum_g, second_sum = lax.psum(
        (first_gain_grad, query_gain_grad, key_gain_grad, second_gain_grad), ("ctx", "tp")
    )
    grad_query, grad_key, grad_value, grad_out = (
        *tuple(
            (
                part.astype(jnp.float32)
                for part in side_by_side(
                    (
                        grad_query.astype(jnp.bfloat16),
                        grad_key.astype(jnp.bfloat16),
                        grad_value.astype(jnp.bfloat16),
                    ),
                    "ctx",
                    0,
                    1,
                )
            )
        ),
        lax.psum_scatter(
            grad_out.astype(jnp.bfloat16), "ctx", scatter_dimension=1, tiled=True
        ).astype(jnp.float32),
    )
    return (
        block_out,
        grad_tokens,
        first_sum,
        grad_query,
        grad_key,
        grad_value,
        query_sum_g,
        key_sum_g,
        grad_out,
        second_sum,
        grad_gate,
        grad_up,
        grad_down,
    )


def solution(mesh):
    return jax.shard_map(
        per_device,
        mesh=mesh,
        in_specs=(
            P(("ctx", "tp"), None),
            P(("ctx", "tp"), None),
            P(),
            P(),
            P(),
            P(None, "tp"),
            P(None, "tp"),
            P(None, "tp"),
            P(),
            P(),
            P("tp", None),
            P(),
            P(None, "tp"),
            P(None, "tp"),
            P("tp", None),
        ),
        out_specs=(
            P(("ctx", "tp"), None),
            P(("ctx", "tp"), None),
            P(),
            P("ctx", "tp"),
            P("ctx", "tp"),
            P("ctx", "tp"),
            P(),
            P(),
            P("tp", "ctx"),
            P(),
            P("ctx", "tp"),
            P("ctx", "tp"),
            P("tp", "ctx"),
        ),
        check_vma=False,
    )
```

profile of v0, /device:TPU:1, one launch (start us, length us, event | category | flops | bytes accessed | tf_op | source)
XLA Modules:
  0.0 816.1 jit_solution(55050828206887850)
XLA Ops:
  11.0 3.4 gather_fusion
  14.5 35.0 %all-gather.6.cloned.1.call-done = bf16[512,1024]{1,0:T(8,128)(2,1)} async-done(((bf16[64,1024]{1,0:T(8,128)(2,1)}), bf16[512,1024]{1,0:T(8,128)(2,1)}) %all-gather.6.cloned.1.call-update) | async-done | bytes 1048592 | tf_op jit(solution)/shard_map/all_gather | solution.py:100
  55.9 53.0 %all-gather.8.cloned.1.call-done = bf16[8192,128]{0,1:T(8,128)(2,1)} async-done(((bf16[512,128]{0,1:T(8,128)(2,1)}), bf16[8192,128]{0,1:T(8,128)(2,1)}) %all-gather.8.cloned.1.call-update) | async-done | bytes 2097168 | tf_op jit(solution)/shard_map/all_gather | solution.py:122
  108.9 75.2 %while.38 = (s32[]{:T(128)}, f32[1,2,512,64]{2,3,1,0:T(8,128)S(1)}, f32[1,2,512]{2,1,0:T(2,128)S(1)}, f32[1,2,512]{2,1,0:T(2,128)S(1)}, s32[512]{0:T(512)S(1)}, ...) while((s32[]{:T(128)}, f32[1,2,512,64]{2,3,1,0:T(8,128)S(1)}, ...), condition=%wide.region_8.9_spmd.clone, body=%wide.region_4.8_spmd.clone.sunk | while | flops 141562368 | bytes 8206687 | solution.py:148
  185.7 34.9 %reduce-scatter.13.cloned.1.call-done = bf16[64,1024]{1,0:T(8,128)(2,1)} async-done(((bf16[512,1024]{1,0:T(8,128)(2,1)}), bf16[64,1024]{1,0:T(8,128)(2,1)}) %reduce-scatter.13.cloned.1.call-update) | async-done | bytes 131088 | tf_op jit(solution)/shard_map/reduce_scatter | solution.py:155
  224.0 39.0 %all-gather.10.cloned.1.call-done = bf16[512,1024]{1,0:T(8,128)(2,1)} async-done(((bf16[64,1024]{1,0:T(8,128)(2,1)}), bf16[512,1024]{1,0:T(8,128)(2,1)}) %all-gather.10.cloned.1.call-update) | async-done | bytes 1048592 | tf_op jit(solution)/shard_map/all_gather | solution.py:163
  263.0 3.6 fusion.92
  266.6 1.8 fusion.91
  268.5 36.1 %all-gather.12.cloned.1.call-done = bf16[512,1024]{1,0:T(8,128)(2,1)} async-done(((bf16[64,1024]{1,0:T(8,128)(2,1)}), bf16[512,1024]{1,0:T(8,128)(2,1)}) %all-gather.12.cloned.1.call-update) | async-done | bytes 1048592 | tf_op jit(solution)/shard_map/all_gather | solution.py:164
  304.5 4.1 multiply_convert_fusion
  310.3 2.0 add_convert_fusion.1
  312.4 40.5 %reduce-scatter.17.cloned.1.call-done = bf16[64,1024]{1,0:T(8,128)(2,1)} async-done(((bf16[512,1024]{1,0:T(8,128)(2,1)}), bf16[64,1024]{1,0:T(8,128)(2,1)}) %reduce-scatter.17.cloned.1.call-update) | async-done | bytes 131088 | tf_op jit(solution)/shard_map/reduce_scatter | solution.py:200
  356.2 3.5 convolution_convert_fusion
  360.6 2.2 convolution_convert_fusion.1
  365.3 4.4 copy.83
  369.7 26.3 %all-gather.14.cloned.1.call-done = bf16[512,1024]{1,0:T(8,128)(2,1)} async-done(((bf16[64,1024]{1,0:T(8,128)(2,1)}), bf16[512,1024]{1,0:T(8,128)(2,1)}) %all-gather.14.cloned.1.call-update) | async-done | bytes 1048592 | tf_op jit(solution)/shard_map/all_gather | solution.py:211
  397.7 2.3 broadcast_in_dim.211.clone
  400.0 143.2 %while.39 = (s32[]{:T(128)}, f32[1,2,512,64]{2,3,1,0:T(8,128)S(1)}, f32[8192,128]{1,0:T(8,128)}, s32[512]{0:T(512)S(1)}, s32[32]{0:T(128)}, /*index=5*/bf16[8192...) while((s32[]{:T(128)}, f32[1,2,512,64]{2,3,1,0:T(8,128)S(1)}, ...), condition=%wide.region_17.18_spmd.clone, body=%wide.region_15.17_spmd.clone.sunk | while | flops 339900928 | bytes 14899605 | solution.py:264
  492.3 1.8 fusion.170
  519.2 1.8 fusion.170
  543.2 3.8 convert_element_type.199
  547.0 3.9 copy.71
  550.9 11.9 %all-to-all-start = ((bf16[16,512,128]{1,2,0:T(8,128)(2,1)}), bf16[16,512,128]{1,2,0:T(8,128)(2,1)}, u32[]{:S(2)}, u32[]{:S(2)}) async-start(bf16[16,512,128]{1,2,0:T(8,128)(2,1)} %copy.71), calls=%async_computation.3 | async-start | bytes 4194304 | tf_op jit(solution)/shard_map/all_to_all | solution.py:29
  562.8 2.5 convolution_convert_fusion.6
  566.9 24.4 %all-to-all-done = bf16[16,512,128]{1,2,0:T(8,128)(2,1)} async-done(((bf16[16,512,128]{1,2,0:T(8,128)(2,1)}), bf16[16,512,128]{1,2,0:T(8,128)(2,1)}, u32[]{:S(2)}, u32[]{:S(2)}) %all-to-all-start) | async-done | bytes 2097184 | tf_op jit(solution)/shard_map/all_to_all | solution.py:29
  591.3 1.9 convert_reduce_fusion
  598.5 2.1 convolution_convert_fusion.4
  605.3 24.2 %reduce-scatter.21.cloned.1.call-done = bf16[128,64]{0,1:T(8,128)(2,1)} async-done(((bf16[128,1024]{0,1:T(8,128)(2,1)}), bf16[128,64]{0,1:T(8,128)(2,1)}) %reduce-scatter.21.cloned.1.call-update) | async-done | bytes 16400 | tf_op jit(solution)/shard_map/reduce_scatter | solution.py:308
  630.8 67.3 %reduce-scatter.25.cloned.1.call-done = bf16[64,256]{1,0:T(8,128)(2,1)} async-done(((bf16[1024,256]{1,0:T(8,128)(2,1)}), bf16[64,256]{1,0:T(8,128)(2,1)}) %reduce-scatter.25.cloned.1.call-update) | async-done | bytes 32784
  702.2 35.5 %reduce-scatter.19.cloned.1.call-done = bf16[64,1024]{1,0:T(8,128)(2,1)} async-done(((bf16[512,1024]{1,0:T(8,128)(2,1)}), bf16[64,1024]{1,0:T(8,128)(2,1)}) %reduce-scatter.19.cloned.1.call-update) | async-done | bytes 131088 | tf_op jit(solution)/shard_map/reduce_scatter | solution.py:279
  738.9 68.7 %all-reduce.4 = (f32[1024]{0:T(1024)}, f32[64]{0:T(128)}, f32[64]{0:T(128)}, f32[1024]{0:T(1024)}) all-reduce(f32[1024]{0:T(1024)S(1)} %get-tuple-element.598, f32[64]{0:T(128)S(1)} %get-tuple-element.596, f32[64]{0:T(128)S(1)} %get-tuple-element.594, f32[1024]{0:T(1024)S(1)} %copy-done.41), channel_id=1, replica_groups=mesh['ctx'=16,'tp'=8] {'ctx','tp'}, use_global_device_ids=true, to_apply=%region_24.25 | all-reduce | flops 2176 | bytes 17408 | tf_op jit(solution)/shard_map/psum | solution.py:289
  807.7 1.9 fusion.53
  (646 shorter events, 255.3 us)
Async XLA Ops:
  7.2 297.4 %copy-start = (bf16[576,1024]{1,0:T(8,128)(2,1)S(1)}, bf16[576,1024]{1,0:T(8,128)(2,1)}, u32[]{:S(2)}) copy-start(bf16[576,1024]{1,0:T(8,128)(2,1)} %param.33) | copy-start | bytes 3538948
  7.2 42.2 %all-gather.6.cloned.1.call-start = ((), (), s32[]{:S(2)}) async-start(), calls=%async_computation.9 | async-start | bytes 1179648 | tf_op jit(solution)/shard_map/all_gather | solution.py:100
  10.1 98.7 %all-gather.8.cloned.1.call-start = ((), (), s32[]{:S(2)}) async-start(), calls=%async_computation.10 | async-start | bytes 2228224 | tf_op jit(solution)/shard_map/all_gather | solution.py:122
  54.7 165.9 %reduce-scatter.13.cloned.1.call-start = ((), (), s32[]{:S(2)}) async-start(), calls=%async_computation.11 | async-start | bytes 1179648 | tf_op jit(solution)/shard_map/reduce_scatter | solution.py:155
  55.1 53.7 %copy-start.20 = (f32[512,32]{0,1:T(8,128)}, f32[512,32]{0,1:T(8,128)S(1)}, u32[]{:S(2)}) copy-start(f32[512,32]{0,1:T(8,128)S(1)} %get-tuple-element.663) | copy-start | bytes 196612
  55.1 53.7 %copy-start.22 = (f32[512,32]{0,1:T(8,128)}, f32[512,32]{0,1:T(8,128)S(1)}, u32[]{:S(2)}) copy-start(f32[512,32]{0,1:T(8,128)S(1)} %get-tuple-element.664) | copy-start | bytes 196612
  55.7 53.2 %copy-start.33 = (f32[512,2]{0,1:T(2,128)}, f32[512,2]{0,1:T(2,128)S(1)}, u32[]{:S(2)}) copy-start(f32[512,2]{0,1:T(2,128)S(1)} %get-tuple-element.667) | copy-start | bytes 12292
  108.9 75.3 %copy-start.16 = (bf16[128,1024]{1,0:T(8,128)(2,1)S(1)}, bf16[128,1024]{1,0:T(8,128)(2,1)}, u32[]{:S(2)}) copy-start(bf16[128,1024]{1,0:T(8,128)(2,1)} %param.29) | copy-start | bytes 786436
  184.1 82.5 %copy-start.3 = (bf16[512,1,2,64]{0,3,2,1:T(8,128)(2,1)}, bf16[512,1,2,64]{0,3,2,1:T(8,128)(2,1)S(1)}, u32[]{:S(2)}) copy-start(bf16[512,1,2,64]{0,3,2,1:T(8,128)(2,1)S(1)} %get-tuple-element.889) | copy-start | bytes 393220
  184.2 82.4 %copy-start.12 = (bf16[1,2,512,64]{2,3,1,0:T(8,128)(2,1)}, bf16[1,2,512,64]{2,3,1,0:T(8,128)(2,1)S(1)}, u32[]{:S(2)}) copy-start(bf16[1,2,512,64]{2,3,1,0:T(8,128)(2,1)S(1)} %fusion.59) | copy-start | bytes 393220
  185.7 77.3 %all-gather.10.cloned.1.call-start = ((), (), s32[]{:S(2)}) async-start(), calls=%async_computation.12 | async-start | bytes 1179648 | tf_op jit(solution)/shard_map/all_gather | solution.py:163
  221.7 132.8 %copy-start.42 = (f32[64]{0:T(128)}, f32[64]{0:T(128)S(1)}, u32[]{:S(2)}) copy-start(f32[64]{0:T(128)S(1)} %fusion.86) | copy-start | bytes 772
  223.3 81.2 %all-gather.12.cloned.1.call-start = ((), (), s32[]{:S(2)}) async-start(), calls=%async_computation.14 | async-start | bytes 1179648 | tf_op jit(solution)/shard_map/all_gather | solution.py:164
  223.9 128.9 %reduce-scatter.17.cloned.1.call-start = ((), (), s32[]{:S(2)}) async-start(), calls=%async_computation.15 | async-start | bytes 1179648 | tf_op jit(solution)/shard_map/reduce_scatter | solution.py:200
  312.3 83.6 %all-gather.14.cloned.1.call-start = ((), (), s32[]{:S(2)}) async-start(), calls=%async_computation.16 | async-start | bytes 1179648 | tf_op jit(solution)/shard_map/all_gather | solution.py:211
  356.2 244.4 %reduce-scatter.23.cloned.1.call-start = ((), (), s32[]{:S(2)}) async-start(), calls=%async_computation.19 | async-start | bytes 1392640 | tf_op jit(solution)/shard_map/reduce_scatter | solution.py:196
  359.8 242.5 %reduce-scatter.27.cloned.1.call-start = ((), (), s32[]{:S(2)}) async-start(), calls=%async_computation.21 | async-start | bytes 2506752
  550.9 40.4 %all-to-all-start = ((bf16[16,512,128]{1,2,0:T(8,128)(2,1)}), bf16[16,512,128]{1,2,0:T(8,128)(2,1)}, u32[]{:S(2)}, u32[]{:S(2)}) async-start(bf16[16,512,128]{1,2,0:T(8,128)(2,1)} %copy.71), calls=%async_computation.3 | async-start | bytes 4194304 | tf_op jit(solution)/shard_map/all_to_all | solution.py:29
  562.8 66.7 %reduce-scatter.21.cloned.1.call-start = ((), (), s32[]{:S(2)}) async-start(), calls=%async_computation.18 | async-start | bytes 278528 | tf_op jit(solution)/shard_map/reduce_scatter | solution.py:308
  565.4 132.8 %reduce-scatter.25.cloned.1.call-start = ((), (), s32[]{:S(2)}) async-start(), calls=%async_computation.20 | async-start | bytes 557056
  595.9 141.8 %reduce-scatter.19.cloned.1.call-start = ((), (), s32[]{:S(2)}) async-start(), calls=%async_computation.17 | async-start | bytes 1179648 | tf_op jit(solution)/shard_map/reduce_scatter | solution.py:279
  598.4 209.2 %reduce-scatter.15.cloned.1.call-start = ((), (), s32[]{:S(2)}) async-start(), calls=%async_computation.13 | async-start | bytes 1179648 | tf_op jit(solution)/shard_map/reduce_scatter | solution.py:173
  600.5 137.2 %copy-start.32 = (f32[1024]{0:T(1024)S(1)}, f32[1024]{0:T(1024)}, u32[]{:S(2)}) copy-start(f32[1024]{0:T(1024)} %param.23) | copy-start | bytes 12292
  600.5 137.2 %copy-start.49 = (f32[64]{0:T(128)S(1)}, f32[64]{0:T(128)}, u32[]{:S(2)}) copy-start(f32[64]{0:T(128)} %copy-done.48) | copy-start | bytes 772
  600.5 138.4 %copy-start.41 = (f32[1024]{0:T(1024)S(1)}, f32[1024]{0:T(1024)}, u32[]{:S(2)}) copy-start(f32[1024]{0:T(1024)} %get-tuple-element.592) | copy-start | bytes 12292
  600.5 207.1 %copy-start.55 = (f32[64]{0:T(128)S(1)}, f32[64]{0:T(128)}, u32[]{:S(2)}) copy-start(f32[64]{0:T(128)} %copy-done.54) | copy-start | bytes 772
  600.5 207.1 %copy-start.6 = (bf16[64,1024]{1,0:T(8,128)(2,1)S(1)}, bf16[64,1024]{1,0:T(8,128)(2,1)}, u32[]{:S(2)}) copy-start(bf16[64,1024]{1,0:T(8,128)(2,1)} %reduce-scatter.13.cloned.1.call-done) | copy-start | bytes 393220
  600.5 207.1 %copy-start.9 = (bf16[64,1024]{1,0:T(8,128)(2,1)S(1)}, bf16[64,1024]{1,0:T(8,128)(2,1)}, u32[]{:S(2)}) copy-start(bf16[64,1024]{1,0:T(8,128)(2,1)} %reduce-scatter.17.cloned.1.call-done) | copy-start | bytes 393220
  600.5 207.1 %copy-start.11 = (bf16[64,1024]{1,0:T(8,128)(2,1)S(1)}, bf16[64,1024]{1,0:T(8,128)(2,1)}, u32[]{:S(2)}) copy-start(bf16[64,1024]{1,0:T(8,128)(2,1)} %param.20) | copy-start | bytes 393220
  600.6 207.1 %copy-start.29 = (f32[1024]{0:T(1024)S(1)}, f32[1024]{0:T(1024)}, u32[]{:S(2)}) copy-start(f32[1024]{0:T(1024)} %param.30) | copy-start | bytes 12292
  600.6 207.1 %copy-start.43 = (f32[64]{0:T(128)S(1)}, f32[64]{0:T(128)}, u32[]{:S(2)}) copy-start(f32[64]{0:T(128)} %copy-done.42) | copy-start | bytes 772
  600.6 207.1 %copy-start.53 = (f32[64]{0:T(128)S(1)}, f32[64]{0:T(128)}, u32[]{:S(2)}) copy-start(f32[64]{0:T(128)} %copy-done.52) | copy-start | bytes 772
  (62 other events, 754.2 us)
Sparse Core Ops, SparseCore 0:
  10.3 39.1 all-gather.5
  54.8 53.9 all-gather.7
  185.8 34.7 reduce-scatter.12
  223.5 39.4 all-gather.9
  264.5 39.9 all-gather.11
  312.5 40.3 reduce-scatter.16
  356.3 39.5 all-gather.13
  399.8 69.9 reduce-scatter.22
  473.7 71.4 reduce-scatter.26
  567.0 62.4 reduce-scatter.20
  633.7 64.3 reduce-scatter.24
  700.4 37.2 reduce-scatter.18
  740.1 40.1 reduce-scatter.14
where the time goes:
time: 821 us; the launch traced here: 816 us
  waiting for transfers between devices  417 us (51%)
  matrix products  166 us (20%)
  other arithmetic  79.4 us (10%)
  blocking collectives  68.7 us (8%)
  local copies, waits for them, and re-layouts  55.1 us (7%)
  between operations  14.9 us (2%)
  starting transfers between devices  12.6 us (2%)
    psum x1, blocking collectives, per_device(): lax.psum((first_gain_grad, query_gain_grad, key_gain_grad, second_gain_gr...  68.7 us
    unnamed x15, waiting for transfers between devices  68 us
    all_gather x1, waiting for transfers between devices, per_device(): piece = lax.all_gather(pairs, 'ctx', axis=0, tiled=True)  53 us
    reduce_scatter x1, waiting for transfers between devices, per_device(): lax.psum_scatter((jnp.dot(gate_grad_b, w_gate.T, preferred_element_type=j...  40.5 us
    all_gather x1, waiting for transfers between devices, per_device(): lax.all_gather(normed_two.astype(jnp.bfloat16), 'tp', axis=0, tiled=True)  39 us
    all_gather x1, waiting for transfers between devices, per_device(): lax.all_gather(cotangent, 'tp', axis=0, tiled=True)  36.1 us
    reduce_scatter x1, waiting for transfers between devices, per_device(): lax.psum_scatter((total_rows + jnp.dot(value_pre_b, w_value.T, preferred_...  35.5 us
    all_gather x1, waiting for transfers between devices, per_device(): lax.all_gather(normed.astype(jnp.bfloat16), 'tp', axis=0, tiled=True)  35 us
  transfers between devices with their start and end apart: 14, of which 11 were waited for; matrix products, arithmetic and copies ran while one was open for 25% of the time, Pallas kernels for 0%

commit v1 on v0

v1 whole, which is shorter than its diff:
```python
from functools import partial
import math

import jax
import jax.numpy as jnp
from jax import lax
from jax.experimental import pallas as pl
from jax.experimental.pallas import tpu as pltpu
from jax.sharding import PartitionSpec as P

eps = 1e-05
theta = 1000000.0
bf16 = jnp.bfloat16
f32 = jnp.float32
vmem_bytes = 56 * 1024 * 1024
log2e = math.log2(math.e)
HEAD = 64
LANES = 128


def dot(a, b):
    return jnp.dot(a, b, preferred_element_type=f32)


def dot_t(a, b):
    return lax.dot_general(a, b, (((1,), (1,)), ((), ())), preferred_element_type=f32)


def t_dot(a, b):
    return lax.dot_general(a, b, (((0,), (0,)), ((), ())), preferred_element_type=f32)


def call(kernel, out_shape, **more):
    return pl.pallas_call(
        kernel,
        out_shape=out_shape,
        compiler_params=pltpu.CompilerParams(vmem_limit_bytes=vmem_bytes),
        **more,
    )


def in_vmem(count):
    return [pl.BlockSpec(memory_space=pltpu.VMEM)] * count


in_smem = pl.BlockSpec(memory_space=pltpu.SMEM)


def exchange(x, axis, groups=None):
    return lax.all_to_all(x, axis, 0, 0, axis_index_groups=groups, tiled=True)


def spread(x, axis, count, groups=None):
    return exchange(jnp.broadcast_to(x[None], (count, *x.shape)), axis, groups)


def left_half(shape):
    return lax.broadcasted_iota(jnp.int32, shape, 1) < HEAD


def swap_quarters(v):
    lane = lax.broadcasted_iota(jnp.int32, v.shape, 1)
    return jnp.where(lane % HEAD < HEAD // 2, pltpu.roll(v, LANES - 32, 1), pltpu.roll(v, 32, 1))


def head_mean(v, left):
    first = jnp.sum(jnp.where(left, v, 0.0), axis=1, keepdims=True)
    second = jnp.sum(jnp.where(left, 0.0, v), axis=1, keepdims=True)
    return jnp.where(left, first, second) * (1.0 / HEAD)


def project_kernel(
    x_ref, gain_ref, w_ref, head_gain_ref, cos_ref, sin_ref,
    normed_ref, pre_ref, qx_ref, qz_ref, kv_ref,
):
    x = x_ref[...].astype(f32)
    scaled = x * lax.rsqrt(jnp.mean(x * x, axis=1, keepdims=True) + eps)
    normed = (scaled * gain_ref[...]).astype(bf16)
    normed_ref[...] = normed
    pre = dot(normed, w_ref[...])
    pre_ref[...] = pre
    cosine, sine = cos_ref[...], sin_ref[...]
    span = x.shape[0]
    left = left_half((span, LANES))

    def prepared(v, gain):
        v = v * lax.rsqrt(head_mean(v * v, left) + eps) * gain
        return v * cosine + swap_quarters(v) * sine

    query = prepared(pre[:, :LANES], head_gain_ref[0:1, :])
    pair = pre[:, LANES:]
    key = prepared(pair, head_gain_ref[1:2, :])
    kv_ref[...] = jnp.where(left, key, pair).astype(bf16)
    for head in range(2):
        own = query if head == 0 else pltpu.roll(query, HEAD, 1)
        own = jnp.where(left, own, 0.0)
        rows = pl.ds(head * span, span)
        qx_ref[rows, :] = (own * (log2e / math.sqrt(HEAD))).astype(bf16)
        qz_ref[rows, :] = (own.astype(bf16).astype(f32) * (1.0 / math.sqrt(HEAD))).astype(bf16)


def earlier_spans(order_ref, list_ref, rank, core, blocks):
    def look(block, count):
        list_ref[count] = block
        slot = ((block // 2) * 2 + core) * 2 + block % 2
        return count + (order_ref[slot] < rank).astype(jnp.int32)

    return lax.fori_loop(0, blocks, look, jnp.int32(0))


def block_rows(index, span):
    return pl.ds(pl.multiple_of(index * span, span), span)


def in_groups(count, size, body):
    whole = count // size

    def some(step, carry):
        body([step * size + k for k in range(size)])
        return carry

    lax.fori_loop(0, whole, some, 0)

    def one(step, carry):
        body([step])
        return carry

    lax.fori_loop(whole * size, count, one, 0)


def attend_kernel(last, order_ref, qx_ref, kv_ref, *refs):
    if last:
        start_ref, out_ref, attended_ref, list_ref, acc_ref = refs
    else:
        acc_ref, list_ref = refs
    me = lax.axis_index("ctx")
    core = me % 2
    side = 1 - core if last else core
    span = qx_ref.shape[0] // 4
    blocks = kv_ref.shape[0] // span
    left = left_half((span, LANES))
    one = jnp.ones((span, LANES), bf16)
    for slot in range(2):
        rows = pl.ds(slot * 2 * span, 2 * span)
        count = earlier_spans(order_ref, list_ref, order_ref[me * 2 + slot], side, blocks)

        def product(index, mask=None):
            pair = kv_ref[block_rows(index, span), :]
            weights = jnp.exp2(dot_t(qx_ref[rows, :], pair))
            if mask is not None:
                weights = jnp.where(mask, weights, 0.0)
            return dot(weights.astype(bf16), jnp.where(left, one, pair))

        if last:
            acc_ref[rows, :] = start_ref[rows, :]
        else:
            row = lax.broadcasted_iota(jnp.int32, (2 * span, span), 0) % span
            col = lax.broadcasted_iota(jnp.int32, (2 * span, span), 1)
            acc_ref[rows, :] = product((me // 2) * 2 + slot, row >= col)

        def add(steps):
            acc_ref[rows, :] += sum(product(list_ref[step]) for step in steps)

        in_groups(count, 4, add)
        if last:
            for head in range(2):
                part = pl.ds((slot * 2 + head) * span, span)
                acc = acc_ref[part, :]
                turned = pltpu.roll(acc, HEAD, 1)
                out = jnp.where(left, jnp.log2(acc), acc / jnp.where(left, 1.0, turned))
                out_ref[part, :] = out
                if head == 0:
                    first = pltpu.roll(out, HEAD, 1)
                else:
                    attended_ref[pl.ds(slot * span, span), :] = jnp.where(left, first, out).astype(bf16)


def pull_kernel(last, order_ref, kv_ref, qz_ref, *refs):
    if last:
        qb_ref, dx_ref, dz_ref, start_ref, dkv_ref, dq_ref, list_ref = refs
        dq_ref[...] = start_ref[...]
    else:
        qx_ref, out_ref, base_ref, recv_ref, dkv_ref, dq_ref, qb_ref, dx_ref, dz_ref, list_ref = refs
        dq_ref[...] = jnp.zeros_like(dq_ref)
    dkv_ref[...] = jnp.zeros_like(dkv_ref)
    me = lax.axis_index("ctx")
    core = me % 2
    side = core if last else 1 - core
    span = qz_ref.shape[0] // 4
    blocks = kv_ref.shape[0] // span
    left = left_half((span, LANES))
    lane = lax.broadcasted_iota(jnp.int32, (span, LANES), 1)
    one = jnp.ones((span, LANES), bf16)
    if not last:
        for slot in range(2):
            rows = pl.ds(slot * span, span)
            mixed = base_ref[rows, :]
            for peer in range(recv_ref.shape[0]):
                mixed = mixed + recv_ref[peer, rows, :].astype(f32)
            mixed = mixed.astype(bf16).astype(f32)
            for head in range(2):
                part = pl.ds((slot * 2 + head) * span, span)
                own = jnp.where(left, 0.0, pltpu.roll(mixed, HEAD, 1) if head == 0 else mixed)
                dz_ref[part, :] = own.astype(bf16)
                out = out_ref[part, :]
                delta = jnp.sum(own * out, axis=1, keepdims=True)
                high = delta.astype(bf16).astype(f32)
                low = (delta - high).astype(bf16).astype(f32)
                own = jnp.where(lane == 0, -high, jnp.where(lane == 1, -low, own))
                dx_ref[part, :] = own.astype(bf16)
                total = pltpu.roll(out, HEAD, 1)
                high = total.astype(bf16).astype(f32)
                middle = (total - high).astype(bf16).astype(f32)
                low = total - high - middle
                query = qx_ref[part, :].astype(f32)
                query = jnp.where(lane == HEAD, -high, query)
                query = jnp.where(lane == HEAD + 1, -middle, query)
                query = jnp.where(lane == HEAD + 2, -low, query)
                qb_ref[part, :] = query.astype(bf16)
    for slot in range(2):
        rows = pl.ds(slot * 2 * span, 2 * span)
        count = earlier_spans(order_ref, list_ref, order_ref[me * 2 + slot], side, blocks)

        def product(index, mask=None):
            part = block_rows(index, span)
            pair = kv_ref[part, :]
            weights = jnp.exp2(dot_t(jnp.where(left, pair, one), qb_ref[rows, :]))
            if mask is not None:
                weights = jnp.where(mask, weights, 0.0)
            pulled = dot_t(jnp.where(left, one, pair), dx_ref[rows, :])
            score = (weights * pulled).astype(bf16)
            dkv_ref[part, :] += dot(score, qz_ref[rows, :]) + dot(weights.astype(bf16), dz_ref[rows, :])
            return t_dot(score, pair)

        def add(steps):
            dq_ref[rows, :] += sum(product(list_ref[step]) for step in steps)

        if last:
            row = lax.broadcasted_iota(jnp.int32, (span, 2 * span), 0)
            col = lax.broadcasted_iota(jnp.int32, (span, 2 * span), 1) % span
            dq_ref[rows, :] += product((me // 2) * 2 + slot, col >= row)
        in_groups(count, 2, add)


def back_kernel(
    dq_ref, recv_ref, pre_ref, head_gain_ref, cos_ref, sin_ref, pre_grad_ref, head_sums_ref
):
    span = cos_ref.shape[0] // 2
    left = left_half((span, LANES))

    def pulled(grad, pre, gain, cosine, sine):
        turned = grad * cosine - swap_quarters(grad) * sine
        factor = lax.rsqrt(head_mean(pre * pre, left) + eps)
        unit = pre * factor
        sums = jnp.sum(turned * unit, axis=0, keepdims=True)
        scaled = turned * gain
        return (scaled - unit * head_mean(scaled * unit, left)) * factor, sums

    totals = [0.0, 0.0]
    for slot in range(2):
        rows = pl.ds(slot * span, span)
        cosine, sine = cos_ref[rows, :], sin_ref[rows, :]
        first = dq_ref[pl.ds(slot * 2 * span, span), :]
        second = dq_ref[pl.ds((slot * 2 + 1) * span, span), :]
        grad = jnp.where(left, first, pltpu.roll(second, HEAD, 1)) * (1.0 / math.sqrt(HEAD))
        pair = recv_ref[0, rows, :].astype(f32)
        for peer in range(1, recv_ref.shape[0]):
            pair = pair + recv_ref[peer, rows, :].astype(f32)
        query, sums = pulled(
            grad, pre_ref[rows, :LANES], head_gain_ref[0:1, :], cosine, sine
        )
        totals[0] = totals[0] + sums
        key, sums = pulled(
            jnp.where(left, pair, 0.0), pre_ref[rows, LANES:], head_gain_ref[1:2, :], cosine, sine
        )
        totals[1] = totals[1] + sums
        pre_grad_ref[rows, :LANES] = query.astype(bf16)
        pre_grad_ref[rows, LANES:] = jnp.where(left, key, pair).astype(bf16)
    folded = totals[0] + pltpu.roll(totals[0], HEAD, 1)
    head_sums_ref[...] = jnp.where(left_half((1, LANES)), folded, pltpu.roll(totals[1], HEAD, 1))


def turning(positions, span_order, me, span):
    table = positions.reshape(-1, span)
    own = [lax.dynamic_index_in_dim(table, span_order[me * 2 + k], 0, False) for k in range(2)]
    places = jnp.concatenate(own).astype(f32)
    freqs = theta ** (-(jnp.arange(HEAD // 2, dtype=f32) * 2.0 / HEAD))
    turned = places[:, None] * freqs[None, :]
    cosine, sine = jnp.cos(turned), jnp.sin(turned)
    return (
        jnp.concatenate([cosine] * 4, axis=1),
        jnp.concatenate([-sine, sine, -sine, sine], axis=1),
    )


def per_device(
    tokens, cotangent, positions, span_order, first_gain, w_query, w_key, w_value,
    query_gain, key_gain, w_out, second_gain, w_gate, w_up, w_down,
):
    ctx_count = lax.axis_size("ctx")
    tp_count = lax.axis_size("tp")
    me = lax.axis_index("ctx")
    mine = lax.axis_index("tp")
    part, width = tokens.shape
    local = part * tp_count
    span = local // 2
    half = ctx_count // 2
    heads = w_out.shape[0]
    hidden_width = w_gate.shape[1]
    same_core = [[2 * k + core for k in range(half)] for core in range(2)]
    other_core = [(k, k ^ 1) for k in range(ctx_count)]
    shape = jax.ShapeDtypeStruct

    x_all = spread(tokens, "tp", tp_count).reshape(local, width)
    side = lax.all_gather(jnp.concatenate([cotangent, w_out], axis=0), "tp", axis=0, tiled=False)
    dy_all = side[:, :part].reshape(local, width)
    w_out_all = side[:, part:]
    w_qkv = jnp.concatenate([w_query, w_key, w_value], axis=1)
    w_qkv_all = lax.all_gather(w_qkv, "tp", axis=0, tiled=False)
    cosine, sine = turning(positions, span_order, me, span)
    head_gain = jnp.stack(
        [jnp.concatenate([query_gain, query_gain]), jnp.concatenate([key_gain, jnp.ones_like(key_gain)])]
    )

    by_span = lambda rows, cols: pl.BlockSpec((rows, cols), lambda k: (k, 0))
    whole = lambda a: pl.BlockSpec(a.shape, lambda k: (0, 0))
    gain_row = first_gain.reshape(1, width)
    normed, pre, qx, qz, kv = call(
        project_kernel,
        (
            shape((local, width), bf16),
            shape((local, 2 * LANES), f32),
            shape((2 * local, LANES), bf16),
            shape((2 * local, LANES), bf16),
            shape((local, LANES), bf16),
        ),
        grid=(2,),
        in_specs=[
            by_span(span, width), whole(gain_row), whole(w_qkv), whole(head_gain),
            by_span(span, LANES), by_span(span, LANES),
        ],
        out_specs=(
            by_span(span, width), by_span(span, 2 * LANES), by_span(2 * span, LANES),
            by_span(2 * span, LANES), by_span(span, LANES),
        ),
        name="project",
    )(x_all, gain_row, w_qkv, head_gain, cosine, sine)

    kv_own = spread(kv, "ctx", half, same_core).reshape(half * local, LANES)
    kv_other = lax.ppermute(kv_own, "ctx", other_core)
    acc = call(
        partial(attend_kernel, False),
        shape((2 * local, LANES), f32),
        in_specs=[in_smem, *in_vmem(2)],
        out_specs=pl.BlockSpec(memory_space=pltpu.VMEM),
        scratch_shapes=[pltpu.SMEM((ctx_count + 1,), jnp.int32)],
        cost_estimate=pl.CostEstimate(flops=4 * 10**9, bytes_accessed=2**21, transcendentals=2**22),
        name="attend_own",
    )(span_order, qx, kv_own)
    out, attended = call(
        partial(attend_kernel, True),
        (shape((2 * local, LANES), f32), shape((local, LANES), bf16)),
        in_specs=[in_smem, *in_vmem(3)],
        out_specs=tuple(in_vmem(2)),
        scratch_shapes=[pltpu.SMEM((ctx_count + 1,), jnp.int32), pltpu.VMEM((2 * local, LANES), f32)],
        cost_estimate=pl.CostEstimate(flops=4 * 10**9, bytes_accessed=2**21, transcendentals=2**22),
        name="attend_other",
    )(span_order, qx, kv_other, acc)

    attended_all = spread(attended, "tp", tp_count)
    resid = x_all.astype(f32) + jnp.einsum(
        "tsd,tdm->sm", attended_all, w_out_all, preferred_element_type=f32
    )
    factor = lax.rsqrt(jnp.mean(resid * resid, axis=1, keepdims=True) + eps)
    unit = resid * factor
    normed_two = (unit * second_gain).astype(bf16)
    gate = dot(normed_two, w_gate)
    up = dot(normed_two, w_up)
    hidden_grad = dot_t(dy_all, w_down)
    sigma = jax.nn.sigmoid(gate)
    swish = gate * sigma
    hidden = (swish * up).astype(bf16)
    gate_grad = (hidden_grad * up * sigma * (1.0 + gate * (1.0 - sigma))).astype(bf16)
    up_grad = (hidden_grad * swish).astype(bf16)
    second_grad = dot_t(gate_grad, w_gate) + dot_t(up_grad, w_up)
    scaled = second_grad * second_gain
    resid_part = ((scaled - unit * jnp.mean(scaled * unit, axis=1, keepdims=True)) * factor).astype(bf16)
    second_sum = jnp.sum(second_grad * unit, axis=0)
    mixed_part = jnp.einsum("sm,tdm->tsd", resid_part, w_out_all, preferred_element_type=f32)
    mixed_recv = exchange(mixed_part.astype(bf16), "tp")
    mixed_base = dot_t(dy_all, w_out)

    down = dot(hidden, w_down).astype(bf16)
    rows_recv = exchange(
        jnp.concatenate([resid_part, down], axis=1).reshape(tp_count, part, 2 * width), "tp"
    )
    rows_sum = jnp.sum(rows_recv.astype(f32), axis=0)
    own_resid = lax.dynamic_slice_in_dim(resid, mine * part, part, 0)
    block_out = (own_resid + rows_sum[:, width:]).astype(bf16)
    resid_grad = cotangent.astype(f32) + rows_sum[:, :width]
    resid_grad_all = spread(resid_grad.astype(bf16), "tp", tp_count).reshape(local, width)
    grad_out = t_dot(resid_grad_all, attended)

    feed = jnp.concatenate(
        [t_dot(normed_two, gate_grad), t_dot(normed_two, up_grad), t_dot(dy_all, hidden)], axis=1
    ).astype(bf16)
    feed = lax.psum_scatter(feed, "ctx", scatter_dimension=0, tiled=True).astype(f32)
    grad_gate = feed[:, :hidden_width]
    grad_up = feed[:, hidden_width : 2 * hidden_width]
    grad_down = feed[:, 2 * hidden_width :].T

    dkv_shape = shape((half * local, LANES), f32)
    dq_shape = shape((2 * local, LANES), f32)
    q_shape = shape((2 * local, LANES), bf16)
    dkv_other, dq_other, qb, dx, dz = call(
        partial(pull_kernel, False),
        (dkv_shape, dq_shape, q_shape, q_shape, q_shape),
        in_specs=[in_smem, *in_vmem(6)],
        out_specs=tuple(in_vmem(5)),
        scratch_shapes=[pltpu.SMEM((ctx_count + 1,), jnp.int32)],
        cost_estimate=pl.CostEstimate(flops=10 * 10**9, bytes_accessed=2**22, transcendentals=2**22),
        name="pull_other",
    )(span_order, kv_other, qz, qx, out, mixed_base, mixed_recv)
    dkv_moved = lax.ppermute(dkv_other.astype(bf16), "ctx", other_core)
    dkv_own, dq = call(
        partial(pull_kernel, True),
        (dkv_shape, dq_shape),
        in_specs=[in_smem, *in_vmem(6)],
        out_specs=tuple(in_vmem(2)),
        scratch_shapes=[pltpu.SMEM((ctx_count + 1,), jnp.int32)],
        cost_estimate=pl.CostEstimate(flops=10 * 10**9, bytes_accessed=2**22, transcendentals=2**22),
        name="pull_own",
    )(span_order, kv_own, qz, qb, dx, dz, dq_other)
    dkv = (dkv_own + dkv_moved.astype(f32)).astype(bf16).reshape(half, local, LANES)
    dkv_recv = exchange(dkv, "ctx", same_core)

    pre_grad, head_sums = call(
        back_kernel,
        (shape((local, 2 * LANES), bf16), shape((1, LANES), f32)),
        in_specs=in_vmem(6),
        out_specs=tuple(in_vmem(2)),
        name="back",
    )(dq, dkv_recv, pre, head_gain, cosine, sine)
    grad_qkv = t_dot(normed, pre_grad)
    first_sum = jnp.sum(grad_qkv * w_qkv.astype(f32), axis=1) / first_gain
    sums = jnp.concatenate([first_sum, second_sum, head_sums[0], jnp.zeros((LANES,), f32)])
    extra = 16
    cols = 2 * LANES

    def with_sums(blocks, sums, count):
        rows = jnp.pad(sums.astype(bf16).reshape(-1, cols), ((0, extra - sums.shape[0] // cols), (0, 0)))
        if blocks.shape[2] > cols:
            rows = jnp.pad(rows, ((0, 0), (0, blocks.shape[2] - cols)))
        return jnp.concatenate([blocks, jnp.broadcast_to(rows[None], (count, extra, rows.shape[1]))], axis=1)

    tp_recv = exchange(with_sums(pre_grad.reshape(tp_count, part, cols), sums, tp_count), "tp")
    sums = jnp.sum(tp_recv[:, part:].astype(f32), axis=0)[: sums.shape[0] // cols].reshape(-1)
    grad_blocks = jnp.concatenate([grad_qkv, grad_out], axis=1).astype(bf16)
    grad_blocks = grad_blocks.reshape(ctx_count, width // ctx_count, cols + LANES)
    ctx_recv = jnp.sum(exchange(with_sums(grad_blocks, sums, ctx_count), "ctx").astype(f32), axis=0)
    own_width = width // ctx_count
    sums = ctx_recv[own_width:, :cols][: sums.shape[0] // cols].reshape(-1)
    grads = ctx_recv[:own_width]

    normed_grad = jnp.einsum(
        "tsc,tdc->sd", tp_recv[:, :part], w_qkv_all, preferred_element_type=f32
    )
    x = tokens.astype(f32)
    factor = lax.rsqrt(jnp.mean(x * x, axis=1, keepdims=True) + eps)
    unit = x * factor
    scaled = normed_grad * first_gain
    tokens_part = (scaled - unit * jnp.mean(scaled * unit, axis=1, keepdims=True)) * factor
    grad_tokens = (resid_grad + tokens_part).astype(bf16)
    return (
        block_out,
        grad_tokens,
        sums[:width],
        grads[:, :LANES],
        grads[:, LANES : LANES + HEAD],
        grads[:, LANES + HEAD : cols],
        sums[2 * width : 2 * width + HEAD],
        sums[2 * width + HEAD : 2 * width + 2 * HEAD],
        grads[:, cols:].T,
        sums[width : 2 * width],
        grad_gate,
        grad_up,
        grad_down,
    )


def solution(mesh):
    return jax.shard_map(
        per_device,
        mesh=mesh,
        in_specs=(
            P(("ctx", "tp"), None),
            P(("ctx", "tp"), None),
            P(),
            P(),
            P(),
            P(None, "tp"),
            P(None, "tp"),
            P(None, "tp"),
            P(),
            P(),
            P("tp", None),
            P(),
            P(None, "tp"),
            P(None, "tp"),
            P("tp", None),
        ),
        out_specs=(
            P(("ctx", "tp"), None),
            P(("ctx", "tp"), None),
            P(),
            P("ctx", "tp"),
            P("ctx", "tp"),
            P("ctx", "tp"),
            P(),
            P(),
            P("tp", "ctx"),
            P(),
            P("ctx", "tp"),
            P("ctx", "tp"),
            P("tp", "ctx"),
        ),
        check_vma=False,
    )
```

time: 821 us -> 343 us (0.42)
  waiting for transfers between devices: 417 us -> 98.5 us
  matrix products: 166 us -> 27.8 us
  other arithmetic: 79.4 us -> 23 us
  Pallas kernels: 0 us -> 53 us
  starting transfers between devices: 12.6 us -> 39.3 us
  local copies, waits for them, and re-layouts: 55.1 us -> 29.9 us
  blocking collectives: 68.7 us -> 49.9 us
    all_gather x5 -> x2, waiting for transfers between devices: 189 us -> 8.86 us  [the longest x1 8.86 us: per_device(): lax.all_gather(jnp.concatenate([cotangent, w_out], axis=0), 'tp', axis=0,...]
    dot_general x133 -> x15, matrix products: 166 us -> 27.8 us  [the longest x5 7.57 us: t_dot(): lax.dot_general(a, b, (((0,), (0,)), ((), ())), preferred_element_type=f32)]
    reduce_scatter x6 -> x0, waiting for transfers between devices: 135 us -> none  [the longest x1 40.5 us: per_device(): lax.psum_scatter((jnp.dot(gate_grad_b, w_gate.T, preferred_element_type=j...]
    psum x1 -> x0, blocking collectives: 68.7 us -> none  [per_device(): lax.psum((first_gain_grad, query_gain_grad, key_gain_grad, second_gain_gr...]
    unnamed x15 -> x4, waiting for transfers between devices: 68 us -> 3.62 us
    all_to_all x1 -> x7, waiting for transfers between devices: 24.4 us -> 86 us  [exchange(): return lax.all_to_all(x, axis, 0, 0, axis_index_groups=groups, tiled=True)]
    pallas_call x0 -> x6, Pallas kernels: none -> 53 us  [the longest x1 14.7 us: per_device(): call(partial(pull_kernel, False), (dkv_shape, dq_shape, q_shape, q_shape,...]
    all_to_all x0 -> x2, blocking collectives: none -> 49.9 us  [exchange(): return lax.all_to_all(x, axis, 0, 0, axis_index_groups=groups, tiled=True)]
  transfers between devices with their start and end apart: 14 -> 12, of which waited for: 11 -> 9; matrix products, arithmetic and copies ran while one was open for 25% -> 20% of each run, Pallas kernels for 0% -> 16%
where the time goes in v1:
time: 343 us; the launch traced here: 340 us
  waiting for transfers between devices  98.5 us (29%)
  Pallas kernels  53 us (15%)
  blocking collectives  49.9 us (15%)
  starting transfers between devices  39.3 us (11%)
  local copies, waits for them, and re-layouts  29.9 us (9%)
  matrix products  27.8 us (8%)
  other arithmetic  23 us (7%)
  between operations  18.2 us (5%)
    all_to_all x7, waiting for transfers between devices, exchange(): return lax.all_to_all(x, axis, 0, 0, axis_index_groups=groups, tiled=True)  86 us
    all_to_all x2, blocking collectives, exchange(): return lax.all_to_all(x, axis, 0, 0, axis_index_groups=groups, tiled=True)  49.9 us
    all_to_all x7, starting transfers between devices, exchange(): return lax.all_to_all(x, axis, 0, 0, axis_index_groups=groups, tiled=True)  34.4 us
    unnamed x80, local copies, waits for them, and re-layouts  18.2 us
    pallas_call x1, Pallas kernels, per_device(): call(partial(pull_kernel, False), (dkv_shape, dq_shape, q_shape, q_shape,...  14.7 us
    pallas_call x1, Pallas kernels, per_device(): call(partial(pull_kernel, True), (dkv_shape, dq_shape), in_specs=[in_smem...  14.4 us
    all_gather x1, waiting for transfers between devices, per_device(): lax.all_gather(jnp.concatenate([cotangent, w_out], axis=0), 'tp', axis=0,...  8.86 us
    pallas_call x1, Pallas kernels, per_device(): call(partial(attend_kernel, True), (shape((2 * local, LANES), f32), shape...  8.21 us
  transfers between devices with their start and end apart: 12, of which 9 were waited for; matrix products, arithmetic and copies ran while one was open for 20% of the time, Pallas kernels for 16%

profile of v1, /device:TPU:1, one launch (start us, length us, event | category | flops | bytes accessed | tf_op | source)
XLA Modules:
  0.0 339.8 jit_solution(5019180322225588368)
XLA Ops:
  11.3 7.0 %all-to-all-start = ((bf16[8,64,1024]{2,1,0:T(8,128)(2,1)}), bf16[8,64,1024]{2,1,0:T(8,128)(2,1)S(1)}, u32[]{:S(2)}, u32[]{:S(2)}) async-start(bf16[8,64,1024]{2,1,0:T(8,128)(2,1)} %broadcast_in_dim.14), calls=%async_computation | async-start | bytes 2097152 | tf_op jit(solution)/shard_map/all_to_all | solution.py:50
  27.1 12.9 %all-to-all-done = bf16[8,64,1024]{2,1,0:T(8,128)(2,1)S(1)} async-done(((bf16[8,64,1024]{2,1,0:T(8,128)(2,1)}), bf16[8,64,1024]{2,1,0:T(8,128)(2,1)S(1)}, u32[]{:S(2)}, u32[]{:S(2)}) %all-to-all-start) | async-done | bytes 1048608 | tf_op jit(solution)/shard_map/all_to_all | solution.py:50
  41.0 3.7 %project.1 = (bf16[512,1024]{1,0:T(8,128)(2,1)}, f32[512,256]{1,0:T(8,128)}, bf16[1024,128]{1,0:T(8,128)(2,1)}, bf16[1024,128]{1,0:T(8,128)(2,1)}, bf16[512,128]{1,0:T(8,128)(2,1)}) custom-call(bf16[512,1024]{1,0:T(8,128)(2,1)} %bitcast.81, f32[1,1024]{1,0:T(1,128)} %bitcast.92, bf16[1024,256]{1,0:T(8,128)(2,1)} %pad_maximum_fusion.3.w_ref, ...), custom_call_target="tpu_custom_call" | custom-call | tf_op jit(solution)/shard_map/project/pallas_call | solution.py:328
  45.7 23.7 %all_to_all.45 = bf16[8,512,128]{2,1,0:T(8,128)(2,1)S(1)} all-to-all(bf16[8,512,128]{2,1,0:T(8,128)(2,1)S(1)} %broadcast_in_dim.15), channel_id=1, replica_groups={{0,16,32,48,64,80,96,112},{8,24,40,56,72,88,104,120},{1,17,33,49,65,81,..., dimensions={0} | all-to-all | bytes 2097152 | tf_op jit(solution)/shard_map/all_to_all | solution.py:50
  69.4 3.4 %collective-permute-start = (bf16[4096,128]{1,0:T(8,128)(2,1)S(1)}, bf16[4096,128]{1,0:T(8,128)(2,1)S(1)}, u32[]{:S(2)}, u32[]{:S(2)}) collective-permute-start(bf16[4096,128]{1,0:T(8,128)(2,1)S(1)} %bitcast.84), channel_id=1, source_target_pairs={{0,8},{8,0},{16,24},{24,16},{32,40},{40,32},{48,56},{56,48},{64,72... | collective-permute-start | bytes 3145736 | tf_op jit(solution)/shard_map/ppermute | solution.py:350
  72.9 8.1 %attend_own.1.refs_0_ = f32[1024,128]{1,0:T(8,128)} custom-call(s32[32]{0:T(128)} %order_ref.7, bf16[1024,128]{1,0:T(8,128)(2,1)} %get-tuple-element.29.qx_ref.refs_0_, bf16[4096,128]{1,0:T(8,128)(2,1)} %bitcast.85), custom_call_target="tpu_custom_call" | custom-call | flops 4000000000 | bytes 2097152 | tf_op jit(solution)/shard_map/attend_own/pallas_call | solution.py:351
  82.0 8.2 %attend_other.1 = (f32[1024,128]{1,0:T(8,128)}, bf16[512,128]{1,0:T(8,128)(2,1)}) custom-call(s32[32]{0:T(128)} %order_ref.7, bf16[1024,128]{1,0:T(8,128)(2,1)} %get-tuple-element.29.qx_ref.refs_0_, bf16[4096,128]{1,0:T(8,128)(2,1)} %copy-done.32, f32[1024,128]{1,0:T(8,128)} %attend_own.1.refs_0_), custom_call_target="tpu_custom_call" | custom-call | flops 4000000000 | bytes 2097152 | tf_op jit(solution)/shard_map/attend_other/pallas_call | solution.py:360
  92.3 4.2 %all-to-all-start.2 = ((bf16[8,512,128]{2,1,0:T(8,128)(2,1)}), bf16[8,512,128]{2,1,0:T(8,128)(2,1)}, u32[]{:S(2)}, u32[]{:S(2)}) async-start(bf16[8,512,128]{2,1,0:T(8,128)(2,1)} %broadcast_in_dim.16), calls=%async_computation.2 | async-start | bytes 2097152 | tf_op jit(solution)/shard_map/all_to_all | solution.py:50
  97.3 8.9 %all-gather.5.cloned.1.call-done = bf16[1536,1024]{1,0:T(8,128)(2,1)} async-done(((bf16[192,1024]{1,0:T(8,128)(2,1)}), bf16[1536,1024]{1,0:T(8,128)(2,1)}) %all-gather.5.cloned.1.call-update) | async-done | bytes 3145744 | tf_op jit(solution)/shard_map/all_gather | solution.py:315
  106.1 2.3 slice.93
  108.4 7.2 %all-to-all-done.2 = bf16[8,512,128]{2,1,0:T(8,128)(2,1)} async-done(((bf16[8,512,128]{2,1,0:T(8,128)(2,1)}), bf16[8,512,128]{2,1,0:T(8,128)(2,1)}, u32[]{:S(2)}, u32[]{:S(2)}) %all-to-all-start.2) | async-done | bytes 1048608 | tf_op jit(solution)/shard_map/all_to_all | solution.py:50
  115.6 3.5 %multiply_reduce_fusion.2 = (f32[512]{0:T(512)S(1)}, f32[512,1024]{1,0:T(8,128)S(1)}) fusion(bf16[8,512,128]{2,1,0:T(8,128)(2,1)} %all-to-all-done.2, bf16[8,192,1024]{2,1,0:T(8,128)(2,1)} %bitcast.89, bf16[512,1024]{1,0:T(8,128)(2,1)} %bitcast.82), kind=kOutput, calls=%fused_computation.9 | convolution fusion | flops 1075838464 | bytes 6293504 | tf_op jit(solution)/shard_map/tsd,tdm->sm/dot_general | solution.py:371
  132.5 4.4 %all-to-all-start.4 = ((bf16[8,512,128]{2,1,0:T(8,128)(2,1)}), bf16[8,512,128]{2,1,0:T(8,128)(2,1)}, u32[]{:S(2)}, u32[]{:S(2)}) async-start(bf16[8,512,128]{2,1,0:T(8,128)(2,1)} %fusion.9), calls=%async_computation.4 | async-start | bytes 2097152 | tf_op jit(solution)/shard_map/all_to_all | solution.py:50
  136.9 2.4 fusion.36.refs_2_
  139.3 24.7 %all-to-all-done.4.refs_3_ = bf16[8,512,128]{2,1,0:T(8,128)(2,1)} async-done(((bf16[8,512,128]{2,1,0:T(8,128)(2,1)}), bf16[8,512,128]{2,1,0:T(8,128)(2,1)}, u32[]{:S(2)}, u32[]{:S(2)}) %all-to-all-start.4) | async-done | bytes 1048608 | tf_op jit(solution)/shard_map/all_to_all | solution.py:50
  163.9 14.7 %pull_other.1 = (f32[4096,128]{1,0:T(8,128)}, f32[1024,128]{1,0:T(8,128)}, bf16[1024,128]{1,0:T(8,128)(2,1)}, bf16[1024,128]{1,0:T(8,128)(2,1)}, bf16[1024,128]{1,0:T(8,128)(2,1)}) custom-call(s32[32]{0:T(128)} %order_ref.7, bf16[4096,128]{1,0:T(8,128)(2,1)} %copy-done.32, bf16[1024,128]{1,0:T(8,128)(2,1)} %get-tuple-element.32.qz_ref, ...), custom_call_target="tpu_custom_call" | custom-call | flops 10000000000 | bytes 4194304 | tf_op jit(solution)/shard_map/pull_other/pallas_call | solution.py:415
  181.6 14.4 %pull_own.1 = (f32[4096,128]{1,0:T(8,128)}, f32[1024,128]{1,0:T(8,128)}) custom-call(s32[32]{0:T(128)} %order_ref.7, bf16[4096,128]{1,0:T(8,128)(2,1)} %bitcast.86, bf16[1024,128]{1,0:T(8,128)(2,1)} %get-tuple-element.32.qz_ref, bf16[1024,128]{1,0:T(8,128)(2,1)} %get-tuple-element.34.refs_0_, bf16[1024,128]{1,0:T(8,128)(2,1)} %get-tuple-element.35.refs_1_, ...), custom_call_target="tpu_custom_call" | custom-call | flops 10000000000 | bytes 4194304 | tf_op jit(solution)/shard_map/pull_own/pallas_call | solution.py:425
  195.9 2.8 add_convert_fusion
  198.7 5.2 %all-to-all-start.5 = ((bf16[8,512,128]{2,1,0:T(8,128)(2,1)}), bf16[8,512,128]{2,1,0:T(8,128)(2,1)}, u32[]{:S(2)}, u32[]{:S(2)}) async-start(bf16[8,512,128]{2,1,0:T(8,128)(2,1)} %bitcast.83), calls=%async_computation.5 | async-start | bytes 2097152 | tf_op jit(solution)/shard_map/all_to_all | solution.py:50
  210.1 11.5 %all-to-all-done.5.recv_ref = bf16[8,512,128]{2,1,0:T(8,128)(2,1)} async-done(((bf16[8,512,128]{2,1,0:T(8,128)(2,1)}), bf16[8,512,128]{2,1,0:T(8,128)(2,1)}, u32[]{:S(2)}, u32[]{:S(2)}) %all-to-all-start.5) | async-done | bytes 1048608 | tf_op jit(solution)/shard_map/all_to_all | solution.py:50
  221.7 4.3 %all-to-all-start.3 = ((bf16[8,64,2048]{2,1,0:T(8,128)(2,1)}), bf16[8,64,2048]{2,1,0:T(8,128)(2,1)}, u32[]{:S(2)}, u32[]{:S(2)}) async-start(bf16[8,64,2048]{2,1,0:T(8,128)(2,1)} %bitcast.74), calls=%async_computation.3 | async-start | bytes 4194304 | tf_op jit(solution)/shard_map/all_to_all | solution.py:50
  231.7 5.8 %copy.58 = bf16[1024,1728]{1,0:T(8,128)(2,1)} copy(bf16[1024,1728]{0,1:T(8,128)(2,1)} %pad_maximum_fusion) | data formatting | bytes 7077888
  237.5 3.9 %back.1 = (bf16[512,256]{1,0:T(8,128)(2,1)}, f32[1,128]{1,0:T(1,128)}) custom-call(f32[1024,128]{1,0:T(8,128)} %get-tuple-element.38.dq_ref, bf16[8,512,128]{2,1,0:T(8,128)(2,1)} %all-to-all-done.5.recv_ref, f32[512,256]{1,0:T(8,128)} %get-tuple-element.41.pre_ref, f32[2,128]{1,0:T(2,128)} %pad_maximum_fusion.9.head_gain_ref, ...), custom_call_target="tpu_custom_call" | custom-call | tf_op jit(solution)/shard_map/back/pallas_call | solution.py:437
  246.1 3.7 %all-to-all-done.3 = bf16[8,64,2048]{2,1,0:T(8,128)(2,1)} async-done(((bf16[8,64,2048]{2,1,0:T(8,128)(2,1)}), bf16[8,64,2048]{2,1,0:T(8,128)(2,1)}, u32[]{:S(2)}, u32[]{:S(2)}) %all-to-all-start.3) | async-done | bytes 2097184 | tf_op jit(solution)/shard_map/all_to_all | solution.py:50
  249.8 5.5 %all-to-all-start.6 = ((bf16[8,80,256]{2,1,0:T(8,128)(2,1)}), bf16[8,80,256]{2,1,0:T(8,128)(2,1)}, u32[]{:S(2)}, u32[]{:S(2)}) async-start(bf16[8,80,256]{2,1,0:T(8,128)(2,1)} %pad_maximum_fusion.5), calls=%async_computation.6 | async-start | bytes 655360 | tf_op jit(solution)/shard_map/all_to_all | solution.py:50
  255.3 2.9 convert_reduce_fusion
  258.2 3.7 %all-to-all-done.6 = bf16[8,80,256]{2,1,0:T(8,128)(2,1)} async-done(((bf16[8,80,256]{2,1,0:T(8,128)(2,1)}), bf16[8,80,256]{2,1,0:T(8,128)(2,1)}, u32[]{:S(2)}, u32[]{:S(2)}) %all-to-all-start.6) | async-done | bytes 327712 | tf_op jit(solution)/shard_map/all_to_all | solution.py:50
  261.9 3.8 %fusion.17 = (f32[64]{0:T(128)S(1)}, f32[64,1024]{1,0:T(8,128)S(1)}) fusion(bf16[64,1024]{1,0:T(8,128)(2,1)S(1)} %copy-done.8, f32[64]{0:T(128)S(1)} %add_rsqrt_fusion.1, f32[1024]{0:T(1024)S(1)} %copy-done.24, bf16[8,1024,256]{2,1,0:T(8,128)(2,1)} %bitcast.75, bf16[8,80,256]{2,1,0:T(8,128)(2,1)} %all-to-all-done.6), kind=kOutput, calls=%fused_computation.43 | convolution fusion | flops 268763072 | bytes 4854272 | tf_op jit(solution)/shard_map/tsc,tdc->sd/dot_general | solution.py:465
  267.8 3.7 %all-to-all-start.7 = ((bf16[8,64,1024]{2,1,0:T(8,128)(2,1)}), bf16[8,64,1024]{2,1,0:T(8,128)(2,1)S(1)}, u32[]{:S(2)}, u32[]{:S(2)}) async-start(bf16[8,64,1024]{2,1,0:T(8,128)(2,1)} %broadcast_in_dim.19), calls=%async_computation.7 | async-start | bytes 2097152 | tf_op jit(solution)/shard_map/all_to_all | solution.py:50
  272.4 22.3 %all-to-all-done.7 = bf16[8,64,1024]{2,1,0:T(8,128)(2,1)S(1)} async-done(((bf16[8,64,1024]{2,1,0:T(8,128)(2,1)}), bf16[8,64,1024]{2,1,0:T(8,128)(2,1)S(1)}, u32[]{:S(2)}, u32[]{:S(2)}) %all-to-all-start.7) | async-done | bytes 1048608 | tf_op jit(solution)/shard_map/all_to_all | solution.py:50
  296.9 26.2 %all_to_all.46 = bf16[16,80,384]{2,1,0:T(8,128)(2,1)S(1)} all-to-all(bf16[16,80,384]{2,1,0:T(8,128)(2,1)S(1)} %pad_maximum_fusion.2), channel_id=1, replica_groups=mesh['ctx'=16,'tp'=8] {'ctx'}, dimensions={0} | all-to-all | bytes 1966080 | tf_op jit(solution)/shard_map/all_to_all | solution.py:50
  326.4 3.1 reduce-scatter.4.cloned.1.call-done
  (150 shorter events, 59.3 us)
Async XLA Ops:
  7.2 115.7 %copy-start = (bf16[576,1024]{1,0:T(8,128)(2,1)S(1)}, bf16[576,1024]{1,0:T(8,128)(2,1)}, u32[]{:S(2)}) copy-start(bf16[576,1024]{1,0:T(8,128)(2,1)} %param.29) | copy-start | bytes 3538948
  7.2 11.1 %copy-start.26 = (s32[32]{0:T(128)S(1)}, s32[32]{0:T(128)}, u32[]{:S(2)}) copy-start(s32[32]{0:T(128)} %order_ref.7) | copy-start | bytes 388
  7.2 14.3 %copy-start.25 = (s32[8192]{0:T(1024)S(1)}, s32[8192]{0:T(1024)}, u32[]{:S(2)}) copy-start(s32[8192]{0:T(1024)} %param.17) | copy-start | bytes 98308
  7.2 14.3 %copy-start.21 = (bf16[1024,64]{0,1:T(8,128)(2,1)S(1)}, bf16[1024,64]{0,1:T(8,128)(2,1)}, u32[]{:S(2)}) copy-start(bf16[1024,64]{0,1:T(8,128)(2,1)} %param.21) | copy-start | bytes 393220
  7.2 98.9 %all-gather.5.cloned.1.call-start = ((), (), s32[]{:S(2)}) async-start(), calls=%async_computation.10 | async-start | bytes 3538944 | tf_op jit(solution)/shard_map/all_gather | solution.py:315
  9.1 12.5 %copy-start.22 = (bf16[1024,64]{0,1:T(8,128)(2,1)S(1)}, bf16[1024,64]{0,1:T(8,128)(2,1)}, u32[]{:S(2)}) copy-start(bf16[1024,64]{0,1:T(8,128)(2,1)} %param.22) | copy-start | bytes 393220
  9.2 14.0 %copy-start.28 = (f32[64]{0:T(128)S(1)}, f32[64]{0:T(128)}, u32[]{:S(2)}) copy-start(f32[64]{0:T(128)} %param.23) | copy-start | bytes 772
  9.2 14.0 %copy-start.29 = (f32[64]{0:T(128)S(1)}, f32[64]{0:T(128)}, u32[]{:S(2)}) copy-start(f32[64]{0:T(128)} %param.24) | copy-start | bytes 772
  11.3 14.9 %copy-start.20 = (bf16[1024,128]{1,0:T(8,128)(2,1)S(1)}, bf16[1024,128]{1,0:T(8,128)(2,1)}, u32[]{:S(2)}) copy-start(bf16[1024,128]{1,0:T(8,128)(2,1)} %param.20) | copy-start | bytes 786436
  11.3 28.8 %all-to-all-start = ((bf16[8,64,1024]{2,1,0:T(8,128)(2,1)}), bf16[8,64,1024]{2,1,0:T(8,128)(2,1)S(1)}, u32[]{:S(2)}, u32[]{:S(2)}) async-start(bf16[8,64,1024]{2,1,0:T(8,128)(2,1)} %broadcast_in_dim.14), calls=%async_computation | async-start | bytes 2097152 | tf_op jit(solution)/shard_map/all_to_all | solution.py:50
  69.4 3.4 %copy-start.11 = (bf16[8,512,128]{2,1,0:T(8,128)(2,1)}, bf16[8,512,128]{2,1,0:T(8,128)(2,1)S(1)}, u32[]{:S(2)}) copy-start(bf16[8,512,128]{2,1,0:T(8,128)(2,1)S(1)} %all_to_all.45) | copy-start | bytes 3145732
  69.4 11.6 %collective-permute-start = (bf16[4096,128]{1,0:T(8,128)(2,1)S(1)}, bf16[4096,128]{1,0:T(8,128)(2,1)S(1)}, u32[]{:S(2)}, u32[]{:S(2)}) collective-permute-start(bf16[4096,128]{1,0:T(8,128)(2,1)S(1)} %bitcast.84), channel_id=1, source_target_pairs={{0,8},{8,0},{16,24},{24,16},{32,40},{40,32},{48,56},{56,48},{64,72... | collective-permute-start | bytes 3145736 | tf_op jit(solution)/shard_map/ppermute | solution.py:350
  92.3 23.4 %all-to-all-start.2 = ((bf16[8,512,128]{2,1,0:T(8,128)(2,1)}), bf16[8,512,128]{2,1,0:T(8,128)(2,1)}, u32[]{:S(2)}, u32[]{:S(2)}) async-start(bf16[8,512,128]{2,1,0:T(8,128)(2,1)} %broadcast_in_dim.16), calls=%async_computation.2 | async-start | bytes 2097152 | tf_op jit(solution)/shard_map/all_to_all | solution.py:50
  96.5 161.7 %all-gather.7.cloned.1.call-start = ((), (), s32[]{:S(2)}) async-start(), calls=%async_computation.11 | async-start | bytes 4718592 | tf_op jit(solution)/shard_map/all_gather | solution.py:319
  108.4 10.8 %copy-start.23 = (f32[1024]{0:T(1024)S(1)}, f32[1024]{0:T(1024)}, u32[]{:S(2)}) copy-start(f32[1024]{0:T(1024)} %param.26) | copy-start | bytes 12292
  132.5 4.4 %copy-start.14 = (bf16[128,1024]{1,0:T(8,128)(2,1)S(1)}, bf16[128,1024]{1,0:T(8,128)(2,1)}, u32[]{:S(2)}) copy-start(bf16[128,1024]{1,0:T(8,128)(2,1)} %param.25) | copy-start | bytes 786436
  132.5 31.4 %all-to-all-start.4 = ((bf16[8,512,128]{2,1,0:T(8,128)(2,1)}), bf16[8,512,128]{2,1,0:T(8,128)(2,1)}, u32[]{:S(2)}, u32[]{:S(2)}) async-start(bf16[8,512,128]{2,1,0:T(8,128)(2,1)} %fusion.9), calls=%async_computation.4 | async-start | bytes 2097152 | tf_op jit(solution)/shard_map/all_to_all | solution.py:50
  180.3 15.6 %collective-permute-start.1 = (bf16[4096,128]{1,0:T(8,128)(2,1)S(1)}, bf16[4096,128]{1,0:T(8,128)(2,1)S(1)}, u32[]{:S(2)}, u32[]{:S(2)}) collective-permute-start(bf16[4096,128]{1,0:T(8,128)(2,1)S(1)} %convert_element_type.101), channel_id=1, source_target_pairs={{0,8},{8,0},{16,24},{24,16},{32,40},{40,32},{48,56},{56,48},{64,72... | collective-permute-start | bytes 3145736 | tf_op jit(solution)/shard_map/ppermute | solution.py:424
  198.7 5.2 %copy-start.8 = (bf16[64,1024]{1,0:T(8,128)(2,1)S(1)}, bf16[64,1024]{1,0:T(8,128)(2,1)}, u32[]{:S(2)}) copy-start(bf16[64,1024]{1,0:T(8,128)(2,1)} %param.15) | copy-start | bytes 393220
  198.7 22.9 %all-to-all-start.5 = ((bf16[8,512,128]{2,1,0:T(8,128)(2,1)}), bf16[8,512,128]{2,1,0:T(8,128)(2,1)}, u32[]{:S(2)}, u32[]{:S(2)}) async-start(bf16[8,512,128]{2,1,0:T(8,128)(2,1)} %bitcast.83), calls=%async_computation.5 | async-start | bytes 2097152 | tf_op jit(solution)/shard_map/all_to_all | solution.py:50
  221.7 28.1 %all-to-all-start.3 = ((bf16[8,64,2048]{2,1,0:T(8,128)(2,1)}), bf16[8,64,2048]{2,1,0:T(8,128)(2,1)}, u32[]{:S(2)}, u32[]{:S(2)}) async-start(bf16[8,64,2048]{2,1,0:T(8,128)(2,1)} %bitcast.74), calls=%async_computation.3 | async-start | bytes 4194304 | tf_op jit(solution)/shard_map/all_to_all | solution.py:50
  226.0 103.4 %reduce-scatter.4.cloned.1.call-start = ((), (), s32[]{:S(2)}) async-start(), calls=%async_computation.12 | async-start | bytes 3899392
  226.1 2.3 copy-start.3
  237.5 4.5 %copy-start.1 = (bf16[1024,256]{1,0:T(8,128)(2,1)S(1)}, bf16[1024,256]{1,0:T(8,128)(2,1)}, u32[]{:S(2)}) copy-start(bf16[1024,256]{1,0:T(8,128)(2,1)} %pad_maximum_fusion.3.w_ref) | copy-start | bytes 1572868
  237.5 4.5 %copy-start.31 = (bf16[512,1024]{1,0:T(8,128)(2,1)S(1)}, bf16[512,1024]{1,0:T(8,128)(2,1)}, u32[]{:S(2)}) copy-start(bf16[512,1024]{1,0:T(8,128)(2,1)} %get-tuple-element.43) | copy-start | bytes 3145732
  241.4 2.9 copy-start.24
  249.8 12.1 %all-to-all-start.6 = ((bf16[8,80,256]{2,1,0:T(8,128)(2,1)}), bf16[8,80,256]{2,1,0:T(8,128)(2,1)}, u32[]{:S(2)}, u32[]{:S(2)}) async-start(bf16[8,80,256]{2,1,0:T(8,128)(2,1)} %pad_maximum_fusion.5), calls=%async_computation.6 | async-start | bytes 655360 | tf_op jit(solution)/shard_map/all_to_all | solution.py:50
  261.9 3.9 %copy-start.7 = (f32[64,2048]{1,0:T(8,128)S(1)}, f32[64,2048]{1,0:T(8,128)}, u32[]{:S(2)}) copy-start(f32[64,2048]{1,0:T(8,128)} %convert_reduce_fusion) | copy-start | bytes 1572868
  261.9 3.9 %copy-start.18 = (bf16[64,1024]{1,0:T(8,128)(2,1)S(1)}, bf16[64,1024]{1,0:T(8,128)(2,1)}, u32[]{:S(2)}) copy-start(bf16[64,1024]{1,0:T(8,128)(2,1)} %param.16) | copy-start | bytes 393220
  266.7 5.7 %copy-start.27 = (pred[16]{0:T(512)(128)(4,1)S(1)}, pred[16]{0:T(512)(128)(4,1)}, u32[]{:S(2)}) copy-start(pred[16]{0:T(512)(128)(4,1)} %constant.56.clone.1) | copy-start | bytes 52
  267.8 27.5 %copy-start.17 = (bf16[512,128]{1,0:T(8,128)(2,1)S(1)}, bf16[512,128]{1,0:T(8,128)(2,1)}, u32[]{:S(2)}) copy-start(bf16[512,128]{1,0:T(8,128)(2,1)} %get-tuple-element.31) | copy-start | bytes 393220
  267.8 26.9 %all-to-all-start.7 = ((bf16[8,64,1024]{2,1,0:T(8,128)(2,1)}), bf16[8,64,1024]{2,1,0:T(8,128)(2,1)S(1)}, u32[]{:S(2)}, u32[]{:S(2)}) async-start(bf16[8,64,1024]{2,1,0:T(8,128)(2,1)} %broadcast_in_dim.19), calls=%async_computation.7 | async-start | bytes 2097152 | tf_op jit(solution)/shard_map/all_to_all | solution.py:50
  (15 other events, 21.9 us)
Sparse Core Ops, SparseCore 0:
  9.7 96.3 all-gather.4
  107.8 119.4 all-gather.6
  237.6 91.8 reduce-scatter.3

commit v2 on v1

v2 whole, which is shorter than its diff:
```python
from functools import partial
import math

import jax
import jax.numpy as jnp
from jax import lax
from jax.experimental import pallas as pl
from jax.experimental.pallas import tpu as pltpu
from jax.sharding import PartitionSpec as P

eps = 1e-05
theta = 1000000.0
bf16 = jnp.bfloat16
f32 = jnp.float32
vmem_bytes = 56 * 1024 * 1024
log2e = math.log2(math.e)
HEAD = 64
LANES = 128


def dot(a, b):
    return jnp.dot(a, b, preferred_element_type=f32)


def dot_t(a, b):
    return lax.dot_general(a, b, (((1,), (1,)), ((), ())), preferred_element_type=f32)


def t_dot(a, b):
    return lax.dot_general(a, b, (((0,), (0,)), ((), ())), preferred_element_type=f32)


def call(kernel, out_shape, **more):
    return pl.pallas_call(
        kernel,
        out_shape=out_shape,
        compiler_params=pltpu.CompilerParams(vmem_limit_bytes=vmem_bytes),
        **more,
    )


def in_vmem(count):
    return [pl.BlockSpec(memory_space=pltpu.VMEM)] * count


in_smem = pl.BlockSpec(memory_space=pltpu.SMEM)


def exchange(x, axis, groups=None):
    return lax.all_to_all(x, axis, 0, 0, axis_index_groups=groups, tiled=True)


def spread(x, axis, count, groups=None):
    return exchange(jnp.broadcast_to(x[None], (count, *x.shape)), axis, groups)


def left_half(shape):
    return lax.broadcasted_iota(jnp.int32, shape, 1) < HEAD


def swap_quarters(v):
    lane = lax.broadcasted_iota(jnp.int32, v.shape, 1)
    return jnp.where(lane % HEAD < HEAD // 2, pltpu.roll(v, LANES - 32, 1), pltpu.roll(v, 32, 1))


def head_mean(v, left):
    first = jnp.sum(jnp.where(left, v, 0.0), axis=1, keepdims=True)
    second = jnp.sum(jnp.where(left, 0.0, v), axis=1, keepdims=True)
    return jnp.where(left, first, second) * (1.0 / HEAD)


def project_kernel(
    x_ref, gain_ref, w_ref, head_gain_ref, cos_ref, sin_ref, normed_ref, pre_ref, query_ref, kv_ref
):
    x = x_ref[...].astype(f32)
    scaled = x * lax.rsqrt(jnp.mean(x * x, axis=1, keepdims=True) + eps)
    normed = (scaled * gain_ref[...]).astype(bf16)
    normed_ref[...] = normed
    pre = dot(normed, w_ref[...])
    pre_ref[...] = pre
    cosine, sine = cos_ref[...], sin_ref[...]
    left = left_half((x.shape[0], LANES))

    def prepared(v, gain):
        v = v * lax.rsqrt(head_mean(v * v, left) + eps) * gain
        return v * cosine + swap_quarters(v) * sine

    query = prepared(pre[:, :LANES], head_gain_ref[0:1, :])
    query_ref[...] = (query * (log2e / math.sqrt(HEAD))).astype(bf16)
    pair = pre[:, LANES:]
    key = prepared(pair, head_gain_ref[1:2, :])
    both = jnp.where(left, key, pair).astype(bf16)
    for peer in range(kv_ref.shape[0]):
        kv_ref[peer] = both


def earlier_spans(order_ref, list_ref, rank, core, blocks):
    def look(block, count):
        list_ref[count] = block
        slot = ((block // 2) * 2 + core) * 2 + block % 2
        return count + (order_ref[slot] < rank).astype(jnp.int32)

    return lax.fori_loop(0, blocks, look, jnp.int32(0))


def block_rows(index, span):
    return pl.ds(pl.multiple_of(index * span, span), span)


def in_groups(count, size, body):
    whole = count // size

    def some(step, carry):
        body([step * size + k for k in range(size)])
        return carry

    lax.fori_loop(0, whole, some, 0)

    def one(step, carry):
        body([step])
        return carry

    lax.fori_loop(whole * size, count, one, 0)


def pieces(v, count):
    parts = []
    for _ in range(count):
        part = v.astype(bf16).astype(f32)
        parts.append(part)
        v = v - part
    return parts


def attend_kernel(order_ref, own_ref, other_ref, kv_ref, acc_ref, sent_ref, list_ref, qx_ref, part_ref):
    me = lax.axis_index("ctx")
    core = me % 2
    span = own_ref.shape[0] // 2
    blocks = kv_ref.shape[0] // span
    left = left_half((span, LANES))
    lane = lax.broadcasted_iota(jnp.int32, (span, LANES), 1)
    one = jnp.ones((span, LANES), bf16)
    for source in range(2):
        for slot in range(2):
            query = (own_ref, other_ref)[source][pl.ds(slot * span, span), :].astype(f32)
            for head in range(2):
                own = query if head == 0 else pltpu.roll(query, HEAD, 1)
                qx_ref[pl.ds(head * span, span), :] = jnp.where(left, own, 0.0).astype(bf16)
            rank = order_ref[(me + source * (1 - 2 * core)) * 2 + slot]
            count = earlier_spans(order_ref, list_ref, rank, core, blocks)
            rows = pl.ds(slot * 2 * span, 2 * span)

            def product(index, mask=None):
                pair = kv_ref[block_rows(index, span), :]
                weights = jnp.exp2(dot_t(qx_ref[...], pair))
                if mask is not None:
                    weights = jnp.where(mask, weights, 0.0)
                return dot(weights.astype(bf16), jnp.where(left, one, pair))

            target = acc_ref if source == 0 else part_ref
            if source == 0:
                row = lax.broadcasted_iota(jnp.int32, (2 * span, span), 0) % span
                col = lax.broadcasted_iota(jnp.int32, (2 * span, span), 1)
                target[rows, :] = product((me // 2) * 2 + slot, row >= col)
            else:
                target[rows, :] = jnp.zeros((2 * span, LANES), f32)

            def add(steps):
                target[rows, :] += sum(product(list_ref[step]) for step in steps)

            in_groups(count, 4, add)
            if source == 1:
                for head in range(2):
                    part = pl.ds((slot * 2 + head) * span, span)
                    acc = target[part, :]
                    high, middle, low = pieces(acc, 3)
                    packed = jnp.where(lane == 0, high, jnp.where(lane == 1, middle, low))
                    packed = jnp.where(lane < 3, packed, jnp.where(left, 0.0, acc))
                    sent_ref[part, :] = packed.astype(bf16)


def finish_kernel(acc_ref, recv_ref, query_ref, out_ref, attended_ref, qb_ref):
    span = query_ref.shape[0] // 2
    left = left_half((span, LANES))
    lane = lax.broadcasted_iota(jnp.int32, (span, LANES), 1)
    for slot in range(2):
        rows = pl.ds(slot * span, span)
        query = query_ref[rows, :].astype(f32)
        outs = []
        for head in range(2):
            part = pl.ds((slot * 2 + head) * span, span)
            recv = recv_ref[part, :].astype(f32)
            acc = acc_ref[part, :]
            total = jnp.sum(jnp.where(left, recv, 0.0), axis=1, keepdims=True)
            total = total + jnp.where(left, acc, pltpu.roll(acc, HEAD, 1))
            logs = jnp.log2(total)
            out = jnp.where(left, logs, (acc + recv) / total)
            out_ref[part, :] = out
            outs.append(out)
            high, middle, low = pieces(logs, 3)
            own = jnp.where(left, query if head == 0 else pltpu.roll(query, HEAD, 1), 0.0)
            own = jnp.where(lane == HEAD, -high, own)
            own = jnp.where(lane == HEAD + 1, -middle, own)
            own = jnp.where(lane == HEAD + 2, -low, own)
            qb_ref[part, :] = own.astype(bf16)
        both = jnp.where(left, pltpu.roll(outs[0], HEAD, 1), outs[1]).astype(bf16)
        for peer in range(attended_ref.shape[0]):
            attended_ref[peer, rows, :] = both


def prepare_kernel(base_ref, recv_ref, out_ref, dx_ref):
    span = base_ref.shape[0] // 2
    left = left_half((span, LANES))
    lane = lax.broadcasted_iota(jnp.int32, (span, LANES), 1)
    for slot in range(2):
        rows = pl.ds(slot * span, span)
        mixed = base_ref[rows, :]
        for peer in range(recv_ref.shape[0]):
            mixed = mixed + recv_ref[peer, rows, :].astype(f32)
        mixed = mixed.astype(bf16).astype(f32)
        for head in range(2):
            part = pl.ds((slot * 2 + head) * span, span)
            own = jnp.where(left, 0.0, pltpu.roll(mixed, HEAD, 1) if head == 0 else mixed)
            delta = jnp.sum(own * out_ref[part, :], axis=1, keepdims=True)
            high, low = pieces(delta, 2)
            own = jnp.where(lane == 0, -high, jnp.where(lane == 1, -low, own))
            dx_ref[part, :] = own.astype(bf16)


def pull_kernel(last, order_ref, kv_ref, qb_ref, dx_ref, *refs):
    if last:
        start_ref, out_ref, dq_out_ref, list_ref, qz_ref, dz_ref, dkv_ref, dq_ref = refs
        dkv_ref[...] = start_ref[...]
    else:
        dkv_ref, dq_out_ref, list_ref, qz_ref, dz_ref, dq_ref = refs
        dkv_ref[...] = jnp.zeros_like(dkv_ref)
    me = lax.axis_index("ctx")
    core = me % 2
    whose = me + 1 - 2 * core if last else me
    span = qb_ref.shape[0] // 4
    blocks = kv_ref.shape[0] // span
    left = left_half((span, LANES))
    one = jnp.ones((span, LANES), bf16)
    zero = jnp.zeros((2 * span, LANES), bf16)
    wide_left = left_half((2 * span, LANES))
    for slot in range(2):
        rows = pl.ds(slot * 2 * span, 2 * span)
        qz_ref[...] = jnp.where(wide_left, qb_ref[rows, :], zero)
        dz_ref[...] = jnp.where(wide_left, zero, dx_ref[rows, :])
        count = earlier_spans(order_ref, list_ref, order_ref[whose * 2 + slot], core, blocks)

        def product(index, mask=None):
            part = block_rows(index, span)
            pair = kv_ref[part, :]
            weights = jnp.exp2(dot_t(jnp.where(left, pair, one), qb_ref[rows, :]))
            if mask is not None:
                weights = jnp.where(mask, weights, 0.0)
            pulled = dot_t(jnp.where(left, one, pair), dx_ref[rows, :])
            score = (weights * pulled).astype(bf16)
            dkv_ref[part, :] += dot(score, qz_ref[...]) + dot(weights.astype(bf16), dz_ref[...])
            return t_dot(score, pair)

        if last:
            dq_ref[...] = jnp.zeros_like(dq_ref)
        else:
            row = lax.broadcasted_iota(jnp.int32, (span, 2 * span), 0)
            col = lax.broadcasted_iota(jnp.int32, (span, 2 * span), 1) % span
            dq_ref[...] = product((me // 2) * 2 + slot, col >= row)

        def add(steps):
            dq_ref[...] += sum(product(list_ref[step]) for step in steps)

        in_groups(count, 2, add)
        both = jnp.where(left, dq_ref[:span, :], pltpu.roll(dq_ref[span:, :], HEAD, 1))
        dq_out_ref[pl.ds(slot * span, span), :] = both.astype(dq_out_ref.dtype)
    if last:
        factor = jnp.where(left_half((1, LANES)), 1.0 / log2e, 1.0)
        out_ref[...] = (dkv_ref[...] * factor).astype(bf16)


def rows_kernel(recv_ref, cotangent_ref, resid_ref, grad_ref, block_ref):
    width = resid_ref.shape[1]
    total = recv_ref[0].astype(f32)
    for peer in range(1, recv_ref.shape[0]):
        total = total + recv_ref[peer].astype(f32)
    grad_ref[...] = cotangent_ref[...].astype(f32) + total[:, :width]
    block_ref[...] = (resid_ref[...] + total[:, width:]).astype(bf16)


def as_rows(v):
    return jnp.concatenate([v[:, k : k + LANES] for k in range(0, v.shape[1], LANES)], axis=0)


def back_kernel(
    dq_ref, dq_recv_ref, recv_ref, pre_ref, head_gain_ref, cos_ref, sin_ref, w_ref, normed_ref,
    gain_ref, second_ref, grad_ref, pre_grad_ref, sent_ref,
):
    span = cos_ref.shape[0] // 2
    peers, _, width = sent_ref.shape
    part = 2 * span // peers
    left = left_half((span, LANES))

    def pulled(grad, pre, gain, cosine, sine):
        turned = grad * cosine - swap_quarters(grad) * sine
        factor = lax.rsqrt(head_mean(pre * pre, left) + eps)
        unit = pre * factor
        sums = jnp.sum(turned * unit, axis=0, keepdims=True)
        scaled = turned * gain
        return (scaled - unit * head_mean(scaled * unit, left)) * factor, sums

    totals = [0.0, 0.0, 0.0]
    for slot in range(2):
        rows = pl.ds(slot * span, span)
        cosine, sine = cos_ref[rows, :], sin_ref[rows, :]
        grad = (dq_ref[rows, :] + dq_recv_ref[rows, :].astype(f32)) * (1.0 / math.sqrt(HEAD))
        pair = recv_ref[0, rows, :].astype(f32)
        for peer in range(1, recv_ref.shape[0]):
            pair = pair + recv_ref[peer, rows, :].astype(f32)
        query, sums = pulled(grad, pre_ref[rows, :LANES], head_gain_ref[0:1, :], cosine, sine)
        totals[0] = totals[0] + sums
        key, sums = pulled(
            jnp.where(left, pair, 0.0), pre_ref[rows, LANES:], head_gain_ref[1:2, :], cosine, sine
        )
        totals[1] = totals[1] + sums
        pre_grad_ref[rows, :LANES] = query.astype(bf16)
        pre_grad_ref[rows, LANES:] = jnp.where(left, key, pair).astype(bf16)
        normed_part = dot_t(pre_grad_ref[rows, :], w_ref[...])
        totals[2] = totals[2] + jnp.sum(
            normed_part * normed_ref[rows, :].astype(f32), axis=0, keepdims=True
        )
        sent = normed_part.astype(bf16).reshape(peers // 2, part, width)
        sent_ref[slot * (peers // 2) : (slot + 1) * (peers // 2), :part, :] = sent
    folded = totals[0] + pltpu.roll(totals[0], HEAD, 1)
    heads = jnp.where(left_half((1, LANES)), folded, pltpu.roll(totals[1], HEAD, 1))
    sums = jnp.concatenate(
        [as_rows(totals[2] / gain_ref[...]), as_rows(second_ref[...]), jnp.broadcast_to(heads, (8, LANES))],
        axis=1,
    )
    sums = jnp.concatenate([sums, jnp.zeros_like(sums)], axis=0).astype(bf16)
    for peer in range(peers):
        sent_ref[peer, part : 2 * part, :] = grad_ref[...].astype(bf16)
        sent_ref[peer, 2 * part :, : 3 * LANES] = sums
        sent_ref[peer, 2 * part :, 3 * LANES :] = jnp.zeros((16, width - 3 * LANES), bf16)


def tokens_kernel(
    recv_ref, tokens_ref, gain_ref, resid_grad_ref, attended_ref, grad_ref, own_ref, other_ref,
    flat_ref,
):
    part = tokens_ref.shape[0]
    rows = own_ref.shape[0] - 16
    total = recv_ref[0, :part].astype(f32)
    sums = recv_ref[0, 2 * part :, : 3 * LANES].astype(f32)
    for peer in range(1, recv_ref.shape[0]):
        total = total + recv_ref[peer, :part].astype(f32)
        sums = sums + recv_ref[peer, 2 * part :, : 3 * LANES].astype(f32)
    for peer in range(recv_ref.shape[0]):
        flat_ref[peer * part : (peer + 1) * part, :] = recv_ref[peer, part : 2 * part]
    by_core(
        own_ref, other_ref, slice(0, rows), slice(0, LANES), t_dot(flat_ref[...], attended_ref[...])
    )
    for target in (own_ref, other_ref):
        target[:rows, LANES:] = jnp.zeros((rows, 2 * LANES), bf16)
        target[rows:, :] = sums.astype(bf16)
    x = tokens_ref[...].astype(f32)
    factor = lax.rsqrt(jnp.mean(x * x, axis=1, keepdims=True) + eps)
    unit = x * factor
    scaled = total * gain_ref[...]
    pulled = (scaled - unit * jnp.mean(scaled * unit, axis=1, keepdims=True)) * factor
    grad_ref[...] = (resid_grad_ref[...] + pulled).astype(bf16)


def by_core(own_ref, other_ref, rows, columns, value):
    core = lax.axis_index("ctx") % 2
    split = value.reshape(value.shape[0] // LANES, 2, LANES // 2, value.shape[1])
    even = split[:, 0].reshape(-1, value.shape[1])
    odd = split[:, 1].reshape(-1, value.shape[1])
    own_ref[rows, columns] = jnp.where(core == 0, even, odd).astype(bf16)
    other_ref[rows, columns] = jnp.where(core == 0, odd, even).astype(bf16)


def weights_kernel(normed_ref, pair_ref, dy_ref, hidden_ref, feed_ref):
    step = 512
    wide = pair_ref.shape[1]
    for start in range(0, normed_ref.shape[1], step):
        columns = slice(start, start + step)
        feed_ref[columns, :wide] = t_dot(normed_ref[:, columns], pair_ref[...]).astype(bf16)
        feed_ref[columns, wide:] = t_dot(dy_ref[:, columns], hidden_ref[...]).astype(bf16)


def grads_kernel(normed_ref, pre_grad_ref, own_ref, other_ref):
    rows = slice(0, own_ref.shape[0])
    wide = pre_grad_ref.shape[1]
    by_core(own_ref, other_ref, rows, slice(0, wide), t_dot(normed_ref[...], pre_grad_ref[...]))


def merge_kernel(own_ref, moved_ref, last_ref, last_moved_ref, sent_ref):
    peers = sent_ref.shape[0]
    rows = own_ref.shape[0]
    part = rows // peers

    def both(first, second):
        return (first.astype(f32) + second.astype(f32)).astype(bf16)

    grads = both(own_ref[...], moved_ref[...])
    sent_ref[:, :part, : 2 * LANES] = grads.reshape(peers, part, 2 * LANES)
    last = both(last_ref[:rows, :LANES], last_moved_ref[:rows, :LANES])
    sent_ref[:, :part, 2 * LANES :] = last.reshape(peers, part, LANES)
    sums = both(last_ref[rows:, :], last_moved_ref[rows:, :])
    for peer in range(peers):
        sent_ref[peer, part:, :] = sums


def total_kernel(recv_ref, query_ref, key_ref, value_ref, out_ref, first_ref, second_ref, heads_ref):
    part = query_ref.shape[0]
    total = recv_ref[0].astype(f32)
    for peer in range(1, recv_ref.shape[0]):
        total = total + recv_ref[peer].astype(f32)
    query_ref[...] = total[:part, :LANES]
    key_ref[...] = total[:part, LANES : LANES + HEAD]
    value_ref[...] = total[:part, LANES + HEAD : 2 * LANES]
    out_ref[...] = total[:part, 2 * LANES :]
    first_ref[...] = total[part : part + 8, :LANES]
    second_ref[...] = total[part : part + 8, LANES : 2 * LANES]
    heads_ref[...] = total[part : part + 8, 2 * LANES :]


def parts_kernel(feed_ref, gate_ref, up_ref, down_ref):
    wide = gate_ref.shape[1]
    gate_ref[...] = feed_ref[:, :wide].astype(f32)
    up_ref[...] = feed_ref[:, wide : 2 * wide].astype(f32)
    down_ref[...] = feed_ref[:, 2 * wide :].astype(f32)


def feed_kernel(
    x_ref, attended_ref, w_own_ref, w_other_ref, gain_ref, w_pair_ref, hidden_grad_ref,
    resid_ref, normed_ref, hidden_ref, pair_grad_ref, part_ref, mixed_ref, sums_ref,
    w_ref, flat_ref, all_ref,
):
    core = lax.axis_index("ctx") % 2
    mine = lax.axis_index("tp")
    width = x_ref.shape[1]
    half = width // 2
    peers, local, heads = attended_ref.shape
    w_ref[core] = w_own_ref[...]
    w_ref[1 - core] = w_other_ref[...]
    rows = 256
    wide = hidden_ref.shape[1]
    gain = gain_ref[...]
    total = jnp.zeros((1, width), f32)
    for start in range(0, local, rows):
        here = pl.ds(start, rows)
        for peer in range(peers):
            flat_ref[:, peer * heads : (peer + 1) * heads] = attended_ref[peer, here, :]
        flat = flat_ref[...]
        for side in range(2):
            columns = pl.ds(side * half, half)
            all_ref[here, columns] = x_ref[here, columns].astype(f32) + dot(flat, w_ref[side])
        resid = all_ref[here, :]
        factor = lax.rsqrt(jnp.mean(resid * resid, axis=1, keepdims=True) + eps)
        normed = (resid * factor * gain).astype(bf16)
        normed_ref[here, :] = normed
        pair = dot(normed, w_pair_ref[...])
        gate, up = pair[:, :wide], pair[:, wide:]
        hidden_grad = hidden_grad_ref[here, :]
        sigma = 1.0 / (1.0 + jnp.exp(-gate))
        swish = gate * sigma
        hidden_ref[here, :] = (swish * up).astype(bf16)
        gate_grad = (hidden_grad * up * sigma * (1.0 + gate * (1.0 - sigma))).astype(bf16)
        pair_grad_ref[here, :wide] = gate_grad
        pair_grad_ref[here, wide:] = (hidden_grad * swish).astype(bf16)
        pulled = dot_t(pair_grad_ref[here, :], w_pair_ref[...])
        unit = all_ref[here, :] * factor
        total = total + jnp.sum(pulled * unit, axis=0, keepdims=True)
        scaled = pulled * gain
        part = (scaled - unit * jnp.mean(scaled * unit, axis=1, keepdims=True)) * factor
        part = part.astype(bf16)
        part_ref[here, :] = part
        mixed = dot_t(part[:, :half], w_ref[0]) + dot_t(part[:, half:], w_ref[1])
        mixed = mixed.astype(bf16)
        for peer in range(peers):
            mixed_ref[peer, here, :] = mixed[:, peer * heads : (peer + 1) * heads]
    sums_ref[...] = total
    resid_ref[...] = all_ref[block_rows(mine, local // peers), :]


def turning(positions, span_order, me, span):
    table = positions.reshape(-1, span)
    own = [lax.dynamic_index_in_dim(table, span_order[me * 2 + k], 0, False) for k in range(2)]
    places = jnp.concatenate(own).astype(f32)
    freqs = theta ** (-(jnp.arange(HEAD // 2, dtype=f32) * 2.0 / HEAD))
    turned = places[:, None] * freqs[None, :]
    cosine, sine = jnp.cos(turned), jnp.sin(turned)
    return (
        jnp.concatenate([cosine] * 4, axis=1),
        jnp.concatenate([-sine, sine, -sine, sine], axis=1),
    )


def per_device(
    tokens, cotangent, positions, span_order, first_gain, w_query, w_key, w_value,
    query_gain, key_gain, w_out, second_gain, w_gate, w_up, w_down,
):
    ctx_count = lax.axis_size("ctx")
    tp_count = lax.axis_size("tp")
    me = lax.axis_index("ctx")
    mine = lax.axis_index("tp")
    part, width = tokens.shape
    local = part * tp_count
    span = local // 2
    half = ctx_count // 2
    heads = w_out.shape[0]
    hidden_width = w_gate.shape[1]
    same_core = [[2 * k + core for k in range(half)] for core in range(2)]
    other_core = [(k, k ^ 1) for k in range(ctx_count)]
    shape = jax.ShapeDtypeStruct
    slots = pltpu.SMEM((ctx_count + 1,), jnp.int32)

    x_all = spread(tokens, "tp", tp_count).reshape(local, width)
    w_half = lax.dynamic_slice_in_dim(w_out, (me % 2) * (width // 2), width // 2, 1)
    w_half = jnp.broadcast_to(w_half[None], (tp_count, heads, width // 2))
    w_qkv = jnp.concatenate([w_query, w_key, w_value], axis=1)
    cosine, sine = turning(positions, span_order, me, span)
    head_gain = jnp.stack(
        [jnp.concatenate([query_gain, query_gain]), jnp.concatenate([key_gain, jnp.ones_like(key_gain)])]
    )

    x_all, cotangent, w_qkv, cosine, sine, head_gain = lax.optimization_barrier(
        (x_all, cotangent, w_qkv, cosine, sine, head_gain)
    )
    dy_all = lax.all_gather(cotangent, "tp", axis=0, tiled=True)

    by_span = lambda rows, cols: pl.BlockSpec((rows, cols), lambda k: (k, 0))
    whole = lambda a: pl.BlockSpec(a.shape, lambda k: (0, 0))
    gain_row = first_gain.reshape(1, width)
    normed, pre, query, kv = call(
        project_kernel,
        (
            shape((local, width), bf16),
            shape((local, 2 * LANES), f32),
            shape((local, LANES), bf16),
            shape((half, local, LANES), bf16),
        ),
        grid=(2,),
        in_specs=[
            by_span(span, width), whole(gain_row), whole(w_qkv), whole(head_gain),
            by_span(span, LANES), by_span(span, LANES),
        ],
        out_specs=(
            by_span(span, width), by_span(span, 2 * LANES), by_span(span, LANES),
            pl.BlockSpec((half, span, LANES), lambda k: (0, k, 0)),
        ),
        name="project",
    )(x_all, gain_row, w_qkv, head_gain, cosine, sine)

    query_other = lax.ppermute(query, "ctx", other_core)
    kv_all = exchange(kv, "ctx", same_core).reshape(half * local, LANES)
    w_pair = jnp.concatenate([w_gate, w_up], axis=1)
    kv_all, w_pair, w_half = lax.optimization_barrier((kv_all, w_pair, w_half))
    w_out_own = exchange(w_half, "tp").reshape(width, width // 2)
    acc, sent = call(
        attend_kernel,
        (shape((2 * local, LANES), f32), shape((2 * local, LANES), bf16)),
        in_specs=[in_smem, *in_vmem(3)],
        out_specs=tuple(in_vmem(2)),
        scratch_shapes=[
            slots, pltpu.VMEM((2 * span, LANES), bf16), pltpu.VMEM((2 * local, LANES), f32)
        ],
        cost_estimate=pl.CostEstimate(flops=8 * 10**9, bytes_accessed=2**21, transcendentals=2**23),
        name="attend",
    )(span_order, query, query_other, kv_all)
    out, attended_wide, qb = call(
        finish_kernel,
        (
            shape((2 * local, LANES), f32),
            shape((tp_count, local, LANES), bf16),
            shape((2 * local, LANES), bf16),
        ),
        in_specs=in_vmem(3),
        out_specs=tuple(in_vmem(3)),
        name="finish",
    )(acc, lax.ppermute(sent, "ctx", other_core), query)
    qb_other = lax.ppermute(qb, "ctx", other_core)
    attended_wide, w_out_own = lax.optimization_barrier((attended_wide, w_out_own))
    w_out_other = lax.ppermute(w_out_own, "ctx", other_core)

    attended_all = exchange(attended_wide, "tp")
    hidden_grad = dot_t(dy_all, w_down)
    mixed_base = dot_t(dy_all, w_out)
    resid, normed_two, hidden, pair_grad, resid_part, mixed_part, second_sum = call(
        feed_kernel,
        (
            shape((part, width), f32),
            shape((local, width), bf16),
            shape((local, hidden_width), bf16),
            shape((local, 2 * hidden_width), bf16),
            shape((local, width), bf16),
            shape((tp_count, local, heads), bf16),
            shape((1, width), f32),
        ),
        in_specs=in_vmem(7),
        out_specs=tuple(in_vmem(7)),
        scratch_shapes=[
            pltpu.VMEM((2, tp_count * heads, width // 2), bf16),
            pltpu.VMEM((256, tp_count * heads), bf16),
            pltpu.VMEM((local, width), f32),
        ],
        cost_estimate=pl.CostEstimate(flops=5 * 10**9, bytes_accessed=2**23, transcendentals=2**18),
        name="feed",
    )(
        x_all, attended_all, w_out_own, w_out_other, second_gain.reshape(1, width), w_pair,
        hidden_grad,
    )
    mixed_recv = exchange(mixed_part, "tp")

    feed = call(
        weights_kernel,
        shape((width, 3 * hidden_width), bf16),
        in_specs=in_vmem(4),
        out_specs=pl.BlockSpec(memory_space=pltpu.VMEM),
        name="weights",
    )(normed_two, pair_grad, dy_all, hidden)
    feed = lax.psum_scatter(feed, "ctx", scatter_dimension=0, tiled=True)
    down = dot(hidden, w_down).astype(bf16)
    rows_sent = jnp.concatenate([resid_part, down], axis=1).reshape(tp_count, part, 2 * width)
    rows_recv = exchange(rows_sent, "tp")

    dx = call(
        prepare_kernel,
        shape((2 * local, LANES), bf16),
        in_specs=in_vmem(3),
        out_specs=pl.BlockSpec(memory_space=pltpu.VMEM),
        name="prepare",
    )(mixed_base, mixed_recv, out)
    dx_other = lax.ppermute(dx, "ctx", other_core)
    keys_shape = (half * local, LANES)
    halves = [pltpu.VMEM((2 * span, LANES), bf16)] * 2
    pull_cost = pl.CostEstimate(flops=20 * 10**9, bytes_accessed=2**22, transcendentals=2**22)
    dkv_start, dq = call(
        partial(pull_kernel, False),
        (shape(keys_shape, f32), shape((local, LANES), f32)),
        in_specs=[in_smem, *in_vmem(3)],
        out_specs=tuple(in_vmem(2)),
        scratch_shapes=[slots, *halves, pltpu.VMEM((2 * span, LANES), f32)],
        cost_estimate=pull_cost,
        name="pull_own",
    )(span_order, kv_all, qb, dx)
    dkv, dq_other = call(
        partial(pull_kernel, True),
        (shape(keys_shape, bf16), shape((local, LANES), bf16)),
        in_specs=[in_smem, *in_vmem(4)],
        out_specs=tuple(in_vmem(2)),
        scratch_shapes=[
            slots, *halves, pltpu.VMEM(keys_shape, f32), pltpu.VMEM((2 * span, LANES), f32)
        ],
        cost_estimate=pull_cost,
        name="pull_other",
    )(span_order, kv_all, qb_other, dx_other, dkv_start)
    dkv, rows_recv = lax.optimization_barrier((dkv, rows_recv))
    resid_grad, block_out = call(
        rows_kernel,
        (shape((part, width), f32), shape((part, width), bf16)),
        in_specs=in_vmem(3),
        out_specs=tuple(in_vmem(2)),
        name="rows",
    )(rows_recv, cotangent, resid)
    dq_recv = lax.ppermute(dq_other, "ctx", other_core)
    dkv_recv = exchange(dkv.reshape(half, local, LANES), "ctx", same_core)

    pre_grad, sent = call(
        back_kernel,
        (shape((local, 2 * LANES), bf16), shape((tp_count, 2 * part + 16, width), bf16)),
        in_specs=in_vmem(12),
        out_specs=tuple(in_vmem(2)),
        name="back",
    )(dq, dq_recv, dkv_recv, pre, head_gain, cosine, sine, w_qkv, normed, gain_row, second_sum, resid_grad)
    recv = exchange(sent, "tp")
    grads_shape = shape((width // 2, 2 * LANES), bf16)
    grads, grads_sent = call(
        grads_kernel,
        (grads_shape, grads_shape),
        in_specs=in_vmem(2),
        out_specs=tuple(in_vmem(2)),
        name="grads",
    )(normed, pre_grad)
    grads_moved = lax.ppermute(grads_sent, "ctx", other_core)
    attended = attended_wide[0]
    recv, grads, grads_moved, attended = lax.optimization_barrier(
        (recv, grads, grads_moved, attended)
    )
    last_shape = shape((width // 2 + 16, 3 * LANES), bf16)
    grad_tokens, last, last_sent = call(
        tokens_kernel,
        (shape((part, width), bf16), last_shape, last_shape),
        in_specs=in_vmem(5),
        out_specs=tuple(in_vmem(3)),
        scratch_shapes=[pltpu.VMEM((local, width), bf16)],
        name="tokens",
    )(recv, tokens, gain_row, resid_grad, attended)
    sent = call(
        merge_kernel,
        shape((half, width // ctx_count + 16, 3 * LANES), bf16),
        in_specs=in_vmem(4),
        out_specs=pl.BlockSpec(memory_space=pltpu.VMEM),
        name="merge",
    )(grads, grads_moved, last, lax.ppermute(last_sent, "ctx", other_core))
    own_rows = width // ctx_count
    grad_query, grad_key, grad_value, grad_out, first_sum, second_sum, head_sums = call(
        total_kernel,
        (
            shape((own_rows, LANES), f32),
            shape((own_rows, HEAD), f32),
            shape((own_rows, HEAD), f32),
            shape((own_rows, LANES), f32),
            shape((8, LANES), f32),
            shape((8, LANES), f32),
            shape((8, LANES), f32),
        ),
        in_specs=in_vmem(1),
        out_specs=tuple(in_vmem(7)),
        name="total",
    )(exchange(sent, "ctx", same_core))
    own_shape = shape((own_rows, hidden_width), f32)
    grad_gate, grad_up, grad_down = call(
        parts_kernel,
        (own_shape, own_shape, own_shape),
        in_specs=in_vmem(1),
        out_specs=tuple(in_vmem(3)),
        name="parts",
    )(feed)
    return (
        block_out,
        grad_tokens,
        first_sum.reshape(width),
        grad_query,
        grad_key,
        grad_value,
        head_sums[0, :HEAD],
        head_sums[0, HEAD:],
        grad_out.T,
        second_sum.reshape(width),
        grad_gate,
        grad_up,
        grad_down.T,
    )


def solution(mesh):
    return jax.shard_map(
        per_device,
        mesh=mesh,
        in_specs=(
            P(("ctx", "tp"), None),
            P(("ctx", "tp"), None),
            P(),
            P(),
            P(),
            P(None, "tp"),
            P(None, "tp"),
            P(None, "tp"),
            P(),
            P(),
            P("tp", None),
            P(),
            P(None, "tp"),
            P(None, "tp"),
            P("tp", None),
        ),
        out_specs=(
            P(("ctx", "tp"), None),
            P(("ctx", "tp"), None),
            P(),
            P("ctx", "tp"),
            P("ctx", "tp"),
            P("ctx", "tp"),
            P(),
            P(),
            P("tp", "ctx"),
            P(),
            P("ctx", "tp"),
            P("ctx", "tp"),
            P("tp", "ctx"),
        ),
        check_vma=False,
    )
```

time: 343 us -> 278 us (0.81)
  blocking collectives: 49.9 us -> 0 us
  starting transfers between devices: 39.3 us -> 63.5 us
  Pallas kernels: 53 us -> 75.4 us
  matrix products: 27.8 us -> 5.46 us
  other arithmetic: 23 us -> 8.93 us
  waiting for transfers between devices: 98.5 us -> 85.2 us
  local copies, waits for them, and re-layouts: 29.9 us -> 20.9 us
    all_to_all x2 -> x0, blocking collectives: 49.9 us -> none  [exchange(): return lax.all_to_all(x, axis, 0, 0, axis_index_groups=groups, tiled=True)]
    pallas_call x5 -> x14, Pallas kernels: 49.3 us -> 71.7 us  [the longest x1 11 us: per_device(): call(feed_kernel, (shape((part, width), f32), shape((local, width), bf16)...]
    all_to_all x7 -> x9, starting transfers between devices: 34.4 us -> 52.6 us  [exchange(): return lax.all_to_all(x, axis, 0, 0, axis_index_groups=groups, tiled=True)]
    dot_general x8 -> x0, matrix products: 17.2 us -> none  [the longest x5 7.57 us: t_dot(): lax.dot_general(a, b, (((0,), (0,)), ((), ())), preferred_element_type=f32)]
    all_gather x2 -> x1, waiting for transfers between devices: 8.86 us -> 0.02 us  [per_device(): dy_all = lax.all_gather(cotangent, 'tp', axis=0, tiled=True)]
    ppermute x2 -> x8, starting transfers between devices: 4.65 us -> 10.8 us  [the longest x1 2.44 us: per_device(): query_other = lax.ppermute(query, 'ctx', other_core)]
    convert_element_type x6 -> x0, other arithmetic: 6.11 us -> none  [the longest x1 2.8 us: per_device(): (dkv_own + dkv_moved.astype(f32)).astype(bf16).reshape(half, local, LANES)]
    unnamed x80 -> x54, local copies, waits for them, and re-layouts: 18.2 us -> 13.1 us
  transfers between devices with their start and end apart: 12 -> 19, of which waited for: 9 -> 11; matrix products, arithmetic and copies ran while one was open for 20% -> 8% of each run, Pallas kernels for 16% -> 21%
where the time goes in v2:
time: 278 us
  waiting for transfers between devices  85.2 us (31%)
  Pallas kernels  75.4 us (27%)
  starting transfers between devices  63.5 us (23%)
  local copies, waits for them, and re-layouts  20.9 us (8%)
  between operations  18.2 us (7%)
  other arithmetic  8.93 us (3%)
  matrix products  5.46 us (2%)
    all_to_all x9, waiting for transfers between devices, exchange(): return lax.all_to_all(x, axis, 0, 0, axis_index_groups=groups, tiled=True)  82.1 us
    all_to_all x9, starting transfers between devices, exchange(): return lax.all_to_all(x, axis, 0, 0, axis_index_groups=groups, tiled=True)  52.6 us
    unnamed x54, local copies, waits for them, and re-layouts  13.1 us
    pallas_call x1, Pallas kernels, per_device(): call(feed_kernel, (shape((part, width), f32), shape((local, width), bf16)...  11 us
    pallas_call x1, Pallas kernels, per_device(): call(attend_kernel, (shape((2 * local, LANES), f32), shape((2 * local, LA...  10.4 us
    pallas_call x1, Pallas kernels, per_device(): call(partial(pull_kernel, True), (shape(keys_shape, bf16), shape((local,...  10 us
    pallas_call x1, Pallas kernels, per_device(): call(partial(pull_kernel, False), (shape(keys_shape, f32), shape((local,...  8.33 us
    pallas_call x1, Pallas kernels, per_device(): call(weights_kernel, shape((width, 3 * hidden_width), bf16), in_specs=in_...  6.26 us
  transfers between devices with their start and end apart: 19, of which 11 were waited for; matrix products, arithmetic and copies ran while one was open for 8% of the time, Pallas kernels for 21%

profile of v2, /device:TPU:1, one launch (start us, length us, event | category | flops | bytes accessed | tf_op | source)
XLA Modules:
  0.0 277.6 jit_solution(7259178134295828141)
XLA Ops:
  9.4 6.9 %all-to-all-start = ((bf16[8,64,1024]{2,1,0:T(8,128)(2,1)}), bf16[8,64,1024]{2,1,0:T(8,128)(2,1)S(1)}, u32[]{:S(2)}, u32[]{:S(2)}) async-start(bf16[8,64,1024]{2,1,0:T(8,128)(2,1)} %broadcast_in_dim.4), calls=%async_computation | async-start | bytes 2097152 | tf_op jit(solution)/shard_map/all_to_all | solution.py:50
  25.1 5.7 %all-to-all-done = bf16[8,64,1024]{2,1,0:T(8,128)(2,1)S(1)} async-done(((bf16[8,64,1024]{2,1,0:T(8,128)(2,1)}), bf16[8,64,1024]{2,1,0:T(8,128)(2,1)S(1)}, u32[]{:S(2)}, u32[]{:S(2)}) %all-to-all-start) | async-done | bytes 1048608 | tf_op jit(solution)/shard_map/all_to_all | solution.py:50
  31.8 3.7 %project.1 = (bf16[512,1024]{1,0:T(8,128)(2,1)}, f32[512,256]{1,0:T(8,128)}, bf16[512,128]{1,0:T(8,128)(2,1)}, bf16[8,512,128]{2,1,0:T(8,128)(2,1)}) custom-call(bf16[512,1024]{1,0:T(8,128)(2,1)} %bitcast.32, f32[1,1024]{1,0:T(1,128)} %bitcast.40, bf16[1024,256]{1,0:T(8,128)(2,1)} %pad_maximum_fusion.2.w_ref, f32[2,128]{1,0:T(2,128)} %pad_maximum_fusion.5.head_gain_ref, ...), custom_call_target="tpu_custom_call" | custom-call | tf_op jit(solution)/shard_map/project/pallas_call | solution.py:536
  35.5 6.4 %all-to-all-start.1 = ((bf16[8,512,128]{2,1,0:T(8,128)(2,1)}), bf16[8,512,128]{2,1,0:T(8,128)(2,1)S(1)}, u32[]{:S(2)}, u32[]{:S(2)}) async-start(bf16[8,512,128]{2,1,0:T(8,128)(2,1)} %get-tuple-element.74), calls=%async_computation.1 | async-start | bytes 2097152 | tf_op jit(solution)/shard_map/all_to_all | solution.py:50
  46.0 2.4 collective-permute-start
  48.4 3.5 %pad_maximum_fusion.w_pair_ref = bf16[1024,1152]{1,0:T(8,128)(2,1)} fusion(bf16[1024,576]{1,0:T(8,128)(2,1)} %copy.37, bf16[1024,576]{1,0:T(8,128)(2,1)S(1)} %copy.36), kind=kLoop, calls=%fused_computation | loop fusion | flops 4718592 | bytes 4718592 | tf_op jit(solution)/shard_map/concatenate | solution.py:558
  52.8 3.2 %all-to-all-done.1 = bf16[8,512,128]{2,1,0:T(8,128)(2,1)S(1)} async-done(((bf16[8,512,128]{2,1,0:T(8,128)(2,1)}), bf16[8,512,128]{2,1,0:T(8,128)(2,1)S(1)}, u32[]{:S(2)}, u32[]{:S(2)}) %all-to-all-start.1) | async-done | bytes 1048608 | tf_op jit(solution)/shard_map/all_to_all | solution.py:50
  57.2 4.9 %all-to-all-start.2 = ((bf16[8,128,512]{2,1,0:T(8,128)(2,1)}), bf16[8,128,512]{2,1,0:T(8,128)(2,1)S(1)}, u32[]{:S(2)}, u32[]{:S(2)}) async-start(bf16[8,128,512]{2,1,0:T(8,128)(2,1)} %broadcast_in_dim.5), calls=%async_computation.2 | async-start | bytes 2097152 | tf_op jit(solution)/shard_map/all_to_all | solution.py:50
  62.2 10.4 %attend.1 = (f32[1024,128]{1,0:T(8,128)}, bf16[1024,128]{1,0:T(8,128)(2,1)}) custom-call(s32[32]{0:T(128)} %order_ref.5, bf16[512,128]{1,0:T(8,128)(2,1)} %get-tuple-element.76.own_ref.query_ref, bf16[512,128]{1,0:T(8,128)(2,1)} %collective-permute-done.other_ref, bf16[4096,128]{1,0:T(8,128)(2,1)} %bitcast.34), custom_call_target="tpu_custom_call" | custom-call | flops 8000000000 | bytes 2097152 | tf_op jit(solution)/shard_map/attend/pallas_call | solution.py:561
  75.1 3.1 %finish.1 = (f32[1024,128]{1,0:T(8,128)}, bf16[8,512,128]{2,1,0:T(8,128)(2,1)}, bf16[1024,128]{1,0:T(8,128)(2,1)}) custom-call(f32[1024,128]{1,0:T(8,128)} %get-tuple-element.77.acc_ref, bf16[1024,128]{1,0:T(8,128)(2,1)} %copy-done.15, bf16[512,128]{1,0:T(8,128)(2,1)} %get-tuple-element.76.own_ref.query_ref), custom_call_target="tpu_custom_call" | custom-call | tf_op jit(solution)/shard_map/finish/pallas_call | solution.py:572
  78.1 10.5 %all-to-all-done.2 = bf16[8,128,512]{2,1,0:T(8,128)(2,1)S(1)} async-done(((bf16[8,128,512]{2,1,0:T(8,128)(2,1)}), bf16[8,128,512]{2,1,0:T(8,128)(2,1)S(1)}, u32[]{:S(2)}, u32[]{:S(2)}) %all-to-all-start.2) | async-done | bytes 1048608 | tf_op jit(solution)/shard_map/all_to_all | solution.py:50
  91.0 3.7 %all-to-all-start.3 = ((bf16[8,512,128]{2,1,0:T(8,128)(2,1)}), bf16[8,512,128]{2,1,0:T(8,128)(2,1)S(1)}, u32[]{:S(2)}, u32[]{:S(2)}) async-start(bf16[8,512,128]{2,1,0:T(8,128)(2,1)} %get-tuple-element.83), calls=%async_computation.3 | async-start | bytes 2097152 | tf_op jit(solution)/shard_map/all_to_all | solution.py:50
  94.8 3.3 %fusion.3.hidden_grad_ref = f32[512,576]{1,0:T(8,128)} fusion(bf16[512,1024]{1,0:T(8,128)(2,1)} %all-gather.2.cloned.1.call-done.dy_ref, bf16[576,1024]{1,0:T(8,128)(2,1)S(1)} %copy-done), kind=kOutput, calls=%fused_computation.22 | convolution fusion | flops 603979776 | bytes 3407872 | tf_op jit(solution)/shard_map/dot_general | solution.py:26
  98.1 12.3 %all-to-all-done.3.attended_ref = bf16[8,512,128]{2,1,0:T(8,128)(2,1)S(1)} async-done(((bf16[8,512,128]{2,1,0:T(8,128)(2,1)}), bf16[8,512,128]{2,1,0:T(8,128)(2,1)S(1)}, u32[]{:S(2)}, u32[]{:S(2)}) %all-to-all-start.3) | async-done | bytes 1048608 | tf_op jit(solution)/shard_map/all_to_all | solution.py:50
  111.4 11.0 %feed.1 = (f32[64,1024]{1,0:T(8,128)}, bf16[512,1024]{1,0:T(8,128)(2,1)}, bf16[512,576]{1,0:T(8,128)(2,1)}, bf16[512,1152]{1,0:T(8,128)(2,1)}, bf16[512,1024]{1,...) custom-call(bf16[512,1024]{1,0:T(8,128)(2,1)} %bitcast.33, bf16[8,512,128]{2,1,0:T(8,128)(2,1)} %copy-done.9, ...), custom_call_target="tpu_custom_call" | custom-call | flops 5000000000 | bytes 8388608 | tf_op jit(solution)/shard_map/feed/pallas_call | solution.py:590
  122.4 3.7 %all-to-all-start.4 = ((bf16[8,512,128]{2,1,0:T(8,128)(2,1)}), bf16[8,512,128]{2,1,0:T(8,128)(2,1)S(1)}, u32[]{:S(2)}, u32[]{:S(2)}) async-start(bf16[8,512,128]{2,1,0:T(8,128)(2,1)} %get-tuple-element.86), calls=%async_computation.4 | async-start | bytes 2097152 | tf_op jit(solution)/shard_map/all_to_all | solution.py:50
  128.2 6.3 %weights.1 = bf16[1024,1728]{1,0:T(8,128)(2,1)} custom-call(bf16[512,1024]{1,0:T(8,128)(2,1)} %get-tuple-element.120.normed_ref, bf16[512,1152]{1,0:T(8,128)(2,1)} %get-tuple-element.121.pair_ref, bf16[512,1024]{1,0:T(8,128)(2,1)} %all-gather.2.cloned.1.call-done.dy_ref, bf16[512,576]{1,0:T(8,128)(2,1)} %get-tuple-element.91.hidden_ref), custom_call_target="tpu_custom_call" | custom-call | tf_op jit(solution)/shard_map/weights/pallas_call | solution.py:616
  138.3 2.7 all-to-all-done.4.recv_ref
  142.1 3.6 %all-to-all-start.5 = ((bf16[8,64,2048]{2,1,0:T(8,128)(2,1)}), bf16[8,64,2048]{2,1,0:T(8,128)(2,1)S(1)}, u32[]{:S(2)}, u32[]{:S(2)}) async-start(bf16[8,64,2048]{2,1,0:T(8,128)(2,1)} %bitcast.31), calls=%async_computation.5 | async-start | bytes 4194304 | tf_op jit(solution)/shard_map/all_to_all | solution.py:50
  145.7 2.6 prepare.1.dx_ref
  150.0 8.3 %pull_own.1 = (f32[4096,128]{1,0:T(8,128)}, f32[512,128]{1,0:T(8,128)}) custom-call(s32[32]{0:T(128)} %order_ref.5, bf16[4096,128]{1,0:T(8,128)(2,1)} %bitcast.35, bf16[1024,128]{1,0:T(8,128)(2,1)} %get-tuple-element.79.qb_ref, bf16[1024,128]{1,0:T(8,128)(2,1)} %prepare.1.dx_ref), custom_call_target="tpu_custom_call" | custom-call | flops 20000000000 | bytes 4194304 | tf_op jit(solution)/shard_map/pull_own/pallas_call | solution.py:639
  159.0 10.0 %pull_other.1 = (bf16[4096,128]{1,0:T(8,128)(2,1)}, bf16[512,128]{1,0:T(8,128)(2,1)}) custom-call(s32[32]{0:T(128)} %order_ref.5, bf16[4096,128]{1,0:T(8,128)(2,1)} %bitcast.36, bf16[1024,128]{1,0:T(8,128)(2,1)} %collective-permute-done.2.qb_ref, bf16[1024,128]{1,0:T(8,128)(2,1)} %copy-done.23, f32[4096,128]{1,0:T(8,128)} %get-tuple-element.88.refs_0_), custom_call_target="tpu_custom_call" | custom-call | flops 20000000000 | bytes 4194304 | tf_op jit(solution)/shard_map/pull_other/pallas_call | solution.py:648
  171.0 12.7 %all-to-all-start.6 = ((bf16[8,512,128]{2,1,0:T(8,128)(2,1)}), bf16[8,512,128]{2,1,0:T(8,128)(2,1)}, u32[]{:S(2)}, u32[]{:S(2)}) async-start(bf16[8,512,128]{2,1,0:T(8,128)(2,1)} %bitcast.39), calls=%async_computation.6 | async-start | bytes 2097152 | tf_op jit(solution)/shard_map/all_to_all | solution.py:50
  183.7 2.7 rows.1
  186.4 13.6 %all-to-all-done.6.recv_ref = bf16[8,512,128]{2,1,0:T(8,128)(2,1)} async-done(((bf16[8,512,128]{2,1,0:T(8,128)(2,1)}), bf16[8,512,128]{2,1,0:T(8,128)(2,1)}, u32[]{:S(2)}, u32[]{:S(2)}) %all-to-all-start.6) | async-done | bytes 1048608 | tf_op jit(solution)/shard_map/all_to_all | solution.py:50
  200.0 5.7 %back.1 = (bf16[512,256]{1,0:T(8,128)(2,1)}, bf16[8,144,1024]{2,1,0:T(8,128)(2,1)}) custom-call(f32[512,128]{1,0:T(8,128)} %get-tuple-element.95.dq_ref, bf16[512,128]{1,0:T(8,128)(2,1)} %copy-done.18, bf16[8,512,128]{2,1,0:T(8,128)(2,1)} %all-to-all-done.6.recv_ref, f32[512,256]{1,0:T(8,128)} %get-tuple-element.98.pre_ref, ...), custom_call_target="tpu_custom_call" | custom-call | tf_op jit(solution)/shard_map/back/pallas_call | solution.py:670
  205.6 5.7 %all-to-all-start.7 = ((bf16[8,144,1024]{2,1,0:T(8,128)(2,1)}), bf16[8,144,1024]{2,1,0:T(8,128)(2,1)S(1)}, u32[]{:S(2)}, u32[]{:S(2)}) async-start(bf16[8,144,1024]{2,1,0:T(8,128)(2,1)} %get-tuple-element.102), calls=%async_computation.7 | async-start | bytes 4718592 | tf_op jit(solution)/shard_map/all_to_all | solution.py:50
  211.4 2.7 grads.1
  216.6 23.6 %all-to-all-done.7.recv_ref = bf16[8,144,1024]{2,1,0:T(8,128)(2,1)S(1)} async-done(((bf16[8,144,1024]{2,1,0:T(8,128)(2,1)}), bf16[8,144,1024]{2,1,0:T(8,128)(2,1)S(1)}, u32[]{:S(2)}, u32[]{:S(2)}) %all-to-all-start.7) | async-done | bytes 2359328 | tf_op jit(solution)/shard_map/all_to_all | solution.py:50
  241.6 3.3 %tokens.1 = (bf16[64,1024]{1,0:T(8,128)(2,1)}, bf16[528,384]{1,0:T(8,128)(2,1)}, bf16[528,384]{1,0:T(8,128)(2,1)}) custom-call(bf16[8,144,1024]{2,1,0:T(8,128)(2,1)} %copy-done.1, bf16[64,1024]{1,0:T(8,128)(2,1)} %tokens_ref.1, f32[1,1024]{1,0:T(1,128)} %bitcast.42, f32[64,1024]{1,0:T(8,128)} %get-tuple-element.101.grad_ref.resid_grad_ref, ...), custom_call_target="tpu_custom_call" | custom-call | tf_op jit(solution)/shard_map/tokens/pallas_call | solution.py:692
  251.4 5.1 %all-to-all-start.8 = ((bf16[8,80,384]{2,1,0:T(8,128)(2,1)}), bf16[8,80,384]{2,1,0:T(8,128)(2,1)S(1)}, u32[]{:S(2)}, u32[]{:S(2)}) async-start(bf16[8,80,384]{2,1,0:T(8,128)(2,1)} %merge.1), calls=%async_computation.8 | async-start | bytes 983040 | tf_op jit(solution)/shard_map/all_to_all | solution.py:50
  258.3 8.6 %all-to-all-done.8.recv_ref = bf16[8,80,384]{2,1,0:T(8,128)(2,1)S(1)} async-done(((bf16[8,80,384]{2,1,0:T(8,128)(2,1)}), bf16[8,80,384]{2,1,0:T(8,128)(2,1)S(1)}, u32[]{:S(2)}, u32[]{:S(2)}) %all-to-all-start.8) | async-done | bytes 491552 | tf_op jit(solution)/shard_map/all_to_all | solution.py:50
  (97 shorter events, 47.5 us)
Async XLA Ops:
  7.2 87.6 %copy-start = (bf16[576,1024]{1,0:T(8,128)(2,1)S(1)}, bf16[576,1024]{1,0:T(8,128)(2,1)}, u32[]{:S(2)}) copy-start(bf16[576,1024]{1,0:T(8,128)(2,1)} %param.29) | copy-start | bytes 3538948
  7.2 9.1 %copy-start.20 = (s32[32]{0:T(128)S(1)}, s32[32]{0:T(128)}, u32[]{:S(2)}) copy-start(s32[32]{0:T(128)} %order_ref.5) | copy-start | bytes 388
  7.2 12.3 %copy-start.19 = (s32[8192]{0:T(1024)S(1)}, s32[8192]{0:T(1024)}, u32[]{:S(2)}) copy-start(s32[8192]{0:T(1024)} %param.17) | copy-start | bytes 98308
  7.2 12.3 %copy-start.16 = (bf16[1024,64]{0,1:T(8,128)(2,1)S(1)}, bf16[1024,64]{0,1:T(8,128)(2,1)}, u32[]{:S(2)}) copy-start(bf16[1024,64]{0,1:T(8,128)(2,1)} %param.21) | copy-start | bytes 393220
  7.2 12.5 %copy-start.17 = (bf16[1024,64]{0,1:T(8,128)(2,1)S(1)}, bf16[1024,64]{0,1:T(8,128)(2,1)}, u32[]{:S(2)}) copy-start(bf16[1024,64]{0,1:T(8,128)(2,1)} %param.22) | copy-start | bytes 393220
  7.2 14.0 %copy-start.22 = (f32[64]{0:T(128)S(1)}, f32[64]{0:T(128)}, u32[]{:S(2)}) copy-start(f32[64]{0:T(128)} %param.24) | copy-start | bytes 772
  7.2 14.0 %copy-start.21 = (f32[64]{0:T(128)S(1)}, f32[64]{0:T(128)}, u32[]{:S(2)}) copy-start(f32[64]{0:T(128)} %param.23) | copy-start | bytes 772
  7.3 14.7 %copy-start.14 = (bf16[1024,128]{1,0:T(8,128)(2,1)S(1)}, bf16[1024,128]{1,0:T(8,128)(2,1)}, u32[]{:S(2)}) copy-start(bf16[1024,128]{1,0:T(8,128)(2,1)} %param.20) | copy-start | bytes 786436
  9.4 21.4 %all-to-all-start = ((bf16[8,64,1024]{2,1,0:T(8,128)(2,1)}), bf16[8,64,1024]{2,1,0:T(8,128)(2,1)S(1)}, u32[]{:S(2)}, u32[]{:S(2)}) async-start(bf16[8,64,1024]{2,1,0:T(8,128)(2,1)} %broadcast_in_dim.4), calls=%async_computation | async-start | bytes 2097152 | tf_op jit(solution)/shard_map/all_to_all | solution.py:50
  35.5 20.6 %all-to-all-start.1 = ((bf16[8,512,128]{2,1,0:T(8,128)(2,1)}), bf16[8,512,128]{2,1,0:T(8,128)(2,1)S(1)}, u32[]{:S(2)}, u32[]{:S(2)}) async-start(bf16[8,512,128]{2,1,0:T(8,128)(2,1)} %get-tuple-element.74), calls=%async_computation.1 | async-start | bytes 2097152 | tf_op jit(solution)/shard_map/all_to_all | solution.py:50
  41.8 52.9 %all-gather.2.cloned.1.call-start = ((), (), s32[]{:S(2)}) async-start(), calls=%async_computation.10 | async-start | bytes 1179648 | tf_op jit(solution)/shard_map/all_gather | solution.py:531
  46.0 16.1 %collective-permute-start = (bf16[512,128]{1,0:T(8,128)(2,1)}, bf16[512,128]{1,0:T(8,128)(2,1)}, u32[]{:S(2)}, u32[]{:S(2)}) collective-permute-start(bf16[512,128]{1,0:T(8,128)(2,1)} %get-tuple-element.76.own_ref.query_ref), channel_id=1, source_target_pairs={{0,8},{8,0},{16,24},{24,16},{32,40},{40,32},{48,56},{56,48},{64,72... | collective-permute-start | bytes 393224 | tf_op jit(solution)/shard_map/ppermute | solution.py:556
  56.1 6.1 %copy-start.7 = (bf16[8,512,128]{2,1,0:T(8,128)(2,1)}, bf16[8,512,128]{2,1,0:T(8,128)(2,1)S(1)}, u32[]{:S(2)}) copy-start(bf16[8,512,128]{2,1,0:T(8,128)(2,1)S(1)} %all-to-all-done.1) | copy-start | bytes 3145732
  57.2 31.4 %all-to-all-start.2 = ((bf16[8,128,512]{2,1,0:T(8,128)(2,1)}), bf16[8,128,512]{2,1,0:T(8,128)(2,1)S(1)}, u32[]{:S(2)}, u32[]{:S(2)}) async-start(bf16[8,128,512]{2,1,0:T(8,128)(2,1)} %broadcast_in_dim.5), calls=%async_computation.2 | async-start | bytes 2097152 | tf_op jit(solution)/shard_map/all_to_all | solution.py:50
  72.5 1.8 collective-permute-start.1
  88.6 9.5 %copy-start.8 = (bf16[8,128,512]{2,1,0:T(8,128)(2,1)}, bf16[8,128,512]{2,1,0:T(8,128)(2,1)S(1)}, u32[]{:S(2)}) copy-start(bf16[8,128,512]{2,1,0:T(8,128)(2,1)S(1)} %all-to-all-done.2) | copy-start | bytes 3145732
  88.6 21.8 %collective-permute-start.3 = (bf16[1024,512]{1,0:T(8,128)(2,1)S(1)}, bf16[1024,512]{1,0:T(8,128)(2,1)}, u32[]{:S(2)}, u32[]{:S(2)}) collective-permute-start(bf16[1024,512]{1,0:T(8,128)(2,1)S(1)} %bitcast.37), channel_id=1, source_target_pairs={{0,8},{8,0},{16,24},{24,16},{32,40},{40,32},{48,56},{56,48},{64,72... | collective-permute-start | bytes 3145736 | tf_op jit(solution)/shard_map/ppermute | solution.py:585
  91.0 19.4 %all-to-all-start.3 = ((bf16[8,512,128]{2,1,0:T(8,128)(2,1)}), bf16[8,512,128]{2,1,0:T(8,128)(2,1)S(1)}, u32[]{:S(2)}, u32[]{:S(2)}) async-start(bf16[8,512,128]{2,1,0:T(8,128)(2,1)} %get-tuple-element.83), calls=%async_computation.3 | async-start | bytes 2097152 | tf_op jit(solution)/shard_map/all_to_all | solution.py:50
  122.4 18.7 %all-to-all-start.4 = ((bf16[8,512,128]{2,1,0:T(8,128)(2,1)}), bf16[8,512,128]{2,1,0:T(8,128)(2,1)S(1)}, u32[]{:S(2)}, u32[]{:S(2)}) async-start(bf16[8,512,128]{2,1,0:T(8,128)(2,1)} %get-tuple-element.86), calls=%async_computation.4 | async-start | bytes 2097152 | tf_op jit(solution)/shard_map/all_to_all | solution.py:50
  126.1 130.4 %reduce-scatter.2.cloned.1.call-start = ((), (), s32[]{:S(2)}) async-start(), calls=%async_computation.11 | async-start | bytes 3899392 | tf_op jit(solution)/shard_map/reduce_scatter | solution.py:623
  126.2 32.2 %collective-permute-start.2 = (bf16[1024,128]{1,0:T(8,128)(2,1)}, bf16[1024,128]{1,0:T(8,128)(2,1)}, u32[]{:S(2)}, u32[]{:S(2)}) collective-permute-start(bf16[1024,128]{1,0:T(8,128)(2,1)} %get-tuple-element.79.qb_ref), channel_id=1, source_target_pairs={{0,8},{8,0},{16,24},{24,16},{32,40},{40,32},{48,56},{56,48},{64,72... | collective-permute-start | bytes 786440 | tf_op jit(solution)/shard_map/ppermute | solution.py:583
  142.1 28.9 %all-to-all-start.5 = ((bf16[8,64,2048]{2,1,0:T(8,128)(2,1)}), bf16[8,64,2048]{2,1,0:T(8,128)(2,1)S(1)}, u32[]{:S(2)}, u32[]{:S(2)}) async-start(bf16[8,64,2048]{2,1,0:T(8,128)(2,1)} %bitcast.31), calls=%async_computation.5 | async-start | bytes 4194304 | tf_op jit(solution)/shard_map/all_to_all | solution.py:50
  148.3 10.0 %collective-permute-start.4 = (bf16[1024,128]{1,0:T(8,128)(2,1)}, bf16[1024,128]{1,0:T(8,128)(2,1)S(1)}, u32[]{:S(2)}, u32[]{:S(2)}) collective-permute-start(bf16[1024,128]{1,0:T(8,128)(2,1)} %prepare.1.dx_ref), channel_id=1, source_target_pairs={{0,8},{8,0},{16,24},{24,16},{32,40},{40,32},{48,56},{56,48},{64,72... | collective-permute-start | bytes 786440 | tf_op jit(solution)/shard_map/ppermute | solution.py:635
  169.0 14.6 %copy-start.24 = (bf16[512,128]{1,0:T(8,128)(2,1)S(1)}, bf16[512,128]{1,0:T(8,128)(2,1)}, u32[]{:S(2)}) copy-start(bf16[512,128]{1,0:T(8,128)(2,1)} %get-tuple-element.96) | copy-start | bytes 393220
  171.0 12.8 %copy-start.2 = (bf16[8,64,2048]{2,1,0:T(8,128)(2,1)}, bf16[8,64,2048]{2,1,0:T(8,128)(2,1)S(1)}, u32[]{:S(2)}) copy-start(bf16[8,64,2048]{2,1,0:T(8,128)(2,1)S(1)} %all-to-all-done.5.recv_ref) | copy-start | bytes 6291460
  171.0 29.0 %all-to-all-start.6 = ((bf16[8,512,128]{2,1,0:T(8,128)(2,1)}), bf16[8,512,128]{2,1,0:T(8,128)(2,1)}, u32[]{:S(2)}, u32[]{:S(2)}) async-start(bf16[8,512,128]{2,1,0:T(8,128)(2,1)} %bitcast.39), calls=%async_computation.6 | async-start | bytes 2097152 | tf_op jit(solution)/shard_map/all_to_all | solution.py:50
  183.6 2.8 %collective-permute-start.5 = (bf16[512,128]{1,0:T(8,128)(2,1)S(1)}, bf16[512,128]{1,0:T(8,128)(2,1)S(1)}, u32[]{:S(2)}, u32[]{:S(2)}) collective-permute-start(bf16[512,128]{1,0:T(8,128)(2,1)S(1)} %copy-done.24), channel_id=1, source_target_pairs={{0,8},{8,0},{16,24},{24,16},{32,40},{40,32},{48,56},{56,48},{64,72... | collective-permute-start | bytes 393224 | tf_op jit(solution)/shard_map/ppermute | solution.py:667
  186.4 13.6 %copy-start.18 = (bf16[512,128]{1,0:T(8,128)(2,1)}, bf16[512,128]{1,0:T(8,128)(2,1)S(1)}, u32[]{:S(2)}) copy-start(bf16[512,128]{1,0:T(8,128)(2,1)S(1)} %collective-permute-done.5.dq_recv_ref) | copy-start | bytes 393220
  205.6 34.6 %all-to-all-start.7 = ((bf16[8,144,1024]{2,1,0:T(8,128)(2,1)}), bf16[8,144,1024]{2,1,0:T(8,128)(2,1)S(1)}, u32[]{:S(2)}, u32[]{:S(2)}) async-start(bf16[8,144,1024]{2,1,0:T(8,128)(2,1)} %get-tuple-element.102), calls=%async_computation.7 | async-start | bytes 4718592 | tf_op jit(solution)/shard_map/all_to_all | solution.py:50
  214.0 2.6 collective-permute-start.6
  245.0 3.5 %collective-permute-start.7 = (bf16[528,384]{1,0:T(8,128)(2,1)}, bf16[528,384]{1,0:T(8,128)(2,1)S(1)}, u32[]{:S(2)}, u32[]{:S(2)}) collective-permute-start(bf16[528,384]{1,0:T(8,128)(2,1)} %get-tuple-element.112), channel_id=1, source_target_pairs={{0,8},{8,0},{16,24},{24,16},{32,40},{40,32},{48,56},{56,48},{64,72... | collective-permute-start | bytes 1216520 | tf_op jit(solution)/shard_map/ppermute | solution.py:706
  251.4 15.4 %all-to-all-start.8 = ((bf16[8,80,384]{2,1,0:T(8,128)(2,1)}), bf16[8,80,384]{2,1,0:T(8,128)(2,1)S(1)}, u32[]{:S(2)}, u32[]{:S(2)}) async-start(bf16[8,80,384]{2,1,0:T(8,128)(2,1)} %merge.1), calls=%async_computation.8 | async-start | bytes 983040 | tf_op jit(solution)/shard_map/all_to_all | solution.py:50
  (12 other events, 18.9 us)
Sparse Core Ops, SparseCore 0:
  52.0 42.3 all-gather.1
  134.6 78.8 reduce-scatter.1

commit v3 on v2

--- a/solution.py
+++ b/solution.py
@@ -12,7 +12,8 @@
 theta = 1000000.0
 bf16 = jnp.bfloat16
 f32 = jnp.float32
-vmem_bytes = 56 * 1024 * 1024
+large = 56 * 1024 * 1024
+small = 24 * 1024 * 1024
 log2e = math.log2(math.e)
 HEAD = 64
 LANES = 128
@@ -30,7 +31,7 @@
     return lax.dot_general(a, b, (((0,), (0,)), ((), ())), preferred_element_type=f32)
 
 
-def call(kernel, out_shape, **more):
+def call(kernel, out_shape, vmem_bytes=small, **more):
     return pl.pallas_call(
         kernel,
         out_shape=out_shape,
@@ -95,12 +96,12 @@
 
 
 def earlier_spans(order_ref, list_ref, rank, core, blocks):
-    def look(block, count):
-        list_ref[count] = block
+    count = jnp.int32(0)
+    for block in range(blocks):
+        list_ref[count] = jnp.int32(block)
         slot = ((block // 2) * 2 + core) * 2 + block % 2
-        return count + (order_ref[slot] < rank).astype(jnp.int32)
-
-    return lax.fori_loop(0, blocks, look, jnp.int32(0))
+        count = count + (order_ref[slot] < rank).astype(jnp.int32)
+    return count
 
 
 def block_rows(index, span):
@@ -132,14 +133,13 @@
     return parts
 
 
-def attend_kernel(order_ref, own_ref, other_ref, kv_ref, acc_ref, sent_ref, list_ref, qx_ref, part_ref):
+def attend_kernel(order_ref, own_ref, other_ref, kv_ref, acc_ref, sent_ref, list_ref, qx_ref, sum_ref):
     me = lax.axis_index("ctx")
     core = me % 2
     span = own_ref.shape[0] // 2
     blocks = kv_ref.shape[0] // span
     left = left_half((span, LANES))
     lane = lax.broadcasted_iota(jnp.int32, (span, LANES), 1)
-    one = jnp.ones((span, LANES), bf16)
     for source in range(2):
         for slot in range(2):
             query = (own_ref, other_ref)[source][pl.ds(slot * span, span), :].astype(f32)
@@ -148,31 +148,32 @@
                 qx_ref[pl.ds(head * span, span), :] = jnp.where(left, own, 0.0).astype(bf16)
             rank = order_ref[(me + source * (1 - 2 * core)) * 2 + slot]
             count = earlier_spans(order_ref, list_ref, rank, core, blocks)
-            rows = pl.ds(slot * 2 * span, 2 * span)
-
-            def product(index, mask=None):
-                pair = kv_ref[block_rows(index, span), :]
-                weights = jnp.exp2(dot_t(qx_ref[...], pair))
+
+            def product(indices, mask=None):
+                pair = jnp.concatenate([kv_ref[block_rows(k, span), :] for k in indices], axis=0)
+                weights = jnp.exp2(dot_t(pair, qx_ref[...]))
                 if mask is not None:
                     weights = jnp.where(mask, weights, 0.0)
-                return dot(weights.astype(bf16), jnp.where(left, one, pair))
-
-            target = acc_ref if source == 0 else part_ref
+                values = jnp.where(left_half(pair.shape), jnp.ones_like(pair), pair)
+                return t_dot(values, weights.astype(bf16))
+
             if source == 0:
-                row = lax.broadcasted_iota(jnp.int32, (2 * span, span), 0) % span
-                col = lax.broadcasted_iota(jnp.int32, (2 * span, span), 1)
-                target[rows, :] = product((me // 2) * 2 + slot, row >= col)
+                row = lax.broadcasted_iota(jnp.int32, (span, 2 * span), 0)
+                col = lax.broadcasted_iota(jnp.int32, (span, 2 * span), 1) % span
+                sum_ref[...] = product([(me // 2) * 2 + slot], col >= row)
             else:
-                target[rows, :] = jnp.zeros((2 * span, LANES), f32)
+                sum_ref[...] = jnp.zeros_like(sum_ref)
 
             def add(steps):
-                target[rows, :] += sum(product(list_ref[step]) for step in steps)
+                sum_ref[...] += product([list_ref[step] for step in steps])
 
             in_groups(count, 4, add)
-            if source == 1:
-                for head in range(2):
-                    part = pl.ds((slot * 2 + head) * span, span)
-                    acc = target[part, :]
+            for head in range(2):
+                part = pl.ds((slot * 2 + head) * span, span)
+                acc = sum_ref[:, head * span : (head + 1) * span].T
+                if source == 0:
+                    acc_ref[part, :] = acc
+                else:
                     high, middle, low = pieces(acc, 3)
                     packed = jnp.where(lane == 0, high, jnp.where(lane == 1, middle, low))
                     packed = jnp.where(lane < 3, packed, jnp.where(left, 0.0, acc))
@@ -258,7 +259,7 @@
             pulled = dot_t(jnp.where(left, one, pair), dx_ref[rows, :])
             score = (weights * pulled).astype(bf16)
             dkv_ref[part, :] += dot(score, qz_ref[...]) + dot(weights.astype(bf16), dz_ref[...])
-            return t_dot(score, pair)
+            return t_dot(pair, score)
 
         if last:
             dq_ref[...] = jnp.zeros_like(dq_ref)
@@ -270,8 +271,9 @@
         def add(steps):
             dq_ref[...] += sum(product(list_ref[step]) for step in steps)
 
-        in_groups(count, 2, add)
-        both = jnp.where(left, dq_ref[:span, :], pltpu.roll(dq_ref[span:, :], HEAD, 1))
+        in_groups(count, 4, add)
+        first, second = dq_ref[:, :span].T, dq_ref[:, span:].T
+        both = jnp.where(left, first, pltpu.roll(second, HEAD, 1))
         dq_out_ref[pl.ds(slot * span, span), :] = both.astype(dq_out_ref.dtype)
     if last:
         factor = jnp.where(left_half((1, LANES)), 1.0 / log2e, 1.0)
@@ -525,8 +527,8 @@
         [jnp.concatenate([query_gain, query_gain]), jnp.concatenate([key_gain, jnp.ones_like(key_gain)])]
     )
 
-    x_all, cotangent, w_qkv, cosine, sine, head_gain = lax.optimization_barrier(
-        (x_all, cotangent, w_qkv, cosine, sine, head_gain)
+    x_all, w_qkv, cosine, sine, head_gain = lax.optimization_barrier(
+        (x_all, w_qkv, cosine, sine, head_gain)
     )
     dy_all = lax.all_gather(cotangent, "tp", axis=0, tiled=True)
 
@@ -556,7 +558,7 @@
     query_other = lax.ppermute(query, "ctx", other_core)
     kv_all = exchange(kv, "ctx", same_core).reshape(half * local, LANES)
     w_pair = jnp.concatenate([w_gate, w_up], axis=1)
-    kv_all, w_pair, w_half = lax.optimization_barrier((kv_all, w_pair, w_half))
+    kv_all, w_pair, w_half, dy_all = lax.optimization_barrier((kv_all, w_pair, w_half, dy_all))
     w_out_own = exchange(w_half, "tp").reshape(width, width // 2)
     acc, sent = call(
         attend_kernel,
@@ -564,7 +566,7 @@
         in_specs=[in_smem, *in_vmem(3)],
         out_specs=tuple(in_vmem(2)),
         scratch_shapes=[
-            slots, pltpu.VMEM((2 * span, LANES), bf16), pltpu.VMEM((2 * local, LANES), f32)
+            slots, pltpu.VMEM((2 * span, LANES), bf16), pltpu.VMEM((LANES, 2 * span), f32)
         ],
         cost_estimate=pl.CostEstimate(flops=8 * 10**9, bytes_accessed=2**21, transcendentals=2**23),
         name="attend",
@@ -607,6 +609,7 @@
         ],
         cost_estimate=pl.CostEstimate(flops=5 * 10**9, bytes_accessed=2**23, transcendentals=2**18),
         name="feed",
+        vmem_bytes=large,
     )(
         x_all, attended_all, w_out_own, w_out_other, second_gain.reshape(1, width), w_pair,
         hidden_grad,
@@ -619,6 +622,7 @@
         in_specs=in_vmem(4),
         out_specs=pl.BlockSpec(memory_space=pltpu.VMEM),
         name="weights",
+        vmem_bytes=large,
     )(normed_two, pair_grad, dy_all, hidden)
     feed = lax.psum_scatter(feed, "ctx", scatter_dimension=0, tiled=True)
     down = dot(hidden, w_down).astype(bf16)
@@ -641,7 +645,7 @@
         (shape(keys_shape, f32), shape((local, LANES), f32)),
         in_specs=[in_smem, *in_vmem(3)],
         out_specs=tuple(in_vmem(2)),
-        scratch_shapes=[slots, *halves, pltpu.VMEM((2 * span, LANES), f32)],
+        scratch_shapes=[slots, *halves, pltpu.VMEM((LANES, 2 * span), f32)],
         cost_estimate=pull_cost,
         name="pull_own",
     )(span_order, kv_all, qb, dx)
@@ -651,7 +655,7 @@
         in_specs=[in_smem, *in_vmem(4)],
         out_specs=tuple(in_vmem(2)),
         scratch_shapes=[
-            slots, *halves, pltpu.VMEM(keys_shape, f32), pltpu.VMEM((2 * span, LANES), f32)
+            slots, *halves, pltpu.VMEM(keys_shape, f32), pltpu.VMEM((LANES, 2 * span), f32)
         ],
         cost_estimate=pull_cost,
         name="pull_other",
@@ -673,6 +677,7 @@
         in_specs=in_vmem(12),
         out_specs=tuple(in_vmem(2)),
         name="back",
+        vmem_bytes=large,
     )(dq, dq_recv, dkv_recv, pre, head_gain, cosine, sine, w_qkv, normed, gain_row, second_sum, resid_grad)
     recv = exchange(sent, "tp")
     grads_shape = shape((width // 2, 2 * LANES), bf16)

time: 278 us -> 269 us (0.968)
  Pallas kernels: 75.4 us -> 56 us
  local copies, waits for them, and re-layouts: 20.9 us -> 30 us
    unnamed x54 -> x92, local copies, waits for them, and re-layouts: 13.1 us -> 24.2 us
    all_gather x1, waiting for transfers between devices: 0.02 us -> 4.63 us  [per_device(): dy_all = lax.all_gather(cotangent, 'tp', axis=0, tiled=True)]
    all_to_all x9, starting transfers between devices: 52.6 us -> 48.6 us  [exchange(): return lax.all_to_all(x, axis, 0, 0, axis_index_groups=groups, tiled=True)]
    ppermute x1, starting transfers between devices: 2.44 us -> 5.23 us  [per_device(): query_other = lax.ppermute(query, 'ctx', other_core)]
  transfers between devices with their start and end apart: 19 -> 19, of which waited for: 11 -> 11; matrix products, arithmetic and copies ran while one was open for 8% -> 8% of each run, Pallas kernels for 21% -> 17%
where the time goes in v3:
time: 269 us; the launch traced here: 268 us
  waiting for transfers between devices  87.4 us (32%)
  starting transfers between devices  63.4 us (24%)
  Pallas kernels  56 us (21%)
  local copies, waits for them, and re-layouts  30 us (11%)
  between operations  18.4 us (7%)
  other arithmetic  8.08 us (3%)
  matrix products  4.49 us (2%)
    all_to_all x9, waiting for transfers between devices, exchange(): return lax.all_to_all(x, axis, 0, 0, axis_index_groups=groups, tiled=True)  79.5 us
    all_to_all x9, starting transfers between devices, exchange(): return lax.all_to_all(x, axis, 0, 0, axis_index_groups=groups, tiled=True)  48.6 us
    unnamed x92, local copies, waits for them, and re-layouts  24.2 us
    pallas_call x1, Pallas kernels, per_device(): call(feed_kernel, (shape((part, width), f32), shape((local, width), bf16)...  11 us
    pallas_call x1, Pallas kernels, per_device(): call(partial(pull_kernel, True), (shape(keys_shape, bf16), shape((local,...  9.52 us
    pallas_call x1, Pallas kernels, per_device(): call(attend_kernel, (shape((2 * local, LANES), f32), shape((2 * local, LA...  8.88 us
    pallas_call x1, Pallas kernels, per_device(): call(weights_kernel, shape((width, 3 * hidden_width), bf16), in_specs=in_...  6.28 us
    pallas_call x1, Pallas kernels, per_device(): call(partial(pull_kernel, False), (shape(keys_shape, f32), shape((local,...  6.13 us
  transfers between devices with their start and end apart: 19, of which 11 were waited for; matrix products, arithmetic and copies ran while one was open for 8% of the time, Pallas kernels for 17%

profile of v3, /device:TPU:1, one launch (start us, length us, event | category | flops | bytes accessed | tf_op | source)
XLA Modules:
  0.0 267.9 jit_solution(12798634427672254104)
XLA Ops:
  8.0 2.0 broadcast_in_dim.4
  10.0 6.9 %all-to-all-start = ((bf16[8,64,1024]{2,1,0:T(8,128)(2,1)}), bf16[8,64,1024]{2,1,0:T(8,128)(2,1)S(1)}, u32[]{:S(2)}, u32[]{:S(2)}) async-start(bf16[8,64,1024]{2,1,0:T(8,128)(2,1)} %broadcast_in_dim.4), calls=%async_computation | async-start | bytes 2097152 | tf_op jit(solution)/shard_map/all_to_all | solution.py:51
  24.6 12.4 %all-to-all-done = bf16[8,64,1024]{2,1,0:T(8,128)(2,1)S(1)} async-done(((bf16[8,64,1024]{2,1,0:T(8,128)(2,1)}), bf16[8,64,1024]{2,1,0:T(8,128)(2,1)S(1)}, u32[]{:S(2)}, u32[]{:S(2)}) %all-to-all-start) | async-done | bytes 1048608 | tf_op jit(solution)/shard_map/all_to_all | solution.py:51
  41.4 6.6 %all-to-all-start.1 = ((bf16[8,512,128]{2,1,0:T(8,128)(2,1)}), bf16[8,512,128]{2,1,0:T(8,128)(2,1)}, u32[]{:S(2)}, u32[]{:S(2)}) async-start(bf16[8,512,128]{2,1,0:T(8,128)(2,1)} %copy-done.9), calls=%async_computation.1 | async-start | bytes 2097152 | tf_op jit(solution)/shard_map/all_to_all | solution.py:51
  48.0 2.5 copy.36
  51.9 5.2 %collective-permute-start = (bf16[512,128]{1,0:T(8,128)(2,1)S(1)}, bf16[512,128]{1,0:T(8,128)(2,1)S(1)}, u32[]{:S(2)}, u32[]{:S(2)}) collective-permute-start(bf16[512,128]{1,0:T(8,128)(2,1)S(1)} %get-tuple-element.76.own_ref.query_ref), channel_id=1, source_target_pairs={{0,8},{8,0},{16,24},{24,16},{32,40},{40,32},{48,56},{56,48},{64,72... | collective-permute-start | bytes 393224 | tf_op jit(solution)/shard_map/ppermute | solution.py:558
  57.1 3.9 %pad_maximum_fusion.w_pair_ref = bf16[1024,1152]{1,0:T(8,128)(2,1)} fusion(bf16[1024,576]{1,0:T(8,128)(2,1)} %copy.37, bf16[1024,576]{1,0:T(8,128)(2,1)} %copy.36), kind=kLoop, calls=%fused_computation | loop fusion | flops 4718592 | bytes 4718592 | tf_op jit(solution)/shard_map/concatenate | solution.py:560
  61.0 4.6 %all-gather.2.cloned.1.call-done.dy_ref = bf16[512,1024]{1,0:T(8,128)(2,1)} async-done(((bf16[64,1024]{1,0:T(8,128)(2,1)}), bf16[512,1024]{1,0:T(8,128)(2,1)}) %all-gather.2.cloned.1.call-update) | async-done | bytes 1048592 | tf_op jit(solution)/shard_map/all_gather | solution.py:533
  66.7 4.2 %all-to-all-start.2 = ((bf16[8,128,512]{2,1,0:T(8,128)(2,1)}), bf16[8,128,512]{2,1,0:T(8,128)(2,1)}, u32[]{:S(2)}, u32[]{:S(2)}) async-start(bf16[8,128,512]{2,1,0:T(8,128)(2,1)} %broadcast_in_dim.5), calls=%async_computation.2 | async-start | bytes 2097152 | tf_op jit(solution)/shard_map/all_to_all | solution.py:51
  71.0 8.9 %attend.1 = (f32[1024,128]{1,0:T(8,128)S(1)}, bf16[1024,128]{1,0:T(8,128)(2,1)S(1)}) custom-call(s32[32]{0:T(128)S(1)} %copy-done.30, bf16[512,128]{1,0:T(8,128)(2,1)S(1)} %get-tuple-element.76.own_ref.query_ref, bf16[512,128]{1,0:T(8,128)(2,1)S(1)} %collective-permute-done.other_ref, bf16[4096,128]{1,0:T(8,128)(2,1)} %bitcast.8.kv_ref), custom_call_target="tpu_custom_call" | custom-call | flops 8000000000 | bytes 2097152 | tf_op jit(solution)/shard_map/attend/pallas_call | solution.py:563
  81.5 1.8 finish.1
  84.9 2.7 %collective-permute-start.3 = (bf16[1024,512]{1,0:T(8,128)(2,1)}, bf16[1024,512]{1,0:T(8,128)(2,1)}, u32[]{:S(2)}, u32[]{:S(2)}) collective-permute-start(bf16[1024,512]{1,0:T(8,128)(2,1)} %bitcast.9.w_own_ref), channel_id=1, source_target_pairs={{0,8},{8,0},{16,24},{24,16},{32,40},{40,32},{48,56},{56,48},{64,72... | collective-permute-start | bytes 3145736 | tf_op jit(solution)/shard_map/ppermute | solution.py:587
  87.7 3.7 %all-to-all-start.3 = ((bf16[8,512,128]{2,1,0:T(8,128)(2,1)}), bf16[8,512,128]{2,1,0:T(8,128)(2,1)S(1)}, u32[]{:S(2)}, u32[]{:S(2)}) async-start(bf16[8,512,128]{2,1,0:T(8,128)(2,1)} %get-tuple-element.83), calls=%async_computation.3 | async-start | bytes 2097152 | tf_op jit(solution)/shard_map/all_to_all | solution.py:51
  91.4 2.1 fusion.3.hidden_grad_ref
  93.5 13.5 %all-to-all-done.3.attended_ref = bf16[8,512,128]{2,1,0:T(8,128)(2,1)S(1)} async-done(((bf16[8,512,128]{2,1,0:T(8,128)(2,1)}), bf16[8,512,128]{2,1,0:T(8,128)(2,1)S(1)}, u32[]{:S(2)}, u32[]{:S(2)}) %all-to-all-start.3) | async-done | bytes 1048608 | tf_op jit(solution)/shard_map/all_to_all | solution.py:51
  108.1 11.0 %feed.1 = (f32[64,1024]{1,0:T(8,128)}, bf16[512,1024]{1,0:T(8,128)(2,1)}, bf16[512,576]{1,0:T(8,128)(2,1)}, bf16[512,1152]{1,0:T(8,128)(2,1)}, bf16[512,1024]{1,...) custom-call(bf16[512,1024]{1,0:T(8,128)(2,1)} %bitcast.32, bf16[8,512,128]{2,1,0:T(8,128)(2,1)} %copy-done.35, ...), custom_call_target="tpu_custom_call" | custom-call | flops 5000000000 | bytes 8388608 | tf_op jit(solution)/shard_map/feed/pallas_call | solution.py:592
  119.0 3.6 %all-to-all-start.4 = ((bf16[8,512,128]{2,1,0:T(8,128)(2,1)}), bf16[8,512,128]{2,1,0:T(8,128)(2,1)S(1)}, u32[]{:S(2)}, u32[]{:S(2)}) async-start(bf16[8,512,128]{2,1,0:T(8,128)(2,1)} %get-tuple-element.86), calls=%async_computation.4 | async-start | bytes 2097152 | tf_op jit(solution)/shard_map/all_to_all | solution.py:51
  124.9 6.3 %weights.1 = bf16[1024,1728]{1,0:T(8,128)(2,1)} custom-call(bf16[512,1024]{1,0:T(8,128)(2,1)} %get-tuple-element.120.normed_ref, bf16[512,1152]{1,0:T(8,128)(2,1)} %get-tuple-element.121.pair_ref, bf16[512,1024]{1,0:T(8,128)(2,1)} %all-gather.2.cloned.1.call-done.dy_ref, bf16[512,576]{1,0:T(8,128)(2,1)} %get-tuple-element.91.hidden_ref), custom_call_target="tpu_custom_call" | custom-call | tf_op jit(solution)/shard_map/weights/pallas_call | solution.py:619
  135.0 2.5 all-to-all-done.4.recv_ref
  138.6 3.6 %all-to-all-start.5 = ((bf16[8,64,2048]{2,1,0:T(8,128)(2,1)}), bf16[8,64,2048]{2,1,0:T(8,128)(2,1)S(1)}, u32[]{:S(2)}, u32[]{:S(2)}) async-start(bf16[8,64,2048]{2,1,0:T(8,128)(2,1)} %bitcast.37), calls=%async_computation.5 | async-start | bytes 4194304 | tf_op jit(solution)/shard_map/all_to_all | solution.py:51
  145.0 1.7 collective-permute-start.4
  146.7 6.1 %pull_own.1 = (f32[4096,128]{1,0:T(8,128)S(1)}, f32[512,128]{1,0:T(8,128)S(1)}) custom-call(s32[32]{0:T(128)S(1)} %copy-done.30, bf16[4096,128]{1,0:T(8,128)(2,1)} %bitcast.8.kv_ref, bf16[1024,128]{1,0:T(8,128)(2,1)} %get-tuple-element.79.qb_ref, bf16[1024,128]{1,0:T(8,128)(2,1)S(1)} %prepare.1.dx_ref), custom_call_target="tpu_custom_call" | custom-call | flops 20000000000 | bytes 4194304 | tf_op jit(solution)/shard_map/pull_own/pallas_call | solution.py:643
  153.6 9.5 %pull_other.1 = (bf16[4096,128]{1,0:T(8,128)(2,1)S(1)}, bf16[512,128]{1,0:T(8,128)(2,1)S(1)}) custom-call(s32[32]{0:T(128)S(1)} %copy-done.30, bf16[4096,128]{1,0:T(8,128)(2,1)} %bitcast.8.kv_ref, bf16[1024,128]{1,0:T(8,128)(2,1)} %collective-permute-done.2.qb_ref, bf16[1024,128]{1,0:T(8,128)(2,1)S(1)} %collective-permute-done.4.dx_ref, ...), custom_call_target="tpu_custom_call" | custom-call | flops 20000000000 | bytes 4194304 | tf_op jit(solution)/shard_map/pull_other/pallas_call | solution.py:652
  164.7 2.7 %all-to-all-done.5.recv_ref = bf16[8,64,2048]{2,1,0:T(8,128)(2,1)S(1)} async-done(((bf16[8,64,2048]{2,1,0:T(8,128)(2,1)}), bf16[8,64,2048]{2,1,0:T(8,128)(2,1)S(1)}, u32[]{:S(2)}, u32[]{:S(2)}) %all-to-all-start.5) | async-done | bytes 2097184 | tf_op jit(solution)/shard_map/all_to_all | solution.py:51
  167.5 7.7 %all-to-all-start.6 = ((bf16[8,512,128]{2,1,0:T(8,128)(2,1)}), bf16[8,512,128]{2,1,0:T(8,128)(2,1)}, u32[]{:S(2)}, u32[]{:S(2)}) async-start(bf16[8,512,128]{2,1,0:T(8,128)(2,1)} %bitcast.33), calls=%async_computation.6 | async-start | bytes 2097152 | tf_op jit(solution)/shard_map/all_to_all | solution.py:51
  175.2 2.0 collective-permute-start.5
  179.7 13.6 %all-to-all-done.6.recv_ref = bf16[8,512,128]{2,1,0:T(8,128)(2,1)} async-done(((bf16[8,512,128]{2,1,0:T(8,128)(2,1)}), bf16[8,512,128]{2,1,0:T(8,128)(2,1)}, u32[]{:S(2)}, u32[]{:S(2)}) %all-to-all-start.6) | async-done | bytes 1048608 | tf_op jit(solution)/shard_map/all_to_all | solution.py:51
  193.2 5.5 %back.1 = (bf16[512,256]{1,0:T(8,128)(2,1)}, bf16[8,144,1024]{2,1,0:T(8,128)(2,1)}) custom-call(f32[512,128]{1,0:T(8,128)} %copy-done.20, bf16[512,128]{1,0:T(8,128)(2,1)} %collective-permute-done.5.dq_recv_ref, bf16[8,512,128]{2,1,0:T(8,128)(2,1)} %all-to-all-done.6.recv_ref, f32[512,256]{1,0:T(8,128)} %copy-done.13, f32[2,128]{1,0:T(2,128)} %copy-done.29, ...), custom_call_target="tpu_custom_call" | custom-call | tf_op jit(solution)/shard_map/back/pallas_call | solution.py:674
  198.7 6.7 %all-to-all-start.7 = ((bf16[8,144,1024]{2,1,0:T(8,128)(2,1)}), bf16[8,144,1024]{2,1,0:T(8,128)(2,1)S(1)}, u32[]{:S(2)}, u32[]{:S(2)}) async-start(bf16[8,144,1024]{2,1,0:T(8,128)(2,1)} %get-tuple-element.102), calls=%async_computation.7 | async-start | bytes 4718592 | tf_op jit(solution)/shard_map/all_to_all | solution.py:51
  211.2 25.3 %all-to-all-done.7.recv_ref = bf16[8,144,1024]{2,1,0:T(8,128)(2,1)S(1)} async-done(((bf16[8,144,1024]{2,1,0:T(8,128)(2,1)}), bf16[8,144,1024]{2,1,0:T(8,128)(2,1)S(1)}, u32[]{:S(2)}, u32[]{:S(2)}) %all-to-all-start.7) | async-done | bytes 2359328 | tf_op jit(solution)/shard_map/all_to_all | solution.py:51
  243.7 5.6 %all-to-all-start.8 = ((bf16[8,80,384]{2,1,0:T(8,128)(2,1)}), bf16[8,80,384]{2,1,0:T(8,128)(2,1)S(1)}, u32[]{:S(2)}, u32[]{:S(2)}) async-start(bf16[8,80,384]{2,1,0:T(8,128)(2,1)} %merge.1), calls=%async_computation.8 | async-start | bytes 983040 | tf_op jit(solution)/shard_map/all_to_all | solution.py:51
  251.1 8.6 %all-to-all-done.8.recv_ref = bf16[8,80,384]{2,1,0:T(8,128)(2,1)S(1)} async-done(((bf16[8,80,384]{2,1,0:T(8,128)(2,1)}), bf16[8,80,384]{2,1,0:T(8,128)(2,1)S(1)}, u32[]{:S(2)}, u32[]{:S(2)}) %all-to-all-start.8) | async-done | bytes 491552 | tf_op jit(solution)/shard_map/all_to_all | solution.py:51
  (135 shorter events, 46.3 us)
Async XLA Ops:
  7.2 84.2 %copy-start = (bf16[576,1024]{1,0:T(8,128)(2,1)S(1)}, bf16[576,1024]{1,0:T(8,128)(2,1)}, u32[]{:S(2)}) copy-start(bf16[576,1024]{1,0:T(8,128)(2,1)} %param.29) | copy-start | bytes 3538948
  7.2 12.8 %copy-start.41 = (s32[8192]{0:T(1024)S(1)}, s32[8192]{0:T(1024)}, u32[]{:S(2)}) copy-start(s32[8192]{0:T(1024)} %param.17) | copy-start | bytes 98308
  7.2 12.9 %copy-start.39 = (bf16[1024,64]{0,1:T(8,128)(2,1)S(1)}, bf16[1024,64]{0,1:T(8,128)(2,1)}, u32[]{:S(2)}) copy-start(bf16[1024,64]{0,1:T(8,128)(2,1)} %param.21) | copy-start | bytes 393220
  7.2 13.0 %copy-start.40 = (bf16[1024,64]{0,1:T(8,128)(2,1)S(1)}, bf16[1024,64]{0,1:T(8,128)(2,1)}, u32[]{:S(2)}) copy-start(bf16[1024,64]{0,1:T(8,128)(2,1)} %param.22) | copy-start | bytes 393220
  7.2 58.4 %all-gather.2.cloned.1.call-start = ((), (), s32[]{:S(2)}) async-start(), calls=%async_computation.10 | async-start | bytes 1179648 | tf_op jit(solution)/shard_map/all_gather | solution.py:533
  8.0 13.8 %copy-start.42 = (f32[64]{0:T(128)S(1)}, f32[64]{0:T(128)}, u32[]{:S(2)}) copy-start(f32[64]{0:T(128)} %param.23) | copy-start | bytes 772
  8.0 13.8 %copy-start.43 = (f32[64]{0:T(128)S(1)}, f32[64]{0:T(128)}, u32[]{:S(2)}) copy-start(f32[64]{0:T(128)} %param.24) | copy-start | bytes 772
  10.0 27.0 %all-to-all-start = ((bf16[8,64,1024]{2,1,0:T(8,128)(2,1)}), bf16[8,64,1024]{2,1,0:T(8,128)(2,1)S(1)}, u32[]{:S(2)}, u32[]{:S(2)}) async-start(bf16[8,64,1024]{2,1,0:T(8,128)(2,1)} %broadcast_in_dim.4), calls=%async_computation | async-start | bytes 2097152 | tf_op jit(solution)/shard_map/all_to_all | solution.py:51
  20.1 16.9 %copy-start.27 = (f32[1024]{0:T(1024)S(1)}, f32[1024]{0:T(1024)}, u32[]{:S(2)}) copy-start(f32[1024]{0:T(1024)} %param.19) | copy-start | bytes 12292
  21.9 16.6 %copy-start.29 = (f32[2,128]{1,0:T(2,128)}, f32[2,128]{1,0:T(2,128)S(1)}, u32[]{:S(2)}) copy-start(f32[2,128]{1,0:T(2,128)S(1)} %pad_maximum_fusion.5.head_gain_ref) | copy-start | bytes 3076
  23.1 15.4 %copy-start.1 = (bf16[1024,256]{1,0:T(8,128)(2,1)}, bf16[1024,256]{1,0:T(8,128)(2,1)S(1)}, u32[]{:S(2)}) copy-start(bf16[1024,256]{1,0:T(8,128)(2,1)S(1)} %pad_maximum_fusion.2.w_ref) | copy-start | bytes 1572868
  24.5 16.8 %copy-start.7 = (f32[512,128]{1,0:T(8,128)}, f32[512,128]{1,0:T(8,128)S(1)}, u32[]{:S(2)}) copy-start(f32[512,128]{1,0:T(8,128)S(1)} %get-tuple-element.72.cos_ref) | copy-start | bytes 786436
  24.6 16.8 %copy-start.8 = (f32[512,128]{1,0:T(8,128)}, f32[512,128]{1,0:T(8,128)S(1)}, u32[]{:S(2)}) copy-start(f32[512,128]{1,0:T(8,128)S(1)} %get-tuple-element.73.sin_ref) | copy-start | bytes 786436
  41.4 24.3 %all-to-all-start.1 = ((bf16[8,512,128]{2,1,0:T(8,128)(2,1)}), bf16[8,512,128]{2,1,0:T(8,128)(2,1)}, u32[]{:S(2)}, u32[]{:S(2)}) async-start(bf16[8,512,128]{2,1,0:T(8,128)(2,1)} %copy-done.9), calls=%async_computation.1 | async-start | bytes 2097152 | tf_op jit(solution)/shard_map/all_to_all | solution.py:51
  51.9 19.1 %collective-permute-start = (bf16[512,128]{1,0:T(8,128)(2,1)S(1)}, bf16[512,128]{1,0:T(8,128)(2,1)S(1)}, u32[]{:S(2)}, u32[]{:S(2)}) collective-permute-start(bf16[512,128]{1,0:T(8,128)(2,1)S(1)} %get-tuple-element.76.own_ref.query_ref), channel_id=1, source_target_pairs={{0,8},{8,0},{16,24},{24,16},{32,40},{40,32},{48,56},{56,48},{64,72... | collective-permute-start | bytes 393224 | tf_op jit(solution)/shard_map/ppermute | solution.py:558
  66.7 18.2 %all-to-all-start.2 = ((bf16[8,128,512]{2,1,0:T(8,128)(2,1)}), bf16[8,128,512]{2,1,0:T(8,128)(2,1)}, u32[]{:S(2)}, u32[]{:S(2)}) async-start(bf16[8,128,512]{2,1,0:T(8,128)(2,1)} %broadcast_in_dim.5), calls=%async_computation.2 | async-start | bytes 2097152 | tf_op jit(solution)/shard_map/all_to_all | solution.py:51
  79.9 1.6 collective-permute-start.1
  84.9 22.2 %collective-permute-start.3 = (bf16[1024,512]{1,0:T(8,128)(2,1)}, bf16[1024,512]{1,0:T(8,128)(2,1)}, u32[]{:S(2)}, u32[]{:S(2)}) collective-permute-start(bf16[1024,512]{1,0:T(8,128)(2,1)} %bitcast.9.w_own_ref), channel_id=1, source_target_pairs={{0,8},{8,0},{16,24},{24,16},{32,40},{40,32},{48,56},{56,48},{64,72... | collective-permute-start | bytes 3145736 | tf_op jit(solution)/shard_map/ppermute | solution.py:587
  87.7 19.4 %all-to-all-start.3 = ((bf16[8,512,128]{2,1,0:T(8,128)(2,1)}), bf16[8,512,128]{2,1,0:T(8,128)(2,1)S(1)}, u32[]{:S(2)}, u32[]{:S(2)}) async-start(bf16[8,512,128]{2,1,0:T(8,128)(2,1)} %get-tuple-element.83), calls=%async_computation.3 | async-start | bytes 2097152 | tf_op jit(solution)/shard_map/all_to_all | solution.py:51
  119.0 18.5 %all-to-all-start.4 = ((bf16[8,512,128]{2,1,0:T(8,128)(2,1)}), bf16[8,512,128]{2,1,0:T(8,128)(2,1)S(1)}, u32[]{:S(2)}, u32[]{:S(2)}) async-start(bf16[8,512,128]{2,1,0:T(8,128)(2,1)} %get-tuple-element.86), calls=%async_computation.4 | async-start | bytes 2097152 | tf_op jit(solution)/shard_map/all_to_all | solution.py:51
  122.6 126.8 %reduce-scatter.2.cloned.1.call-start = ((), (), s32[]{:S(2)}) async-start(), calls=%async_computation.11 | async-start | bytes 3899392 | tf_op jit(solution)/shard_map/reduce_scatter | solution.py:627
  124.1 29.5 %collective-permute-start.2 = (bf16[1024,128]{1,0:T(8,128)(2,1)}, bf16[1024,128]{1,0:T(8,128)(2,1)}, u32[]{:S(2)}, u32[]{:S(2)}) collective-permute-start(bf16[1024,128]{1,0:T(8,128)(2,1)} %get-tuple-element.79.qb_ref), channel_id=1, source_target_pairs={{0,8},{8,0},{16,24},{24,16},{32,40},{40,32},{48,56},{56,48},{64,72... | collective-permute-start | bytes 786440 | tf_op jit(solution)/shard_map/ppermute | solution.py:585
  138.6 28.9 %all-to-all-start.5 = ((bf16[8,64,2048]{2,1,0:T(8,128)(2,1)}), bf16[8,64,2048]{2,1,0:T(8,128)(2,1)S(1)}, u32[]{:S(2)}, u32[]{:S(2)}) async-start(bf16[8,64,2048]{2,1,0:T(8,128)(2,1)} %bitcast.37), calls=%async_computation.5 | async-start | bytes 4194304 | tf_op jit(solution)/shard_map/all_to_all | solution.py:51
  145.0 8.6 %collective-permute-start.4 = (bf16[1024,128]{1,0:T(8,128)(2,1)S(1)}, bf16[1024,128]{1,0:T(8,128)(2,1)S(1)}, u32[]{:S(2)}, u32[]{:S(2)}) collective-permute-start(bf16[1024,128]{1,0:T(8,128)(2,1)S(1)} %prepare.1.dx_ref), channel_id=1, source_target_pairs={{0,8},{8,0},{16,24},{24,16},{32,40},{40,32},{48,56},{56,48},{64,72... | collective-permute-start | bytes 786440 | tf_op jit(solution)/shard_map/ppermute | solution.py:639
  164.7 12.5 %copy-start.15 = (bf16[64,1024]{1,0:T(8,128)(2,1)S(1)}, bf16[64,1024]{1,0:T(8,128)(2,1)}, u32[]{:S(2)}) copy-start(bf16[64,1024]{1,0:T(8,128)(2,1)} %cotangent_ref.1) | copy-start | bytes 393220
  167.5 25.8 %all-to-all-start.6 = ((bf16[8,512,128]{2,1,0:T(8,128)(2,1)}), bf16[8,512,128]{2,1,0:T(8,128)(2,1)}, u32[]{:S(2)}, u32[]{:S(2)}) async-start(bf16[8,512,128]{2,1,0:T(8,128)(2,1)} %bitcast.33), calls=%async_computation.6 | async-start | bytes 2097152 | tf_op jit(solution)/shard_map/all_to_all | solution.py:51
  175.2 4.5 %collective-permute-start.5 = (bf16[512,128]{1,0:T(8,128)(2,1)S(1)}, bf16[512,128]{1,0:T(8,128)(2,1)}, u32[]{:S(2)}, u32[]{:S(2)}) collective-permute-start(bf16[512,128]{1,0:T(8,128)(2,1)S(1)} %copy-done.32), channel_id=1, source_target_pairs={{0,8},{8,0},{16,24},{24,16},{32,40},{40,32},{48,56},{56,48},{64,72... | collective-permute-start | bytes 393224 | tf_op jit(solution)/shard_map/ppermute | solution.py:671
  198.7 37.8 %copy-start.28 = (f32[1024]{0:T(1024)S(1)}, f32[1024]{0:T(1024)}, u32[]{:S(2)}) copy-start(f32[1024]{0:T(1024)} %param.19) | copy-start | bytes 12292
  198.7 37.8 %all-to-all-start.7 = ((bf16[8,144,1024]{2,1,0:T(8,128)(2,1)}), bf16[8,144,1024]{2,1,0:T(8,128)(2,1)S(1)}, u32[]{:S(2)}, u32[]{:S(2)}) async-start(bf16[8,144,1024]{2,1,0:T(8,128)(2,1)} %get-tuple-element.102), calls=%async_computation.7 | async-start | bytes 4718592 | tf_op jit(solution)/shard_map/all_to_all | solution.py:51
  208.1 2.4 collective-permute-start.6
  240.6 2.2 collective-permute-start.7
  243.7 16.0 %all-to-all-start.8 = ((bf16[8,80,384]{2,1,0:T(8,128)(2,1)}), bf16[8,80,384]{2,1,0:T(8,128)(2,1)S(1)}, u32[]{:S(2)}, u32[]{:S(2)}) async-start(bf16[8,80,384]{2,1,0:T(8,128)(2,1)} %merge.1), calls=%async_computation.8 | async-start | bytes 983040 | tf_op jit(solution)/shard_map/all_to_all | solution.py:51
  (31 other events, 75.3 us)
Sparse Core Ops, SparseCore 0:
  9.7 55.8 all-gather.1
  131.3 89.0 reduce-scatter.1

commit v4 on v3

--- a/solution.py
+++ b/solution.py
@@ -70,17 +70,24 @@
     return jnp.where(left, first, second) * (1.0 / HEAD)
 
 
-def project_kernel(
-    x_ref, gain_ref, w_ref, head_gain_ref, cos_ref, sin_ref, normed_ref, pre_ref, query_ref, kv_ref
-):
+def copies_kernel(block_ref, out_ref):
+    for peer in range(out_ref.shape[0]):
+        out_ref[peer] = block_ref[...]
+
+
+def projected(x_ref, gain_ref, w_ref):
     x = x_ref[...].astype(f32)
     scaled = x * lax.rsqrt(jnp.mean(x * x, axis=1, keepdims=True) + eps)
     normed = (scaled * gain_ref[...]).astype(bf16)
-    normed_ref[...] = normed
-    pre = dot(normed, w_ref[...])
-    pre_ref[...] = pre
+    return normed, dot(normed, w_ref[...])
+
+
+def project_kernel(
+    x_ref, gain_ref, w_ref, head_gain_ref, cos_ref, sin_ref, query_ref, kv_ref
+):
+    _, pre = projected(x_ref, gain_ref, w_ref)
     cosine, sine = cos_ref[...], sin_ref[...]
-    left = left_half((x.shape[0], LANES))
+    left = left_half((x_ref.shape[0], LANES))
 
     def prepared(v, gain):
         v = v * lax.rsqrt(head_mean(v * v, left) + eps) * gain
@@ -93,6 +100,10 @@
     both = jnp.where(left, key, pair).astype(bf16)
     for peer in range(kv_ref.shape[0]):
         kv_ref[peer] = both
+
+
+def keep_kernel(x_ref, gain_ref, w_ref, normed_ref, pre_ref):
+    normed_ref[...], pre_ref[...] = projected(x_ref, gain_ref, w_ref)
 
 
 def earlier_spans(order_ref, list_ref, rank, core, blocks):
@@ -345,18 +356,14 @@
         sent_ref[peer, 2 * part :, 3 * LANES :] = jnp.zeros((16, width - 3 * LANES), bf16)
 
 
-def tokens_kernel(
-    recv_ref, tokens_ref, gain_ref, resid_grad_ref, attended_ref, grad_ref, own_ref, other_ref,
-    flat_ref,
-):
-    part = tokens_ref.shape[0]
+def last_kernel(recv_ref, attended_ref, own_ref, other_ref, flat_ref):
     rows = own_ref.shape[0] - 16
-    total = recv_ref[0, :part].astype(f32)
+    peers = recv_ref.shape[0]
+    part = flat_ref.shape[0] // peers
     sums = recv_ref[0, 2 * part :, : 3 * LANES].astype(f32)
-    for peer in range(1, recv_ref.shape[0]):
-        total = total + recv_ref[peer, :part].astype(f32)
+    for peer in range(1, peers):
         sums = sums + recv_ref[peer, 2 * part :, : 3 * LANES].astype(f32)
-    for peer in range(recv_ref.shape[0]):
+    for peer in range(peers):
         flat_ref[peer * part : (peer + 1) * part, :] = recv_ref[peer, part : 2 * part]
     by_core(
         own_ref, other_ref, slice(0, rows), slice(0, LANES), t_dot(flat_ref[...], attended_ref[...])
@@ -364,6 +371,13 @@
     for target in (own_ref, other_ref):
         target[:rows, LANES:] = jnp.zeros((rows, 2 * LANES), bf16)
         target[rows:, :] = sums.astype(bf16)
+
+
+def tokens_kernel(recv_ref, tokens_ref, gain_ref, resid_grad_ref, grad_ref):
+    part = tokens_ref.shape[0]
+    total = recv_ref[0, :part].astype(f32)
+    for peer in range(1, recv_ref.shape[0]):
+        total = total + recv_ref[peer, :part].astype(f32)
     x = tokens_ref[...].astype(f32)
     factor = lax.rsqrt(jnp.mean(x * x, axis=1, keepdims=True) + eps)
     unit = x * factor
@@ -520,7 +534,13 @@
 
     x_all = spread(tokens, "tp", tp_count).reshape(local, width)
     w_half = lax.dynamic_slice_in_dim(w_out, (me % 2) * (width // 2), width // 2, 1)
-    w_half = jnp.broadcast_to(w_half[None], (tp_count, heads, width // 2))
+    w_half = call(
+        copies_kernel,
+        shape((tp_count, heads, width // 2), bf16),
+        in_specs=in_vmem(1),
+        out_specs=pl.BlockSpec(memory_space=pltpu.VMEM),
+        name="copies",
+    )(w_half)
     w_qkv = jnp.concatenate([w_query, w_key, w_value], axis=1)
     cosine, sine = turning(positions, span_order, me, span)
     head_gain = jnp.stack(
@@ -535,30 +555,35 @@
     by_span = lambda rows, cols: pl.BlockSpec((rows, cols), lambda k: (k, 0))
     whole = lambda a: pl.BlockSpec(a.shape, lambda k: (0, 0))
     gain_row = first_gain.reshape(1, width)
-    normed, pre, query, kv = call(
+    query, kv = call(
         project_kernel,
-        (
-            shape((local, width), bf16),
-            shape((local, 2 * LANES), f32),
-            shape((local, LANES), bf16),
-            shape((half, local, LANES), bf16),
-        ),
+        (shape((local, LANES), bf16), shape((half, local, LANES), bf16)),
         grid=(2,),
         in_specs=[
             by_span(span, width), whole(gain_row), whole(w_qkv), whole(head_gain),
             by_span(span, LANES), by_span(span, LANES),
         ],
         out_specs=(
-            by_span(span, width), by_span(span, 2 * LANES), by_span(span, LANES),
+            by_span(span, LANES),
             pl.BlockSpec((half, span, LANES), lambda k: (0, k, 0)),
         ),
         name="project",
     )(x_all, gain_row, w_qkv, head_gain, cosine, sine)
+    normed, pre = call(
+        keep_kernel,
+        (shape((local, width), bf16), shape((local, 2 * LANES), f32)),
+        grid=(2,),
+        in_specs=[by_span(span, width), whole(gain_row), whole(w_qkv)],
+        out_specs=(by_span(span, width), by_span(span, 2 * LANES)),
+        name="keep",
+    )(x_all, gain_row, w_qkv)
 
     query_other = lax.ppermute(query, "ctx", other_core)
     kv_all = exchange(kv, "ctx", same_core).reshape(half * local, LANES)
     w_pair = jnp.concatenate([w_gate, w_up], axis=1)
-    kv_all, w_pair, w_half, dy_all = lax.optimization_barrier((kv_all, w_pair, w_half, dy_all))
+    kv_all, w_pair, w_half, dy_all, normed, pre = lax.optimization_barrier(
+        (kv_all, w_pair, w_half, dy_all, normed, pre)
+    )
     w_out_own = exchange(w_half, "tp").reshape(width, width // 2)
     acc, sent = call(
         attend_kernel,
@@ -694,14 +719,21 @@
         (recv, grads, grads_moved, attended)
     )
     last_shape = shape((width // 2 + 16, 3 * LANES), bf16)
-    grad_tokens, last, last_sent = call(
+    last, last_sent = call(
+        last_kernel,
+        (last_shape, last_shape),
+        in_specs=in_vmem(2),
+        out_specs=tuple(in_vmem(2)),
+        scratch_shapes=[pltpu.VMEM((local, width), bf16)],
+        name="last",
+    )(recv, attended)
+    grad_tokens = call(
         tokens_kernel,
-        (shape((part, width), bf16), last_shape, last_shape),
-        in_specs=in_vmem(5),
-        out_specs=tuple(in_vmem(3)),
-        scratch_shapes=[pltpu.VMEM((local, width), bf16)],
+        shape((part, width), bf16),
+        in_specs=in_vmem(4),
+        out_specs=pl.BlockSpec(memory_space=pltpu.VMEM),
         name="tokens",
-    )(recv, tokens, gain_row, resid_grad, attended)
+    )(recv, tokens, gain_row, resid_grad)
     sent = call(
         merge_kernel,
         shape((half, width // ctx_count + 16, 3 * LANES), bf16),

time: 269 us -> 262 us (0.974)
  waiting for transfers between devices: 87.4 us -> 76.1 us
  starting transfers between devices: 63.4 us -> 66.8 us
    all_to_all x9, waiting for transfers between devices: 79.5 us -> 71.7 us  [exchange(): return lax.all_to_all(x, axis, 0, 0, axis_index_groups=groups, tiled=True)]
    all_gather x1, waiting for transfers between devices: 4.63 us -> 1.18 us  [per_device(): dy_all = lax.all_gather(cotangent, 'tp', axis=0, tiled=True)]
    pallas_call x1, Pallas kernels: 9.52 us -> 6.67 us  [per_device(): call(partial(pull_kernel, True), (shape(keys_shape, bf16), shape((local,...]
    pallas_call x1, Pallas kernels: 6.13 us -> 8.94 us  [per_device(): call(partial(pull_kernel, False), (shape(keys_shape, f32), shape((local,...]
    unnamed x92 -> x94, local copies, waits for them, and re-layouts: 24.2 us -> 24.5 us
  transfers between devices with their start and end apart: 19 -> 19, of which waited for: 11 -> 10; matrix products, arithmetic and copies ran while one was open for 8% -> 9% of each run, Pallas kernels for 17% -> 17%
where the time goes in v4:
time: 262 us; the launch traced here: 261 us
  waiting for transfers between devices  76.1 us (29%)
  starting transfers between devices  66.8 us (25%)
  Pallas kernels  57.3 us (22%)
  local copies, waits for them, and re-layouts  29.3 us (11%)
  between operations  18.5 us (7%)
  other arithmetic  7.15 us (3%)
  matrix products  5.65 us (2%)
    all_to_all x9, waiting for transfers between devices, exchange(): return lax.all_to_all(x, axis, 0, 0, axis_index_groups=groups, tiled=True)  71.7 us
    all_to_all x9, starting transfers between devices, exchange(): return lax.all_to_all(x, axis, 0, 0, axis_index_groups=groups, tiled=True)  46.7 us
    unnamed x94, local copies, waits for them, and re-layouts  24.5 us
    pallas_call x1, Pallas kernels, per_device(): call(feed_kernel, (shape((part, width), f32), shape((local, width), bf16)...  11 us
    pallas_call x1, Pallas kernels, per_device(): call(partial(pull_kernel, False), (shape(keys_shape, f32), shape((local,...  8.94 us
    pallas_call x1, Pallas kernels, per_device(): call(attend_kernel, (shape((2 * local, LANES), f32), shape((2 * local, LA...  8.88 us
    pallas_call x1, Pallas kernels, per_device(): call(partial(pull_kernel, True), (shape(keys_shape, bf16), shape((local,...  6.67 us
    pallas_call x1, Pallas kernels, per_device(): call(weights_kernel, shape((width, 3 * hidden_width), bf16), in_specs=in_...  6.29 us
  transfers between devices with their start and end apart: 19, of which 10 were waited for; matrix products, arithmetic and copies ran while one was open for 9% of the time, Pallas kernels for 17%

profile of v4, /device:TPU:1, one launch (start us, length us, event | category | flops | bytes accessed | tf_op | source)
XLA Modules:
  0.0 260.7 jit_solution(10334713334354915477)
XLA Ops:
  10.0 6.9 %all-to-all-start = ((bf16[8,64,1024]{2,1,0:T(8,128)(2,1)}), bf16[8,64,1024]{2,1,0:T(8,128)(2,1)S(1)}, u32[]{:S(2)}, u32[]{:S(2)}) async-start(bf16[8,64,1024]{2,1,0:T(8,128)(2,1)} %broadcast_in_dim.2), calls=%async_computation | async-start | bytes 2097152 | tf_op jit(solution)/shard_map/all_to_all | solution.py:51
  23.7 13.3 %all-to-all-done = bf16[8,64,1024]{2,1,0:T(8,128)(2,1)S(1)} async-done(((bf16[8,64,1024]{2,1,0:T(8,128)(2,1)}), bf16[8,64,1024]{2,1,0:T(8,128)(2,1)S(1)}, u32[]{:S(2)}, u32[]{:S(2)}) %all-to-all-start) | async-done | bytes 1048608 | tf_op jit(solution)/shard_map/all_to_all | solution.py:51
  39.5 6.9 %all-to-all-start.1 = ((bf16[8,512,128]{2,1,0:T(8,128)(2,1)}), bf16[8,512,128]{2,1,0:T(8,128)(2,1)}, u32[]{:S(2)}, u32[]{:S(2)}) async-start(bf16[8,512,128]{2,1,0:T(8,128)(2,1)} %copy-done.11), calls=%async_computation.1 | async-start | bytes 2097152 | tf_op jit(solution)/shard_map/all_to_all | solution.py:51
  46.4 2.4 copy.36
  48.8 2.4 copy.37
  51.2 5.0 %collective-permute-start = (bf16[512,128]{1,0:T(8,128)(2,1)S(1)}, bf16[512,128]{1,0:T(8,128)(2,1)S(1)}, u32[]{:S(2)}, u32[]{:S(2)}) collective-permute-start(bf16[512,128]{1,0:T(8,128)(2,1)S(1)} %get-tuple-element.79.own_ref.query_ref), channel_id=1, source_target_pairs={{0,8},{8,0},{16,24},{24,16},{32,40},{40,32},{48,56},{56,48},{64,72... | collective-permute-start | bytes 393224 | tf_op jit(solution)/shard_map/ppermute | solution.py:581
  56.2 3.9 %pad_maximum_fusion.w_pair_ref = bf16[1024,1152]{1,0:T(8,128)(2,1)} fusion(bf16[1024,576]{1,0:T(8,128)(2,1)} %copy.37, bf16[1024,576]{1,0:T(8,128)(2,1)} %copy.36), kind=kLoop, calls=%fused_computation | loop fusion | flops 4718592 | bytes 4718592 | tf_op jit(solution)/shard_map/concatenate | solution.py:583
  65.0 3.6 %all-to-all-start.2 = ((bf16[8,128,512]{2,1,0:T(8,128)(2,1)}), bf16[8,128,512]{2,1,0:T(8,128)(2,1)S(1)}, u32[]{:S(2)}, u32[]{:S(2)}) async-start(bf16[8,128,512]{2,1,0:T(8,128)(2,1)} %copy-done.5), calls=%async_computation.2 | async-start | bytes 2097152 | tf_op jit(solution)/shard_map/all_to_all | solution.py:51
  68.6 8.9 %attend.1 = (f32[1024,128]{1,0:T(8,128)S(1)}, bf16[1024,128]{1,0:T(8,128)(2,1)S(1)}) custom-call(s32[32]{0:T(128)S(1)} %copy-done.32, bf16[512,128]{1,0:T(8,128)(2,1)S(1)} %get-tuple-element.79.own_ref.query_ref, bf16[512,128]{1,0:T(8,128)(2,1)S(1)} %collective-permute-done.other_ref, bf16[4096,128]{1,0:T(8,128)(2,1)} %bitcast.8.kv_ref), custom_call_target="tpu_custom_call" | custom-call | flops 8000000000 | bytes 2097152 | tf_op jit(solution)/shard_map/attend/pallas_call | solution.py:588
  83.0 2.1 collective-permute-start.3
  85.2 4.4 %all-to-all-start.3 = ((bf16[8,512,128]{2,1,0:T(8,128)(2,1)}), bf16[8,512,128]{2,1,0:T(8,128)(2,1)}, u32[]{:S(2)}, u32[]{:S(2)}) async-start(bf16[8,512,128]{2,1,0:T(8,128)(2,1)} %get-tuple-element.86), calls=%async_computation.3 | async-start | bytes 2097152 | tf_op jit(solution)/shard_map/all_to_all | solution.py:51
  89.6 2.1 fusion.3.hidden_grad_ref
  91.7 13.6 %all-to-all-done.3.attended_ref = bf16[8,512,128]{2,1,0:T(8,128)(2,1)} async-done(((bf16[8,512,128]{2,1,0:T(8,128)(2,1)}), bf16[8,512,128]{2,1,0:T(8,128)(2,1)}, u32[]{:S(2)}, u32[]{:S(2)}) %all-to-all-start.3) | async-done | bytes 1048608 | tf_op jit(solution)/shard_map/all_to_all | solution.py:51
  105.4 11.0 %feed.1 = (f32[64,1024]{1,0:T(8,128)}, bf16[512,1024]{1,0:T(8,128)(2,1)}, bf16[512,576]{1,0:T(8,128)(2,1)}, bf16[512,1152]{1,0:T(8,128)(2,1)}, bf16[512,1024]{1,...) custom-call(bf16[512,1024]{1,0:T(8,128)(2,1)} %bitcast.33, ...), custom_call_target="tpu_custom_call" | custom-call | flops 5000000000 | bytes 8388608 | tf_op jit(solution)/shard_map/feed/pallas_call | solution.py:617
  116.4 3.6 %all-to-all-start.4 = ((bf16[8,512,128]{2,1,0:T(8,128)(2,1)}), bf16[8,512,128]{2,1,0:T(8,128)(2,1)S(1)}, u32[]{:S(2)}, u32[]{:S(2)}) async-start(bf16[8,512,128]{2,1,0:T(8,128)(2,1)} %get-tuple-element.89), calls=%async_computation.4 | async-start | bytes 2097152 | tf_op jit(solution)/shard_map/all_to_all | solution.py:51
  122.2 6.3 %weights.1 = bf16[1024,1728]{1,0:T(8,128)(2,1)} custom-call(bf16[512,1024]{1,0:T(8,128)(2,1)} %get-tuple-element.122.normed_ref, bf16[512,1152]{1,0:T(8,128)(2,1)} %get-tuple-element.123.pair_ref, bf16[512,1024]{1,0:T(8,128)(2,1)} %all-gather.2.cloned.1.call-done.dy_ref, bf16[512,576]{1,0:T(8,128)(2,1)} %get-tuple-element.94.hidden_ref), custom_call_target="tpu_custom_call" | custom-call | tf_op jit(solution)/shard_map/weights/pallas_call | solution.py:644
  128.6 2.2 convolution_convert_fusion
  132.3 2.6 all-to-all-done.4.recv_ref
  135.9 3.6 %all-to-all-start.5 = ((bf16[8,64,2048]{2,1,0:T(8,128)(2,1)}), bf16[8,64,2048]{2,1,0:T(8,128)(2,1)S(1)}, u32[]{:S(2)}, u32[]{:S(2)}) async-start(bf16[8,64,2048]{2,1,0:T(8,128)(2,1)} %bitcast.39), calls=%async_computation.5 | async-start | bytes 4194304 | tf_op jit(solution)/shard_map/all_to_all | solution.py:51
  144.0 8.9 %pull_own.1 = (f32[4096,128]{1,0:T(8,128)S(1)}, f32[512,128]{1,0:T(8,128)S(1)}) custom-call(s32[32]{0:T(128)S(1)} %copy-done.32, bf16[4096,128]{1,0:T(8,128)(2,1)} %bitcast.8.kv_ref, bf16[1024,128]{1,0:T(8,128)(2,1)} %get-tuple-element.82.qb_ref, bf16[1024,128]{1,0:T(8,128)(2,1)S(1)} %prepare.1.dx_ref), custom_call_target="tpu_custom_call" | custom-call | flops 20000000000 | bytes 4194304 | tf_op jit(solution)/shard_map/pull_own/pallas_call | solution.py:668
  153.6 6.7 %pull_other.1 = (bf16[4096,128]{1,0:T(8,128)(2,1)S(1)}, bf16[512,128]{1,0:T(8,128)(2,1)S(1)}) custom-call(s32[32]{0:T(128)S(1)} %copy-done.32, bf16[4096,128]{1,0:T(8,128)(2,1)} %bitcast.8.kv_ref, bf16[1024,128]{1,0:T(8,128)(2,1)} %collective-permute-done.2.qb_ref, bf16[1024,128]{1,0:T(8,128)(2,1)S(1)} %collective-permute-done.4.dx_ref, ...), custom_call_target="tpu_custom_call" | custom-call | flops 20000000000 | bytes 4194304 | tf_op jit(solution)/shard_map/pull_other/pallas_call | solution.py:677
  161.9 2.8 %all-to-all-done.5.recv_ref = bf16[8,64,2048]{2,1,0:T(8,128)(2,1)S(1)} async-done(((bf16[8,64,2048]{2,1,0:T(8,128)(2,1)}), bf16[8,64,2048]{2,1,0:T(8,128)(2,1)S(1)}, u32[]{:S(2)}, u32[]{:S(2)}) %all-to-all-start.5) | async-done | bytes 2097184 | tf_op jit(solution)/shard_map/all_to_all | solution.py:51
  164.8 6.9 %all-to-all-start.6 = ((bf16[8,512,128]{2,1,0:T(8,128)(2,1)}), bf16[8,512,128]{2,1,0:T(8,128)(2,1)}, u32[]{:S(2)}, u32[]{:S(2)}) async-start(bf16[8,512,128]{2,1,0:T(8,128)(2,1)} %bitcast.34), calls=%async_computation.6 | async-start | bytes 2097152 | tf_op jit(solution)/shard_map/all_to_all | solution.py:51
  171.7 2.2 collective-permute-start.5
  176.4 11.4 %all-to-all-done.6.recv_ref = bf16[8,512,128]{2,1,0:T(8,128)(2,1)} async-done(((bf16[8,512,128]{2,1,0:T(8,128)(2,1)}), bf16[8,512,128]{2,1,0:T(8,128)(2,1)}, u32[]{:S(2)}, u32[]{:S(2)}) %all-to-all-start.6) | async-done | bytes 1048608 | tf_op jit(solution)/shard_map/all_to_all | solution.py:51
  187.8 5.6 %back.1 = (bf16[512,256]{1,0:T(8,128)(2,1)}, bf16[8,144,1024]{2,1,0:T(8,128)(2,1)}) custom-call(f32[512,128]{1,0:T(8,128)} %copy-done.22, bf16[512,128]{1,0:T(8,128)(2,1)} %collective-permute-done.5.dq_recv_ref, bf16[8,512,128]{2,1,0:T(8,128)(2,1)} %all-to-all-done.6.recv_ref, f32[512,256]{1,0:T(8,128)} %copy-done.15, f32[2,128]{1,0:T(2,128)} %copy-done.31, ...), custom_call_target="tpu_custom_call" | custom-call | tf_op jit(solution)/shard_map/back/pallas_call | solution.py:699
  193.4 6.7 %all-to-all-start.7 = ((bf16[8,144,1024]{2,1,0:T(8,128)(2,1)}), bf16[8,144,1024]{2,1,0:T(8,128)(2,1)S(1)}, u32[]{:S(2)}, u32[]{:S(2)}) async-start(bf16[8,144,1024]{2,1,0:T(8,128)(2,1)} %get-tuple-element.105), calls=%async_computation.7 | async-start | bytes 4718592 | tf_op jit(solution)/shard_map/all_to_all | solution.py:51
  202.8 3.1 %collective-permute-start.6 = (bf16[512,256]{1,0:T(8,128)(2,1)S(1)}, bf16[512,256]{1,0:T(8,128)(2,1)S(1)}, u32[]{:S(2)}, u32[]{:S(2)}) collective-permute-start(bf16[512,256]{1,0:T(8,128)(2,1)S(1)} %get-tuple-element.108), channel_id=1, source_target_pairs={{0,8},{8,0},{16,24},{24,16},{32,40},{40,32},{48,56},{56,48},{64,72... | collective-permute-start | bytes 786440 | tf_op jit(solution)/shard_map/ppermute | solution.py:716
  208.1 22.2 %all-to-all-done.7.recv_ref = bf16[8,144,1024]{2,1,0:T(8,128)(2,1)S(1)} async-done(((bf16[8,144,1024]{2,1,0:T(8,128)(2,1)}), bf16[8,144,1024]{2,1,0:T(8,128)(2,1)S(1)}, u32[]{:S(2)}, u32[]{:S(2)}) %all-to-all-start.7) | async-done | bytes 2359328 | tf_op jit(solution)/shard_map/all_to_all | solution.py:51
  231.8 3.0 %collective-permute-start.7 = (bf16[528,384]{1,0:T(8,128)(2,1)S(1)}, bf16[528,384]{1,0:T(8,128)(2,1)S(1)}, u32[]{:S(2)}, u32[]{:S(2)}) collective-permute-start(bf16[528,384]{1,0:T(8,128)(2,1)S(1)} %get-tuple-element.114), channel_id=1, source_target_pairs={{0,8},{8,0},{16,24},{24,16},{32,40},{40,32},{48,56},{56,48},{64,72... | collective-permute-start | bytes 1216520 | tf_op jit(solution)/shard_map/ppermute | solution.py:743
  237.1 4.1 %all-to-all-start.8 = ((bf16[8,80,384]{2,1,0:T(8,128)(2,1)}), bf16[8,80,384]{2,1,0:T(8,128)(2,1)}, u32[]{:S(2)}, u32[]{:S(2)}) async-start(bf16[8,80,384]{2,1,0:T(8,128)(2,1)} %copy-done.10), calls=%async_computation.8 | async-start | bytes 983040 | tf_op jit(solution)/shard_map/all_to_all | solution.py:51
  245.8 5.8 %all-to-all-done.8.recv_ref = bf16[8,80,384]{2,1,0:T(8,128)(2,1)} async-done(((bf16[8,80,384]{2,1,0:T(8,128)(2,1)}), bf16[8,80,384]{2,1,0:T(8,128)(2,1)}, u32[]{:S(2)}, u32[]{:S(2)}) %all-to-all-start.8) | async-done | bytes 491552 | tf_op jit(solution)/shard_map/all_to_all | solution.py:51
  (139 shorter events, 48.1 us)
Async XLA Ops:
  7.2 82.4 %copy-start = (bf16[576,1024]{1,0:T(8,128)(2,1)S(1)}, bf16[576,1024]{1,0:T(8,128)(2,1)}, u32[]{:S(2)}) copy-start(bf16[576,1024]{1,0:T(8,128)(2,1)} %param.29) | copy-start | bytes 3538948
  7.2 12.9 %copy-start.42 = (s32[8192]{0:T(1024)S(1)}, s32[8192]{0:T(1024)}, u32[]{:S(2)}) copy-start(s32[8192]{0:T(1024)} %param.17) | copy-start | bytes 98308
  7.2 12.9 %copy-start.40 = (bf16[1024,64]{0,1:T(8,128)(2,1)S(1)}, bf16[1024,64]{0,1:T(8,128)(2,1)}, u32[]{:S(2)}) copy-start(bf16[1024,64]{0,1:T(8,128)(2,1)} %param.21) | copy-start | bytes 393220
  7.2 13.1 %copy-start.41 = (bf16[1024,64]{0,1:T(8,128)(2,1)S(1)}, bf16[1024,64]{0,1:T(8,128)(2,1)}, u32[]{:S(2)}) copy-start(bf16[1024,64]{0,1:T(8,128)(2,1)} %param.22) | copy-start | bytes 393220
  7.2 57.7 %all-gather.2.cloned.1.call-start = ((), (), s32[]{:S(2)}) async-start(), calls=%async_computation.10 | async-start | bytes 1179648 | tf_op jit(solution)/shard_map/all_gather | solution.py:553
  8.0 13.9 %copy-start.43 = (f32[64]{0:T(128)S(1)}, f32[64]{0:T(128)}, u32[]{:S(2)}) copy-start(f32[64]{0:T(128)} %param.23) | copy-start | bytes 772
  8.0 13.9 %copy-start.44 = (f32[64]{0:T(128)S(1)}, f32[64]{0:T(128)}, u32[]{:S(2)}) copy-start(f32[64]{0:T(128)} %param.24) | copy-start | bytes 772
  8.0 14.0 %copy-start.39 = (bf16[1024,128]{1,0:T(8,128)(2,1)S(1)}, bf16[1024,128]{1,0:T(8,128)(2,1)}, u32[]{:S(2)}) copy-start(bf16[1024,128]{1,0:T(8,128)(2,1)} %param.20) | copy-start | bytes 786436
  10.0 26.9 %all-to-all-start = ((bf16[8,64,1024]{2,1,0:T(8,128)(2,1)}), bf16[8,64,1024]{2,1,0:T(8,128)(2,1)S(1)}, u32[]{:S(2)}, u32[]{:S(2)}) async-start(bf16[8,64,1024]{2,1,0:T(8,128)(2,1)} %broadcast_in_dim.2), calls=%async_computation | async-start | bytes 2097152 | tf_op jit(solution)/shard_map/all_to_all | solution.py:51
  20.1 16.8 %copy-start.29 = (f32[1024]{0:T(1024)S(1)}, f32[1024]{0:T(1024)}, u32[]{:S(2)}) copy-start(f32[1024]{0:T(1024)} %param.19) | copy-start | bytes 12292
  21.9 16.5 %copy-start.31 = (f32[2,128]{1,0:T(2,128)}, f32[2,128]{1,0:T(2,128)S(1)}, u32[]{:S(2)}) copy-start(f32[2,128]{1,0:T(2,128)S(1)} %pad_maximum_fusion.5.head_gain_ref) | copy-start | bytes 3076
  22.2 38.0 %copy-start.2 = (bf16[1024,256]{1,0:T(8,128)(2,1)}, bf16[1024,256]{1,0:T(8,128)(2,1)S(1)}, u32[]{:S(2)}) copy-start(bf16[1024,256]{1,0:T(8,128)(2,1)S(1)} %pad_maximum_fusion.2.w_ref) | copy-start | bytes 1572868
  23.7 15.8 %copy-start.8 = (f32[512,128]{1,0:T(8,128)}, f32[512,128]{1,0:T(8,128)S(1)}, u32[]{:S(2)}) copy-start(f32[512,128]{1,0:T(8,128)S(1)} %get-tuple-element.73.cos_ref) | copy-start | bytes 786436
  23.7 15.8 %copy-start.9 = (f32[512,128]{1,0:T(8,128)}, f32[512,128]{1,0:T(8,128)S(1)}, u32[]{:S(2)}) copy-start(f32[512,128]{1,0:T(8,128)S(1)} %get-tuple-element.74.sin_ref) | copy-start | bytes 786436
  36.9 23.2 %copy-start.1 = (bf16[8,64,1024]{2,1,0:T(8,128)(2,1)}, bf16[8,64,1024]{2,1,0:T(8,128)(2,1)S(1)}, u32[]{:S(2)}) copy-start(bf16[8,64,1024]{2,1,0:T(8,128)(2,1)S(1)} %all-to-all-done) | copy-start | bytes 3145732
  39.5 25.5 %all-to-all-start.1 = ((bf16[8,512,128]{2,1,0:T(8,128)(2,1)}), bf16[8,512,128]{2,1,0:T(8,128)(2,1)}, u32[]{:S(2)}, u32[]{:S(2)}) async-start(bf16[8,512,128]{2,1,0:T(8,128)(2,1)} %copy-done.11), calls=%async_computation.1 | async-start | bytes 2097152 | tf_op jit(solution)/shard_map/all_to_all | solution.py:51
  51.2 17.3 %collective-permute-start = (bf16[512,128]{1,0:T(8,128)(2,1)S(1)}, bf16[512,128]{1,0:T(8,128)(2,1)S(1)}, u32[]{:S(2)}, u32[]{:S(2)}) collective-permute-start(bf16[512,128]{1,0:T(8,128)(2,1)S(1)} %get-tuple-element.79.own_ref.query_ref), channel_id=1, source_target_pairs={{0,8},{8,0},{16,24},{24,16},{32,40},{40,32},{48,56},{56,48},{64,72... | collective-permute-start | bytes 393224 | tf_op jit(solution)/shard_map/ppermute | solution.py:581
  65.0 18.1 %all-to-all-start.2 = ((bf16[8,128,512]{2,1,0:T(8,128)(2,1)}), bf16[8,128,512]{2,1,0:T(8,128)(2,1)S(1)}, u32[]{:S(2)}, u32[]{:S(2)}) async-start(bf16[8,128,512]{2,1,0:T(8,128)(2,1)} %copy-done.5), calls=%async_computation.2 | async-start | bytes 2097152 | tf_op jit(solution)/shard_map/all_to_all | solution.py:51
  77.5 3.0 %collective-permute-start.1 = (bf16[1024,128]{1,0:T(8,128)(2,1)S(1)}, bf16[1024,128]{1,0:T(8,128)(2,1)S(1)}, u32[]{:S(2)}, u32[]{:S(2)}) collective-permute-start(bf16[1024,128]{1,0:T(8,128)(2,1)S(1)} %get-tuple-element.81), channel_id=1, source_target_pairs={{0,8},{8,0},{16,24},{24,16},{32,40},{40,32},{48,56},{56,48},{64,72... | collective-permute-start | bytes 786440 | tf_op jit(solution)/shard_map/ppermute | solution.py:609
  83.0 22.3 %collective-permute-start.3 = (bf16[1024,512]{1,0:T(8,128)(2,1)S(1)}, bf16[1024,512]{1,0:T(8,128)(2,1)}, u32[]{:S(2)}, u32[]{:S(2)}) collective-permute-start(bf16[1024,512]{1,0:T(8,128)(2,1)S(1)} %bitcast.40), channel_id=1, source_target_pairs={{0,8},{8,0},{16,24},{24,16},{32,40},{40,32},{48,56},{56,48},{64,72... | collective-permute-start | bytes 3145736 | tf_op jit(solution)/shard_map/ppermute | solution.py:612
  85.2 20.2 %all-to-all-start.3 = ((bf16[8,512,128]{2,1,0:T(8,128)(2,1)}), bf16[8,512,128]{2,1,0:T(8,128)(2,1)}, u32[]{:S(2)}, u32[]{:S(2)}) async-start(bf16[8,512,128]{2,1,0:T(8,128)(2,1)} %get-tuple-element.86), calls=%async_computation.3 | async-start | bytes 2097152 | tf_op jit(solution)/shard_map/all_to_all | solution.py:51
  116.4 18.5 %all-to-all-start.4 = ((bf16[8,512,128]{2,1,0:T(8,128)(2,1)}), bf16[8,512,128]{2,1,0:T(8,128)(2,1)S(1)}, u32[]{:S(2)}, u32[]{:S(2)}) async-start(bf16[8,512,128]{2,1,0:T(8,128)(2,1)} %get-tuple-element.89), calls=%async_computation.4 | async-start | bytes 2097152 | tf_op jit(solution)/shard_map/all_to_all | solution.py:51
  119.9 124.1 %reduce-scatter.2.cloned.1.call-start = ((), (), s32[]{:S(2)}) async-start(), calls=%async_computation.11 | async-start | bytes 3899392 | tf_op jit(solution)/shard_map/reduce_scatter | solution.py:652
  121.4 32.2 %collective-permute-start.2 = (bf16[1024,128]{1,0:T(8,128)(2,1)}, bf16[1024,128]{1,0:T(8,128)(2,1)}, u32[]{:S(2)}, u32[]{:S(2)}) collective-permute-start(bf16[1024,128]{1,0:T(8,128)(2,1)} %get-tuple-element.82.qb_ref), channel_id=1, source_target_pairs={{0,8},{8,0},{16,24},{24,16},{32,40},{40,32},{48,56},{56,48},{64,72... | collective-permute-start | bytes 786440 | tf_op jit(solution)/shard_map/ppermute | solution.py:610
  135.9 28.9 %all-to-all-start.5 = ((bf16[8,64,2048]{2,1,0:T(8,128)(2,1)}), bf16[8,64,2048]{2,1,0:T(8,128)(2,1)S(1)}, u32[]{:S(2)}, u32[]{:S(2)}) async-start(bf16[8,64,2048]{2,1,0:T(8,128)(2,1)} %bitcast.39), calls=%async_computation.5 | async-start | bytes 4194304 | tf_op jit(solution)/shard_map/all_to_all | solution.py:51
  142.2 11.4 %collective-permute-start.4 = (bf16[1024,128]{1,0:T(8,128)(2,1)S(1)}, bf16[1024,128]{1,0:T(8,128)(2,1)S(1)}, u32[]{:S(2)}, u32[]{:S(2)}) collective-permute-start(bf16[1024,128]{1,0:T(8,128)(2,1)S(1)} %prepare.1.dx_ref), channel_id=1, source_target_pairs={{0,8},{8,0},{16,24},{24,16},{32,40},{40,32},{48,56},{56,48},{64,72... | collective-permute-start | bytes 786440 | tf_op jit(solution)/shard_map/ppermute | solution.py:664
  164.8 23.0 %all-to-all-start.6 = ((bf16[8,512,128]{2,1,0:T(8,128)(2,1)}), bf16[8,512,128]{2,1,0:T(8,128)(2,1)}, u32[]{:S(2)}, u32[]{:S(2)}) async-start(bf16[8,512,128]{2,1,0:T(8,128)(2,1)} %bitcast.34), calls=%async_computation.6 | async-start | bytes 2097152 | tf_op jit(solution)/shard_map/all_to_all | solution.py:51
  171.7 4.7 %collective-permute-start.5 = (bf16[512,128]{1,0:T(8,128)(2,1)S(1)}, bf16[512,128]{1,0:T(8,128)(2,1)}, u32[]{:S(2)}, u32[]{:S(2)}) collective-permute-start(bf16[512,128]{1,0:T(8,128)(2,1)S(1)} %copy-done.34), channel_id=1, source_target_pairs={{0,8},{8,0},{16,24},{24,16},{32,40},{40,32},{48,56},{56,48},{64,72... | collective-permute-start | bytes 393224 | tf_op jit(solution)/shard_map/ppermute | solution.py:696
  193.4 37.0 %all-to-all-start.7 = ((bf16[8,144,1024]{2,1,0:T(8,128)(2,1)}), bf16[8,144,1024]{2,1,0:T(8,128)(2,1)S(1)}, u32[]{:S(2)}, u32[]{:S(2)}) async-start(bf16[8,144,1024]{2,1,0:T(8,128)(2,1)} %get-tuple-element.105), calls=%async_computation.7 | async-start | bytes 4718592 | tf_op jit(solution)/shard_map/all_to_all | solution.py:51
  202.8 4.6 %collective-permute-start.6 = (bf16[512,256]{1,0:T(8,128)(2,1)S(1)}, bf16[512,256]{1,0:T(8,128)(2,1)S(1)}, u32[]{:S(2)}, u32[]{:S(2)}) collective-permute-start(bf16[512,256]{1,0:T(8,128)(2,1)S(1)} %get-tuple-element.108), channel_id=1, source_target_pairs={{0,8},{8,0},{16,24},{24,16},{32,40},{40,32},{48,56},{56,48},{64,72... | collective-permute-start | bytes 786440 | tf_op jit(solution)/shard_map/ppermute | solution.py:716
  231.8 4.4 %collective-permute-start.7 = (bf16[528,384]{1,0:T(8,128)(2,1)S(1)}, bf16[528,384]{1,0:T(8,128)(2,1)S(1)}, u32[]{:S(2)}, u32[]{:S(2)}) collective-permute-start(bf16[528,384]{1,0:T(8,128)(2,1)S(1)} %get-tuple-element.114), channel_id=1, source_target_pairs={{0,8},{8,0},{16,24},{24,16},{32,40},{40,32},{48,56},{56,48},{64,72... | collective-permute-start | bytes 1216520 | tf_op jit(solution)/shard_map/ppermute | solution.py:743
  237.1 14.4 %all-to-all-start.8 = ((bf16[8,80,384]{2,1,0:T(8,128)(2,1)}), bf16[8,80,384]{2,1,0:T(8,128)(2,1)}, u32[]{:S(2)}, u32[]{:S(2)}) async-start(bf16[8,80,384]{2,1,0:T(8,128)(2,1)} %copy-done.10), calls=%async_computation.8 | async-start | bytes 983040 | tf_op jit(solution)/shard_map/all_to_all | solution.py:51
  (32 other events, 104.4 us)
Sparse Core Ops, SparseCore 0:
  9.7 55.2 all-gather.1
  128.7 90.2 reduce-scatter.1
